TPU v7x, 32 devices: a whole 2x2x4 slice. The times are simulated.
32 devices in a mesh: shard: 2 (over y), ctx: 4 (over z), tp: 4 (over x, core).
Axes of the slice: x: 2, y: 2, z: 4, core: 2. Of those that a mesh axis runs over, the one named last changes fastest.
Arguments:
- tokens: bfloat16 [4, 256, 4, 1024], P('shard', None, 'ctx'), may hold values from -6 to 6
- cotangent: bfloat16 [4, 256, 4, 1024], P('shard', None, 'ctx'), may hold values from -6 to 6
- norm_gain: bfloat16 [2, 1024], replicated, may hold values from 0.25 to 1.75
- norm_bias: bfloat16 [2, 1024], replicated, may hold values from -1 to 1
- w_qkv: bfloat16 [1024, 3, 1024], P('shard', None, 'tp'), may hold values from -0.1875 to 0.1875
- qv_bias: bfloat16 [2, 1024], P(None, 'tp'), may hold values from -1 to 1
- w_out: bfloat16 [1024, 1024], P('shard', 'tp'), may hold values from -0.75 to 0.75
- out_bias: bfloat16 [2, 1024], replicated, may hold values from -2.5 to 2.5
- w_up: bfloat16 [1024, 4096], P('shard', 'tp'), may hold values from -0.1875 to 0.1875
- hidden_bias: bfloat16 [4096], P('tp'), may hold values from -1 to 1
- w_down: bfloat16 [1024, 4096], P('shard', 'tp'), may hold values from -0.09375 to 0.09375
Outputs:
- mixed: bfloat16 [4, 256, 4, 1024], P('shard', None, 'ctx')
- input_grad: float32 [4, 256, 4, 1024], P('shard', None, 'ctx')
- grad_norm_gain: float32 [2, 1024], replicated
- grad_norm_bias: float32 [2, 1024], replicated
- grad_qkv: float32 [1024, 3, 1024], P(('shard', 'ctx'), None, 'tp')
- grad_qv_bias: float32 [2, 1024], P(None, 'tp')
- grad_out: float32 [1024, 1024], P(('shard', 'ctx'), 'tp')
- grad_out_bias: float32 [2, 1024], replicated
- grad_up: float32 [1024, 4096], P(('shard', 'ctx'), 'tp')
- grad_hidden_bias: float32 [4096], P('tp')
- grad_down: float32 [1024, 4096], P(('shard', 'ctx'), 'tp')
All inputs are finite; a program needn't handle non-finite values.
Results may differ from a plain program's by a relative error of at most 0.019.
Values may be sent and summed in bfloat16 or wider, within the bound.
A program may use at most 128 MiB of HBM per device.

v0:
```python
import math

import jax
import jax.numpy as jnp
from jax import lax
from jax.sharding import PartitionSpec as P

H = 16
HD = 64


EPSILON = 1e-05
FLOOR_SCORE = -1e30


def shifted(value, axis, steps):
    count = lax.axis_size(axis)
    pairs = [(source, (source + steps) % count) for source in range(count)]
    return lax.ppermute(value, axis, pairs)


def normalize(values, scale_by, offset):
    average = jnp.mean(values, axis=-1, keepdims=True)
    centred = values - average
    spread = jnp.mean(centred * centred, axis=-1, keepdims=True)
    return centred * lax.rsqrt(spread + EPSILON) * scale_by + offset


def gelu_tanh(values):
    return jax.nn.gelu(values, approximate=True)


def score_block(query_h, key_h, query_pos, key_pos, slopes):
    logits = jnp.einsum("sqhd,skhd->shqk", query_h, key_h, preferred_element_type=jnp.float32) * (
        1.0 / math.sqrt(query_h.shape[-1])
    )
    distance = (query_pos[:, None] - key_pos[None, :]).astype(jnp.float32)
    logits = logits - slopes[None, :, None, None] * distance[None, None]
    allowed = (key_pos[None, :] <= query_pos[:, None])[None, None]
    return (logits, allowed)


def grad_block(query_h, grad_h, log_total, delta_row, query_pos, key_h, value_h, key_pos, slopes):
    scale_by = 1.0 / math.sqrt(query_h.shape[-1])
    logits, allowed = score_block(query_h, key_h, query_pos, key_pos, slopes)
    probs = jnp.where(allowed, jnp.exp(logits - log_total[..., None]), 0.0)
    prob_grad = jnp.einsum("sqhd,skhd->shqk", grad_h, value_h, preferred_element_type=jnp.float32)
    score_grad = (probs * (prob_grad - delta_row[..., None])).astype(jnp.bfloat16)
    query_term = (
        jnp.einsum("shqk,skhd->sqhd", score_grad, key_h, preferred_element_type=jnp.float32)
        * scale_by
    )
    key_term = (
        jnp.einsum("shqk,sqhd->skhd", score_grad, query_h, preferred_element_type=jnp.float32)
        * scale_by
    )
    value_term = jnp.einsum(
        "shqk,sqhd->skhd", probs.astype(jnp.bfloat16), grad_h, preferred_element_type=jnp.float32
    )
    return (query_term, key_term, value_term)


def per_device(
    tokens,
    cotangent,
    norm_gain,
    norm_bias,
    w_qkv,
    qv_bias,
    w_out,
    out_bias,
    w_up,
    hidden_bias,
    w_down,
):
    seq_dev, group_len, model_width = (tokens.shape[0], tokens.shape[1], tokens.shape[3])
    tok_rows = seq_dev * group_len
    local_width = w_qkv.shape[2]
    heads_loc = local_width // HD
    cycle_size = lax.axis_size("ctx")
    cycle_index = lax.axis_index("ctx")
    slopes = jnp.exp2(
        -8.0
        * (lax.axis_index("tp") * heads_loc + jnp.arange(heads_loc, dtype=jnp.int32) + 1).astype(
            jnp.float32
        )
        / H
    )
    positions = jnp.arange(group_len, dtype=jnp.int32)
    own_pos = positions * cycle_size + cycle_index

    def split_heads(matrix):
        return matrix.reshape(seq_dev, group_len, heads_loc, HD)

    resident = tokens.reshape(tok_rows, model_width).astype(jnp.float32)
    gains = norm_gain.astype(jnp.float32)
    shifts = norm_bias.astype(jnp.float32)
    out_shift = out_bias.astype(jnp.float32)
    qv_shift = qv_bias.astype(jnp.float32)
    hidden_shift = hidden_bias.astype(jnp.float32)
    gathered = (
        lax.all_gather(w_qkv, "shard", axis=0, tiled=True),
        lax.all_gather(w_out, "shard", axis=0, tiled=True),
        lax.all_gather(w_up, "shard", axis=0, tiled=True),
        lax.all_gather(w_down, "shard", axis=0, tiled=True),
    )
    full_qkv, full_out, full_up, full_down = gathered
    normed_one = normalize(resident, gains[0], shifts[0]).astype(jnp.bfloat16)
    projected = jnp.einsum("td,dcf->tcf", normed_one, full_qkv, preferred_element_type=jnp.float32)
    query_bf = (projected[:, 0] + qv_shift[0]).astype(jnp.bfloat16)
    key_bf = projected[:, 1].astype(jnp.bfloat16)
    value_bf = (projected[:, 2] + qv_shift[1]).astype(jnp.bfloat16)
    query_heads = split_heads(query_bf)
    kv_pair = jnp.stack([key_bf, value_bf], 1).reshape(seq_dev, group_len, 2, local_width)
    kv_single = kv_pair.reshape(seq_dev, group_len, 1, 2, local_width)
    stat_zeros = jnp.zeros((seq_dev, heads_loc, group_len), jnp.float32)
    initial = (
        jnp.full((seq_dev, heads_loc, group_len), FLOOR_SCORE, jnp.float32),
        stat_zeros,
        jnp.zeros((seq_dev, heads_loc, group_len, HD), jnp.float32),
    )
    running = initial
    arrived = lax.all_gather(kv_single, "ctx", axis=2, tiled=True)

    def per_source(running_in, source_step):
        source_block = lax.dynamic_index_in_dim(arrived, source_step, 2, keepdims=False)
        src_keys = split_heads(source_block[:, :, 0])
        src_values = split_heads(source_block[:, :, 1])
        key_pos = positions * cycle_size + source_step
        logits, allowed = score_block(query_heads, src_keys, own_pos, key_pos, slopes)
        run_top, run_total, run_sum = running_in
        row_top = jnp.max(jnp.where(allowed, logits, FLOOR_SCORE), axis=-1)
        fresh_top = jnp.maximum(run_top, row_top)
        weights = jnp.where(allowed, jnp.exp(logits - fresh_top[..., None]), 0.0)
        fade_by = jnp.exp(run_top - fresh_top)
        run_total = run_total * fade_by + jnp.sum(weights, axis=-1)
        run_sum = run_sum * fade_by[..., None] + jnp.einsum(
            "shqk,skhd->shqd",
            weights.astype(jnp.bfloat16),
            src_values,
            preferred_element_type=jnp.float32,
        )
        return ((fresh_top, run_total, run_sum), None)

    running, unused = lax.scan(per_source, running, jnp.arange(arrived.shape[2], dtype=jnp.int32))
    run_top, run_total, run_sum = running
    attended = run_sum / run_total[..., None]
    log_total = run_top + jnp.log(run_total)
    attended_seq = attended.transpose(0, 2, 1, 3)
    attended_bf = attended_seq.reshape(tok_rows, local_width).astype(jnp.bfloat16)
    branch = lax.psum(
        jnp.einsum("tf,df->td", attended_bf, full_out, preferred_element_type=jnp.float32).astype(
            jnp.bfloat16
        ),
        "tp",
    ).astype(jnp.float32)
    resid = resident + branch + out_shift[0]
    normed_two = normalize(resid, gains[1], shifts[1]).astype(jnp.bfloat16)
    pre_act = jnp.dot(normed_two, full_up, preferred_element_type=jnp.float32) + hidden_shift
    act_bf = gelu_tanh(pre_act).astype(jnp.bfloat16)
    feed = lax.psum(
        jnp.einsum("tf,df->td", act_bf, full_down, preferred_element_type=jnp.float32).astype(
            jnp.bfloat16
        ),
        "tp",
    ).astype(jnp.float32)
    output = (resid + feed + out_shift[1]).astype(jnp.bfloat16).reshape(tokens.shape)
    back_qkv, back_out, back_up, back_down = gathered
    out_grad = cotangent.reshape(tok_rows, model_width).astype(jnp.float32)
    out_grad_bf = out_grad.astype(jnp.bfloat16)
    grad_down = jnp.einsum("td,tf->df", out_grad_bf, act_bf, preferred_element_type=jnp.float32)
    act_grad = jnp.dot(out_grad_bf, back_down, preferred_element_type=jnp.float32)
    pre_grad = jax.vjp(gelu_tanh, pre_act)[1](act_grad)[0]
    pre_grad_bf = pre_grad.astype(jnp.bfloat16)
    grad_up = jnp.einsum("td,tf->df", normed_two, pre_grad_bf, preferred_element_type=jnp.float32)
    hidden_grad = jnp.sum(pre_grad_bf.astype(jnp.float32), axis=0)
    norm_two_grad = lax.psum(
        jnp.einsum("tf,df->td", pre_grad_bf, back_up, preferred_element_type=jnp.float32).astype(
            jnp.bfloat16
        ),
        "tp",
    ).astype(jnp.float32)
    resid_part, gain_two, shift_two = jax.vjp(normalize, resid, gains[1], shifts[1])[1](
        norm_two_grad
    )
    resid_grad = out_grad + resid_part
    resid_bf = resid_grad.astype(jnp.bfloat16)
    grad_out = jnp.einsum("td,tf->df", resid_bf, attended_bf, preferred_element_type=jnp.float32)
    attend_grad_bf = jnp.dot(resid_bf, back_out, preferred_element_type=jnp.float32).astype(
        jnp.bfloat16
    )
    grad_heads = split_heads(attend_grad_bf)
    delta_row = jnp.sum(grad_heads.astype(jnp.float32) * attended_seq, axis=-1).transpose(0, 2, 1)
    head_zeros = jnp.zeros((seq_dev, group_len, heads_loc, HD), jnp.float32)

    def cycle_turn(turn_index, running):
        query_grad, visiting, key_grads = running
        for half_step in range(2):
            source = (cycle_index - 2 * turn_index - half_step) % cycle_size
            key_pos = positions * cycle_size + source
            query_term, key_term, value_term = grad_block(
                query_heads,
                grad_heads,
                log_total,
                delta_row,
                own_pos,
                split_heads(visiting[:, :, 0]),
                split_heads(visiting[:, :, 1]),
                key_pos,
                slopes,
            )
            query_grad = query_grad + query_term
            key_grads = key_grads + jnp.stack(
                [
                    key_term.reshape(seq_dev, group_len, local_width),
                    value_term.reshape(seq_dev, group_len, local_width),
                ],
                2,
            )
            visiting = shifted(visiting, "ctx", 1)
            key_grads = shifted(key_grads.astype(jnp.bfloat16), "ctx", 1).astype(key_grads.dtype)
        return (query_grad, visiting, key_grads)

    pair_zeros = jnp.zeros((seq_dev, group_len, 2, local_width), jnp.float32)
    query_grad, unused, key_grads = lax.fori_loop(
        0, cycle_size // 2, cycle_turn, (head_zeros, kv_pair, pair_zeros)
    )
    qkv_grad_bf = jnp.stack(
        [
            query_grad.reshape(tok_rows, local_width),
            key_grads[:, :, 0].reshape(tok_rows, local_width),
            key_grads[:, :, 1].reshape(tok_rows, local_width),
        ],
        1,
    ).astype(jnp.bfloat16)
    grad_qkv = jnp.einsum(
        "td,tcf->dcf", normed_one, qkv_grad_bf, preferred_element_type=jnp.float32
    )
    qv_grad = jnp.stack(
        [
            jnp.sum(qkv_grad_bf[:, 0].astype(jnp.float32), axis=0),
            jnp.sum(qkv_grad_bf[:, 2].astype(jnp.float32), axis=0),
        ]
    )
    norm_one_grad = lax.psum(
        jnp.einsum("tcf,dcf->td", qkv_grad_bf, back_qkv, preferred_element_type=jnp.float32).astype(
            jnp.bfloat16
        ),
        "tp",
    ).astype(jnp.float32)
    input_part, gain_one, shift_one = jax.vjp(normalize, resident, gains[0], shifts[0])[1](
        norm_one_grad
    )
    input_grad = (resid_grad + input_part).reshape(tokens.shape)
    gain_grads = jnp.stack([gain_one, gain_two])
    shift_grads = jnp.stack([shift_one, shift_two])
    out_bias_grad = jnp.stack([jnp.sum(resid_grad, axis=0), jnp.sum(out_grad, axis=0)])
    grad_qkv, grad_out, grad_up, grad_down = (
        lax.psum_scatter(grad_qkv, ("shard", "ctx"), scatter_dimension=0, tiled=True),
        lax.psum_scatter(grad_out, ("shard", "ctx"), scatter_dimension=0, tiled=True),
        lax.psum_scatter(grad_up, ("shard", "ctx"), scatter_dimension=0, tiled=True),
        lax.psum_scatter(grad_down, ("shard", "ctx"), scatter_dimension=0, tiled=True),
    )
    gain_grads, shift_grads, qv_grad, out_bias_grad, hidden_grad = lax.psum(
        (gain_grads, shift_grads, qv_grad, out_bias_grad, hidden_grad), ("shard", "ctx")
    )
    return (
        output,
        input_grad,
        gain_grads,
        shift_grads,
        grad_qkv,
        qv_grad,
        grad_out,
        out_bias_grad,
        grad_up,
        hidden_grad,
        grad_down,
    )


def solution(mesh):
    in_specs = (
        P("shard", None, "ctx", None),
        P("shard", None, "ctx", None),
        P(),
        P(),
        P("shard", None, "tp"),
        P(None, "tp"),
        P("shard", "tp"),
        P(),
        P("shard", "tp"),
        P("tp"),
        P("shard", "tp"),
    )
    out_specs = (
        P("shard", None, "ctx", None),
        P("shard", None, "ctx", None),
        P(),
        P(),
        P(("shard", "ctx"), None, "tp"),
        P(None, "tp"),
        P(("shard", "ctx"), "tp"),
        P(),
        P(("shard", "ctx"), "tp"),
        P("tp"),
        P(("shard", "ctx"), "tp"),
    )
    return jax.shard_map(
        per_device, mesh=mesh, in_specs=in_specs, out_specs=out_specs, check_vma=False
    )
```

profile of v0, /device:TPU:0, one launch (start us, length us, event | category | flops | bytes accessed | tf_op | source)
XLA Modules:
  0.0 780.9 jit_solution(4230939786621775822)
XLA Ops:
  10.5 29.1 %all-gather.5.cloned.1.call-done = bf16[1024,3,256]{2,0,1:T(8,128)(2,1)} async-done(((bf16[512,3,256]{2,0,1:T(8,128)(2,1)}), bf16[1024,3,256]{2,0,1:T(8,128)(2,1)}) %all-gather.5.cloned.1.call-update) | async-done | bytes 1572880 | tf_op jit(solution)/shard_map/all_gather | solution.py:102
  43.8 8.8 %all_gather.17 = bf16[1024,256]{1,0:T(8,128)(2,1)} all-gather(bf16[512,256]{1,0:T(8,128)(2,1)S(1)} %copy-done.32), channel_id=1, replica_groups=mesh['shard'=2,'ctx'=4,'tp'=4] {'shard'}, dimensions={0}, use_global_device_ids=true | all-gather | bytes 786432 | tf_op jit(solution)/shard_map/all_gather | solution.py:103
  53.5 36.1 %all-gather.7.cloned.1.call-done = bf16[2,256,4,2,256]{4,1,3,0,2:T(8,128)(2,1)} async-done(((bf16[2,256,1,2,256]{4,1,3,0,2:T(8,128)(2,1)}), bf16[2,256,4,2,256]{4,1,3,0,2:T(8,128)(2,1)}) %all-gather.7.cloned.1.call-update) | async-done | bytes 2097168 | tf_op jit(solution)/shard_map/all_gather | solution.py:123
  89.6 35.1 %while.38 = (s32[]{:T(128)}, f32[2,4,256]{2,1,0:T(4,128)S(1)}, f32[2,4,256]{2,1,0:T(4,128)S(1)}, f32[2,4,256,64]{2,3,1,0:T(8,128)}, s32[4]{0:T(128)S(1)}, /*inde...) while((s32[]{:T(128)}, f32[2,4,256]{2,1,0:T(4,128)S(1)}, ...), condition=%wide.region_5.6_spmd.clone, body=%wide.region_2.5_spmd.clone.sunk | while | flops 142420752 | bytes 21633332 | solution.py:145
  132.0 32.3 %all-reduce.6.cloned.1.call-done = bf16[512,1024]{1,0:T(8,128)(2,1)} async-done(((bf16[512,1024]{1,0:T(8,128)(2,1)}), bf16[512,1024]{1,0:T(8,128)(2,1)}) %all-reduce.6.cloned.1.call-update) | async-done | bytes 1048592 | tf_op jit(solution)/shard_map/psum | solution.py:151
  166.7 32.7 %all-gather.9.cloned.1.call-done = bf16[1024,1024]{1,0:T(8,128)(2,1)} async-done(((bf16[512,1024]{1,0:T(8,128)(2,1)}), bf16[1024,1024]{1,0:T(8,128)(2,1)}) %all-gather.9.cloned.1.call-update) | async-done | bytes 2097168 | tf_op jit(solution)/shard_map/all_gather | solution.py:104
  203.6 30.3 %all-gather.11.cloned.1.call-done = bf16[1024,1024]{1,0:T(8,128)(2,1)} async-done(((bf16[512,1024]{1,0:T(8,128)(2,1)}), bf16[1024,1024]{1,0:T(8,128)(2,1)}) %all-gather.11.cloned.1.call-update) | async-done | bytes 2097168 | tf_op jit(solution)/shard_map/all_gather | solution.py:105
  233.9 4.8 convert_reduce_fusion.3
  247.0 31.2 %all-reduce.8.cloned.1.call-done = bf16[512,1024]{1,0:T(8,128)(2,1)} async-done(((bf16[512,1024]{1,0:T(8,128)(2,1)}), bf16[512,1024]{1,0:T(8,128)(2,1)}) %all-reduce.8.cloned.1.call-update) | async-done | bytes 1048592 | tf_op jit(solution)/shard_map/psum | solution.py:177
  284.6 103.8 %while.39 = (s32[]{:T(128)}, f32[2,256,4,64]{1,3,2,0:T(8,128)}, bf16[2,256,2,256]{1,3,0,2:T(8,128)(2,1)}, f32[2,256,2,256]{1,3,0,2:T(8,128)}, s32[]{:T(128)}, /*...) while((s32[]{:T(128)}, f32[2,256,4,64]{1,3,2,0:T(8,128)}, ...), condition=%wide.region_15.16_spmd.clone.clone.clone.clone, body=%wide.region_14.15_spmd.clone.clone.clone.clone.sunk | while | flops 683672832 | bytes 55355044 | solution.py:225
  292.0 9.6 %collective-permute-done = bf16[2,256,2,256]{1,3,0,2:T(8,128)(2,1)} collective-permute-done((bf16[2,256,2,256]{1,3,0,2:T(8,128)(2,1)}, bf16[2,256,2,256]{1,3,0,2:T(8,128)(2,1)}, u32[]{:S(2)}, u32[]{:S(2)}) %collective-permute-start) | collective-permute-done | bytes 524320 | tf_op jit(solution)/shard_map/while/body/eval_jaxpr/ppermute | solution.py:19
  304.9 6.6 collective-permute-done.2
  315.3 14.0 %collective-permute-done.3 = bf16[2,256,2,256]{1,3,0,2:T(8,128)(2,1)S(1)} collective-permute-done((bf16[2,256,2,256]{1,3,0,2:T(8,128)(2,1)S(1)}, bf16[2,256,2,256]{1,3,0,2:T(8,128)(2,1)S(1)}, u32[]{:S(2)}, u32[]{:S(2)}) %collective-permute-start.3) | collective-permute-done | bytes 524320 | tf_op jit(solution)/shard_map/while/body/eval_jaxpr/ppermute | solution.py:19
  330.5 7.9 %collective-permute-done.1 = bf16[2,256,2,256]{1,3,0,2:T(8,128)(2,1)} collective-permute-done((bf16[2,256,2,256]{1,3,0,2:T(8,128)(2,1)}, bf16[2,256,2,256]{1,3,0,2:T(8,128)(2,1)}, u32[]{:S(2)}, u32[]{:S(2)}) %collective-permute-start.1) | collective-permute-done | bytes 524320 | tf_op jit(solution)/shard_map/while/body/eval_jaxpr/ppermute | solution.py:19
  342.7 12.6 %collective-permute-done = bf16[2,256,2,256]{1,3,0,2:T(8,128)(2,1)} collective-permute-done((bf16[2,256,2,256]{1,3,0,2:T(8,128)(2,1)}, bf16[2,256,2,256]{1,3,0,2:T(8,128)(2,1)}, u32[]{:S(2)}, u32[]{:S(2)}) %collective-permute-start) | collective-permute-done | bytes 524320 | tf_op jit(solution)/shard_map/while/body/eval_jaxpr/ppermute | solution.py:19
  366.3 14.9 %collective-permute-done.3 = bf16[2,256,2,256]{1,3,0,2:T(8,128)(2,1)S(1)} collective-permute-done((bf16[2,256,2,256]{1,3,0,2:T(8,128)(2,1)S(1)}, bf16[2,256,2,256]{1,3,0,2:T(8,128)(2,1)S(1)}, u32[]{:S(2)}, u32[]{:S(2)}) %collective-permute-start.3) | collective-permute-done | bytes 524320 | tf_op jit(solution)/shard_map/while/body/eval_jaxpr/ppermute | solution.py:19
  382.4 6.0 collective-permute-done.1
  394.6 5.1 convolution_bitcast_fusion
  415.4 27.6 %all-reduce.10.cloned.1.call-done = (bf16[512,1024]{1,0:T(8,128)(2,1)}, bf16[512,1024]{1,0:T(8,128)(2,1)}) async-done(((bf16[512,1024]{1,0:T(8,128)(2,1)}, bf16[512,1024]{1,0:T(8,128)(2,1)}), (bf16[512,1024]{1,0:T(8,128)(2,1)}, bf16[512,1024]{1,0:T(8,128)(2,1)})) %all-reduce.10.cloned.1.call-update) | async-done | bytes 2097168 | tf_op jit(solution)/shard_map/psum | solution.py:161
  453.1 40.0 %all-reduce = (f32[2,1024]{1,0:T(2,128)}, f32[2,1024]{1,0:T(2,128)}, f32[2,256]{1,0:T(2,128)}, f32[2,1024]{1,0:T(2,128)}, f32[1024]{0:T(1024)}) all-reduce(f32[2,1024]{1,0:T(2,128)S(1)} %get-tuple-element.700, f32[2,1024]{1,0:T(2,128)S(1)} %get-tuple-element.701, ...), channel_id=1, replica_groups=mesh['shard'=2,'ctx'=4,'tp'=4] {'shard','ctx'}, use_global_device_ids=true, to_apply=%region_21.22 | all-reduce | flops 7680 | bytes 61440 | tf_op jit(solution)/shard_map/psum | solution.py:264
  493.2 43.6 %reduce-scatter.11.cloned.1.call-done = f32[128,1024]{0,1:T(8,128)} async-done(((f32[1024,1024]{0,1:T(8,128)}), f32[128,1024]{0,1:T(8,128)}) %reduce-scatter.11.cloned.1.call-update) | async-done | bytes 524304 | tf_op jit(solution)/shard_map/reduce_scatter | solution.py:262
  538.8 65.2 %reduce-scatter.7.cloned.1.call-done = f32[128,256]{1,0:T(8,128)} async-done(((f32[1024,256]{1,0:T(8,128)}), f32[128,256]{1,0:T(8,128)}) %reduce-scatter.7.cloned.1.call-update) | async-done | bytes 131088 | tf_op jit(solution)/shard_map/reduce_scatter | solution.py:260
  604.0 78.4 %reduce-scatter.5.cloned.1.call-done = f32[128,3,256]{2,0,1:T(8,128)} async-done(((f32[1024,3,256]{2,0,1:T(8,128)}), f32[128,3,256]{2,0,1:T(8,128)}) %reduce-scatter.5.cloned.1.call-update) | async-done | bytes 393232 | tf_op jit(solution)/shard_map/reduce_scatter | solution.py:259
  682.4 92.0 %reduce-scatter.9.cloned.1.call-done = f32[128,1024]{1,0:T(8,128)} async-done(((f32[1024,1024]{1,0:T(8,128)}), f32[128,1024]{1,0:T(8,128)}) %reduce-scatter.9.cloned.1.call-update) | async-done | bytes 524304 | tf_op jit(solution)/shard_map/reduce_scatter | solution.py:261
  (320 shorter events, 129.0 us)
Async XLA Ops:
  7.2 32.3 %all-gather.5.cloned.1.call-start = ((), (), s32[]{:S(2)}) async-start(), calls=%async_computation.4 | async-start | bytes 2359296 | tf_op jit(solution)/shard_map/all_gather | solution.py:102
  8.0 81.7 %all-gather.7.cloned.1.call-start = ((), (), s32[]{:S(2)}) async-start(), calls=%async_computation.5 | async-start | bytes 2621440 | tf_op jit(solution)/shard_map/all_gather | solution.py:123
  10.4 31.5 %copy-start.29 = (bf16[512,1024]{1,0:T(8,128)(2,1)}, bf16[512,1024]{1,0:T(8,128)(2,1)S(1)}, u32[]{:S(2)}) copy-start(bf16[512,1024]{1,0:T(8,128)(2,1)S(1)} %fusion.56) | copy-start | bytes 3145732
  43.6 120.8 %all-reduce.6.cloned.1.call-start = ((), (), s32[]{:S(2)}) async-start(), calls=%async_computation.6 | async-start | bytes 2097152 | tf_op jit(solution)/shard_map/psum | solution.py:151
  129.4 34.9 %copy-start.1 = (bf16[2,256,1,1024]{3,1,2,0:T(8,128)(2,1)S(1)}, bf16[2,256,1,1024]{3,1,2,0:T(8,128)(2,1)}, u32[]{:S(2)}) copy-start(bf16[2,256,1,1024]{3,1,2,0:T(8,128)(2,1)} %param.15) | copy-start | bytes 3145732
  129.4 69.9 %all-gather.9.cloned.1.call-start = ((), (), s32[]{:S(2)}) async-start(), calls=%async_computation.7 | async-start | bytes 3145728 | tf_op jit(solution)/shard_map/all_gather | solution.py:104
  130.0 104.0 %all-gather.11.cloned.1.call-start = ((), (), s32[]{:S(2)}) async-start(), calls=%async_computation.8 | async-start | bytes 3145728 | tf_op jit(solution)/shard_map/all_gather | solution.py:105
  130.6 147.7 %all-reduce.8.cloned.1.call-start = ((), (), s32[]{:S(2)}) async-start(), calls=%async_computation.9 | async-start | bytes 2097152 | tf_op jit(solution)/shard_map/psum | solution.py:177
  166.7 114.4 %copy-start.3 = (f32[512,1024]{1,0:T(8,128)}, f32[512,1024]{1,0:T(8,128)S(1)}, u32[]{:S(2)}) copy-start(f32[512,1024]{1,0:T(8,128)S(1)} %get-tuple-element.665) | copy-start | bytes 6291460
  199.3 34.6 %copy-start.20 = (bf16[2,256,1,1024]{3,1,2,0:T(8,128)(2,1)S(1)}, bf16[2,256,1,1024]{3,1,2,0:T(8,128)(2,1)}, u32[]{:S(2)}) copy-start(bf16[2,256,1,1024]{3,1,2,0:T(8,128)(2,1)} %param.16) | copy-start | bytes 3145732
  242.0 201.1 %all-reduce.10.cloned.1.call-start = ((), (), s32[]{:S(2)}) async-start(), calls=%async_computation.14 | async-start | bytes 4194304 | tf_op jit(solution)/shard_map/psum | solution.py:161
  284.6 17.0 %collective-permute-start = (bf16[2,256,2,256]{1,3,0,2:T(8,128)(2,1)}, bf16[2,256,2,256]{1,3,0,2:T(8,128)(2,1)}, u32[]{:S(2)}, u32[]{:S(2)}) collective-permute-start(bf16[2,256,2,256]{1,3,0,2:T(8,128)(2,1)} %get-tuple-element.912), channel_id=1, source_target_pairs={{0,4},{4,8},{8,12},{12,0},{1,5},{5,9},{9,13},{13,1},{2,6},{6,10},{... | collective-permute-start | bytes 1572872 | tf_op jit(solution)/shard_map/while/body/eval_jaxpr/ppermute | solution.py:19
  290.5 21.0 %collective-permute-start.2 = (bf16[2,256,2,256]{1,3,0,2:T(8,128)(2,1)S(1)}, bf16[2,256,2,256]{1,3,0,2:T(8,128)(2,1)}, u32[]{:S(2)}, u32[]{:S(2)}) collective-permute-start(bf16[2,256,2,256]{1,3,0,2:T(8,128)(2,1)S(1)} %fusion.199), channel_id=1, source_target_pairs={{0,4},{4,8},{8,12},{12,0},{1,5},{5,9},{9,13},{13,1},{2,6},{6,10},{... | collective-permute-start | bytes 1572872 | tf_op jit(solution)/shard_map/while/body/eval_jaxpr/ppermute | solution.py:19
  312.6 16.7 %collective-permute-start.3 = (bf16[2,256,2,256]{1,3,0,2:T(8,128)(2,1)S(1)}, bf16[2,256,2,256]{1,3,0,2:T(8,128)(2,1)S(1)}, u32[]{:S(2)}, u32[]{:S(2)}) collective-permute-start(bf16[2,256,2,256]{1,3,0,2:T(8,128)(2,1)S(1)} %fusion.200), channel_id=1, source_target_pairs={{0,4},{4,8},{8,12},{12,0},{1,5},{5,9},{9,13},{13,1},{2,6},{6,10},{... | collective-permute-start | bytes 1572872 | tf_op jit(solution)/shard_map/while/body/eval_jaxpr/ppermute | solution.py:19
  312.7 25.7 %collective-permute-start.1 = (bf16[2,256,2,256]{1,3,0,2:T(8,128)(2,1)}, bf16[2,256,2,256]{1,3,0,2:T(8,128)(2,1)}, u32[]{:S(2)}, u32[]{:S(2)}) collective-permute-start(bf16[2,256,2,256]{1,3,0,2:T(8,128)(2,1)} %collective-permute-done), channel_id=1, source_target_pairs={{0,4},{4,8},{8,12},{12,0},{1,5},{5,9},{9,13},{13,1},{2,6},{6,10},{... | collective-permute-start | bytes 1572872 | tf_op jit(solution)/shard_map/while/body/eval_jaxpr/ppermute | solution.py:19
  338.4 17.0 %collective-permute-start = (bf16[2,256,2,256]{1,3,0,2:T(8,128)(2,1)}, bf16[2,256,2,256]{1,3,0,2:T(8,128)(2,1)}, u32[]{:S(2)}, u32[]{:S(2)}) collective-permute-start(bf16[2,256,2,256]{1,3,0,2:T(8,128)(2,1)} %get-tuple-element.912), channel_id=1, source_target_pairs={{0,4},{4,8},{8,12},{12,0},{1,5},{5,9},{9,13},{13,1},{2,6},{6,10},{... | collective-permute-start | bytes 1572872 | tf_op jit(solution)/shard_map/while/body/eval_jaxpr/ppermute | solution.py:19
  342.7 20.7 %collective-permute-start.2 = (bf16[2,256,2,256]{1,3,0,2:T(8,128)(2,1)S(1)}, bf16[2,256,2,256]{1,3,0,2:T(8,128)(2,1)}, u32[]{:S(2)}, u32[]{:S(2)}) collective-permute-start(bf16[2,256,2,256]{1,3,0,2:T(8,128)(2,1)S(1)} %fusion.199), channel_id=1, source_target_pairs={{0,4},{4,8},{8,12},{12,0},{1,5},{5,9},{9,13},{13,1},{2,6},{6,10},{... | collective-permute-start | bytes 1572872 | tf_op jit(solution)/shard_map/while/body/eval_jaxpr/ppermute | solution.py:19
  364.5 16.7 %collective-permute-start.3 = (bf16[2,256,2,256]{1,3,0,2:T(8,128)(2,1)S(1)}, bf16[2,256,2,256]{1,3,0,2:T(8,128)(2,1)S(1)}, u32[]{:S(2)}, u32[]{:S(2)}) collective-permute-start(bf16[2,256,2,256]{1,3,0,2:T(8,128)(2,1)S(1)} %fusion.200), channel_id=1, source_target_pairs={{0,4},{4,8},{8,12},{12,0},{1,5},{5,9},{9,13},{13,1},{2,6},{6,10},{... | collective-permute-start | bytes 1572872 | tf_op jit(solution)/shard_map/while/body/eval_jaxpr/ppermute | solution.py:19
  364.6 23.8 %collective-permute-start.1 = (bf16[2,256,2,256]{1,3,0,2:T(8,128)(2,1)}, bf16[2,256,2,256]{1,3,0,2:T(8,128)(2,1)}, u32[]{:S(2)}, u32[]{:S(2)}) collective-permute-start(bf16[2,256,2,256]{1,3,0,2:T(8,128)(2,1)} %collective-permute-done), channel_id=1, source_target_pairs={{0,4},{4,8},{8,12},{12,0},{1,5},{5,9},{9,13},{13,1},{2,6},{6,10},{... | collective-permute-start | bytes 1572872 | tf_op jit(solution)/shard_map/while/body/eval_jaxpr/ppermute | solution.py:19
  393.4 143.4 %reduce-scatter.11.cloned.1.call-start = ((), (), s32[]{:S(2)}) async-start(), calls=%async_computation.13 | async-start | bytes 4718592 | tf_op jit(solution)/shard_map/reduce_scatter | solution.py:262
  399.7 204.3 %reduce-scatter.7.cloned.1.call-start = ((), (), s32[]{:S(2)}) async-start(), calls=%async_computation.11 | async-start | bytes 1179648 | tf_op jit(solution)/shard_map/reduce_scatter | solution.py:260
  403.7 278.7 %reduce-scatter.5.cloned.1.call-start = ((), (), s32[]{:S(2)}) async-start(), calls=%async_computation.10 | async-start | bytes 3538944 | tf_op jit(solution)/shard_map/reduce_scatter | solution.py:259
  408.0 366.4 %reduce-scatter.9.cloned.1.call-start = ((), (), s32[]{:S(2)}) async-start(), calls=%async_computation.12 | async-start | bytes 4718592 | tf_op jit(solution)/shard_map/reduce_scatter | solution.py:261
  414.2 28.8 %copy-start.2 = (bf16[2,256,1,1024]{3,1,2,0:T(8,128)(2,1)S(1)}, bf16[2,256,1,1024]{3,1,2,0:T(8,128)(2,1)}, u32[]{:S(2)}) copy-start(bf16[2,256,1,1024]{3,1,2,0:T(8,128)(2,1)} %param.15) | copy-start | bytes 3145732
  (48 other events, 109.5 us)
Sparse Core Ops, SparseCore 0:
  9.6 29.8 all-gather.4
  43.7 45.8 all-gather.6
  129.5 34.7 all-reduce.5
  165.8 33.4 all-gather.8
  200.8 33.1 all-gather.10
  242.1 36.0 all-reduce.7
  393.5 49.5 all-reduce.9
  447.2 89.5 reduce-scatter.10
  540.8 63.2 reduce-scatter.6
  608.5 73.9 reduce-scatter.4
  687.1 87.2 reduce-scatter.8
where the time goes:
time: 782 us; the launch traced here: 781 us
  waiting for transfers between devices  577 us (74%)
  matrix products  55.5 us (7%)
  blocking collectives  48.8 us (6%)
  local copies, waits for them, and re-layouts  37.9 us (5%)
  other arithmetic  33.5 us (4%)
  between operations  14.5 us (2%)
  loops' own time  8.45 us (1%)
    reduce_scatter x1, waiting for transfers between devices, per_device(): lax.psum_scatter(grad_up, ('shard', 'ctx'), scatter_dimension=0, tiled=True)  92 us
    reduce_scatter x1, waiting for transfers between devices, per_device(): lax.psum_scatter(grad_qkv, ('shard', 'ctx'), scatter_dimension=0, tiled=T...  78.4 us
    ppermute x8, waiting for transfers between devices, shifted(): return lax.ppermute(value, axis, pairs)  76.5 us
    reduce_scatter x1, waiting for transfers between devices, per_device(): lax.psum_scatter(grad_out, ('shard', 'ctx'), scatter_dimension=0, tiled=T...  65.2 us
    reduce_scatter x1, waiting for transfers between devices, per_device(): lax.psum_scatter(grad_down, ('shard', 'ctx'), scatter_dimension=0, tiled=...  43.6 us
    psum x1, blocking collectives, per_device(): lax.psum((gain_grads, shift_grads, qv_grad, out_bias_grad, hidden_grad),...  40 us
    all_gather x1, waiting for transfers between devices, per_device(): arrived = lax.all_gather(kv_single, 'ctx', axis=2, tiled=True)  36.1 us
    all_gather x1, waiting for transfers between devices, per_device(): lax.all_gather(w_up, 'shard', axis=0, tiled=True)  32.7 us
  transfers between devices with their start and end apart: 19, of which 19 were waited for; matrix products, arithmetic and copies ran while one was open for 8% of the time, Pallas kernels for 0%

commit v1 on v0

v1 whole, which is shorter than its diff:
```python
import functools
import math

import jax
import jax.numpy as jnp
from jax import lax
from jax.experimental import pallas as pl
from jax.experimental.pallas import tpu as pltpu
from jax.sharding import PartitionSpec as P

H = 16
HD = 64


EPSILON = 1e-05
FLOOR_SCORE = -1e30


def shifted(value, axis, steps):
    count = lax.axis_size(axis)
    pairs = [(source, (source + steps) % count) for source in range(count)]
    return lax.ppermute(value, axis, pairs)


def normalize(values, scale_by, offset):
    average = jnp.mean(values, axis=-1, keepdims=True)
    centred = values - average
    spread = jnp.mean(centred * centred, axis=-1, keepdims=True)
    return centred * lax.rsqrt(spread + EPSILON) * scale_by + offset


def gelu_tanh(values):
    return jax.nn.gelu(values, approximate=True)


def score_block(query_h, key_h, query_pos, key_pos, slopes):
    logits = jnp.einsum("sqhd,skhd->shqk", query_h, key_h, preferred_element_type=jnp.float32) * (
        1.0 / math.sqrt(query_h.shape[-1])
    )
    distance = (query_pos[:, None] - key_pos[None, :]).astype(jnp.float32)
    logits = logits - slopes[None, :, None, None] * distance[None, None]
    allowed = (key_pos[None, :] <= query_pos[:, None])[None, None]
    return (logits, allowed)


def grad_block(query_h, grad_h, log_total, delta_row, query_pos, key_h, value_h, key_pos, slopes):
    scale_by = 1.0 / math.sqrt(query_h.shape[-1])
    logits, allowed = score_block(query_h, key_h, query_pos, key_pos, slopes)
    probs = jnp.where(allowed, jnp.exp(logits - log_total[..., None]), 0.0)
    prob_grad = jnp.einsum("sqhd,skhd->shqk", grad_h, value_h, preferred_element_type=jnp.float32)
    score_grad = (probs * (prob_grad - delta_row[..., None])).astype(jnp.bfloat16)
    query_term = (
        jnp.einsum("shqk,skhd->sqhd", score_grad, key_h, preferred_element_type=jnp.float32)
        * scale_by
    )
    key_term = (
        jnp.einsum("shqk,sqhd->skhd", score_grad, query_h, preferred_element_type=jnp.float32)
        * scale_by
    )
    value_term = jnp.einsum(
        "shqk,sqhd->skhd", probs.astype(jnp.bfloat16), grad_h, preferred_element_type=jnp.float32
    )
    return (query_term, key_term, value_term)


def exchanged(value, axis, mask):
    count = lax.axis_size(axis)
    return lax.ppermute(value, axis, [(source, source ^ mask) for source in range(count)])


def power_of_two(count):
    return count > 1 and count & (count - 1) == 0


def add_bf(left, right):
    return (left.astype(jnp.float32) + right.astype(jnp.float32)).astype(jnp.bfloat16)


def sum_over_tp(partial):
    count = lax.axis_size("tp")
    partial = partial.astype(jnp.bfloat16)
    if not power_of_two(count):
        return lax.psum(partial, "tp").astype(jnp.float32)
    rows = partial.shape[0] // 2
    even = lax.axis_index("tp") % 2 == 0
    low, high = partial[:rows], partial[rows:]
    total = add_bf(
        jnp.where(even, low, high), exchanged(jnp.where(even, high, low), "tp", 1)
    )
    mask = 2
    while mask < count:
        total = add_bf(total, exchanged(total, "tp", mask))
        mask *= 2
    other = exchanged(total, "tp", 1)
    return jnp.concatenate(
        [jnp.where(even, total, other), jnp.where(even, other, total)], 0
    ).astype(jnp.float32)


def sum_small(values, axes):
    flat = jnp.concatenate([value.reshape(-1) for value in values]).reshape(-1, 128)
    for axis in axes:
        count = lax.axis_size(axis)
        if not power_of_two(count):
            flat = lax.psum(flat, axis)
            continue
        mask = 1
        while mask < count:
            flat = flat + exchanged(flat, axis, mask)
            mask *= 2
    flat = flat.reshape(-1)
    results, start = [], 0
    for value in values:
        results.append(flat[start : start + value.size].reshape(value.shape))
        start += value.size
    return results


def whole_rows(block):
    if lax.axis_size("shard") != 2:
        return lax.all_gather(block, "shard", axis=0, tiled=True)
    other = exchanged(block, "shard", 1)
    first = lax.axis_index("shard") == 0
    return jnp.concatenate([jnp.where(first, block, other), jnp.where(first, other, block)], 0)


def outer(left, right):
    return jnp.einsum("td,tf->df", left, right, preferred_element_type=jnp.float32)


def owned_grad(left, right):
    count = lax.axis_size("ctx")
    if lax.axis_size("shard") != 2:
        return lax.psum_scatter(
            outer(left, right), ("shard", "ctx"), scatter_dimension=0, tiled=True
        )
    half_width = left.shape[1] // 2
    shard = lax.axis_index("shard")
    theirs = lax.dynamic_slice_in_dim(left, (1 - shard) * half_width, half_width, 1)
    mine = lax.dynamic_slice_in_dim(left, shard * half_width, half_width, 1)
    half = outer(mine, right) + exchanged(
        outer(theirs, right).astype(jnp.bfloat16), "shard", 1
    ).astype(jnp.float32)
    if count > 8:
        return lax.psum_scatter(half, "ctx", scatter_dimension=0, tiled=True)
    chunks = half.reshape(count, half_width // count, half.shape[1])
    me = lax.axis_index("ctx")

    def chunk(back):
        return lax.dynamic_index_in_dim(
            chunks, lax.rem(me + 2 * count - back, count), 0, keepdims=False
        )

    moving = chunk(1)
    for step in range(count - 1):
        arrived = shifted(moving.astype(jnp.bfloat16), "ctx", 1)
        moving = arrived.astype(jnp.float32) + chunk(step + 2)
    return moving


def spread_heads(groups):
    count = lax.axis_size("ctx")
    me = lax.axis_index("ctx")
    slots = []
    for step in range(count):
        group = lax.dynamic_index_in_dim(groups, lax.rem(me + step, count), 0, keepdims=False)
        slots.append(shifted(group, "ctx", step) if step else group)
    return jnp.stack(slots)


def return_heads(slots):
    count = lax.axis_size("ctx")
    me = lax.axis_index("ctx")
    groups = [shifted(slots[step], "ctx", -step) if step else slots[0] for step in range(count)]
    return lax.dynamic_slice_in_dim(jnp.stack(groups + groups), count - me, count, 0)


def head_parts(ref, column, blocks):
    slots, rows = ref.shape[0], ref.shape[2] // blocks
    return [
        jnp.concatenate(
            [
                ref[slot, 0, block * rows : (block + 1) * rows, column : column + HD]
                for slot in range(slots)
            ],
            0,
        )
        for block in range(blocks)
    ]


def dot_rows(left, right):
    return lax.dot_general(
        left, right, (((1,), (1,)), ((), ())), preferred_element_type=jnp.float32
    )


def dot_plain(left, right):
    return lax.dot_general(
        left, right, (((1,), (0,)), ((), ())), preferred_element_type=jnp.float32
    )


def dot_columns(left, right):
    return lax.dot_general(
        left, right, (((0,), (0,)), ((), ())), preferred_element_type=jnp.float32
    )


def block_weights(query, keys, bias_row, place_row, place_column, scale_by):
    logits = dot_rows(query, keys) * scale_by + bias_row
    logits = jnp.where(place_row <= place_column, logits, FLOOR_SCORE)
    weights = jnp.exp(logits - jnp.max(logits, axis=1, keepdims=True))
    return weights, 1.0 / jnp.sum(weights, axis=1, keepdims=True)


def attend_kernel(blocks, heads, scale_by, bias_ref, row_ref, column_ref, in_ref, out_ref):
    slots, rows = in_ref.shape[0], in_ref.shape[2] // blocks
    size = slots * rows
    for head in range(heads):
        queries, keys, values = (
            head_parts(in_ref, (kind * heads + head) * HD, blocks) for kind in range(3)
        )
        for block in range(blocks):
            reach = (block + 1) * size
            weights, inverse = block_weights(
                queries[block],
                jnp.concatenate(keys[: block + 1], 0),
                bias_ref[head, :, :reach],
                row_ref[:, :reach],
                column_ref[block * size : reach, :],
                scale_by,
            )
            result = (
                dot_plain(
                    weights.astype(jnp.bfloat16), jnp.concatenate(values[: block + 1], 0)
                )
                * inverse
            ).astype(out_ref.dtype)
            for slot in range(slots):
                out_ref[
                    slot, 0, block * rows : (block + 1) * rows, head * HD : (head + 1) * HD
                ] = result[slot * rows : (slot + 1) * rows]


def attend_back_kernel(
    blocks, heads, scale_by, bias_ref, row_ref, column_ref, in_ref, grad_ref, out_ref
):
    slots, rows = in_ref.shape[0], in_ref.shape[2] // blocks
    size = slots * rows

    def store(block, column, value):
        value = value.astype(out_ref.dtype)
        for slot in range(slots):
            out_ref[slot, 0, block * rows : (block + 1) * rows, column : column + HD] = value[
                slot * rows : (slot + 1) * rows
            ]

    for head in range(heads):
        columns = [(kind * heads + head) * HD for kind in range(3)]
        queries, keys, values = (head_parts(in_ref, column, blocks) for column in columns)
        grads = head_parts(grad_ref, head * HD, blocks)
        key_grads, value_grads = [None] * blocks, [None] * blocks
        for block in range(blocks - 1, -1, -1):
            reach = (block + 1) * size
            near_keys = jnp.concatenate(keys[: block + 1], 0)
            weights, inverse = block_weights(
                queries[block],
                near_keys,
                bias_ref[head, :, :reach],
                row_ref[:, :reach],
                column_ref[block * size : reach, :],
                scale_by,
            )
            probs = weights * inverse
            prob_grad = dot_rows(grads[block], jnp.concatenate(values[: block + 1], 0))
            delta = jnp.sum(probs * prob_grad, axis=1, keepdims=True)
            score_grad = (probs * (prob_grad - delta)).astype(jnp.bfloat16)
            store(block, columns[0], dot_plain(score_grad, near_keys) * scale_by)
            key_term = dot_columns(score_grad, queries[block])
            value_term = dot_columns(probs.astype(jnp.bfloat16), grads[block])
            for near in range(block + 1):
                span = slice(near * size, (near + 1) * size)
                if key_grads[near] is None:
                    key_grads[near], value_grads[near] = key_term[span], value_term[span]
                else:
                    key_grads[near] = key_grads[near] + key_term[span]
                    value_grads[near] = value_grads[near] + value_term[span]
        for block in range(blocks):
            store(block, columns[1], key_grads[block] * scale_by)
            store(block, columns[2], value_grads[block])


def head_call(kernel, blocks, heads, tables, arrays, width, flops):
    slots, seqs, rows = arrays[0].shape[:3]

    def table_spec(table):
        return pl.BlockSpec(table.shape, lambda seq: (0,) * table.ndim)

    def slot_spec(columns):
        return pl.BlockSpec((slots, 1, rows, columns), lambda seq: (0, seq, 0, 0))

    return pl.pallas_call(
        functools.partial(kernel, blocks, heads, 1.0 / math.sqrt(HD)),
        grid=(seqs,),
        out_shape=jax.ShapeDtypeStruct((slots, seqs, rows, width), jnp.bfloat16),
        in_specs=[table_spec(table) for table in tables]
        + [slot_spec(array.shape[3]) for array in arrays],
        out_specs=slot_spec(width),
        compiler_params=pltpu.CompilerParams(vmem_limit_bytes=40 * 2**20),
        cost_estimate=pl.CostEstimate(
            flops=flops, bytes_accessed=2 * slots * seqs * rows * 512, transcendentals=0
        ),
    )(*tables, *arrays)


def attend_spread(queries, keys, values, slopes, seqs, rows):
    count = lax.axis_size("ctx")
    me = lax.axis_index("ctx")
    heads = slopes.shape[0] // count
    tokens = seqs * rows
    blocks = 4 if rows % 64 == 0 else 1
    width = heads * HD
    grouped = jnp.stack([queries, keys, values], 1).reshape(tokens, 3, count, width)
    grouped = grouped.transpose(2, 0, 1, 3).reshape(count, tokens, 3 * width)
    spread = spread_heads(grouped).reshape(count, seqs, rows, 3 * width)
    own_slopes = lax.dynamic_slice_in_dim(slopes, me * heads, heads, 0)
    owner = lax.rem(me + count - jnp.arange(count, dtype=jnp.int32), count)
    places = (
        jnp.arange(rows, dtype=jnp.int32).reshape(blocks, 1, rows // blocks) * count
        + owner[None, :, None]
    )
    places = places.reshape(-1).astype(jnp.float32)
    tables = (
        (own_slopes[:, None] * places[None, :])[:, None, :],
        places[None, :],
        places[:, None],
    )
    pairs = heads * seqs * (rows * count) ** 2 * HD
    attended = head_call(
        attend_kernel, blocks, heads, tables, (spread,), width, 3 * pairs
    )

    def homeward(slots, kinds):
        groups = return_heads(slots.reshape(count, tokens, kinds * width))
        groups = groups.reshape(count, tokens, kinds, width).transpose(1, 2, 0, 3)
        return groups.reshape(tokens, kinds, count * width)

    def back(grads):
        grouped_grads = grads.reshape(tokens, count, width).transpose(1, 0, 2)
        spread_grads = spread_heads(grouped_grads).reshape(count, seqs, rows, width)
        slots = head_call(
            attend_back_kernel, blocks, heads, tables, (spread, spread_grads), 3 * width, 8 * pairs
        )
        return homeward(slots, 3)

    return homeward(attended, 1)[:, 0], back


def attend_ring(query_bf, key_bf, value_bf, slopes, seq_dev, group_len):
    tok_rows = seq_dev * group_len
    heads_loc = slopes.shape[0]
    local_width = query_bf.shape[1]
    cycle_size = lax.axis_size("ctx")
    cycle_index = lax.axis_index("ctx")
    positions = jnp.arange(group_len, dtype=jnp.int32)
    own_pos = positions * cycle_size + cycle_index

    def split_heads(matrix):
        return matrix.reshape(seq_dev, group_len, heads_loc, HD)

    query_heads = split_heads(query_bf)
    kv_pair = jnp.stack([key_bf, value_bf], 1).reshape(seq_dev, group_len, 2, local_width)
    kv_single = kv_pair.reshape(seq_dev, group_len, 1, 2, local_width)
    stat_zeros = jnp.zeros((seq_dev, heads_loc, group_len), jnp.float32)
    initial = (
        jnp.full((seq_dev, heads_loc, group_len), FLOOR_SCORE, jnp.float32),
        stat_zeros,
        jnp.zeros((seq_dev, heads_loc, group_len, HD), jnp.float32),
    )
    running = initial
    arrived = lax.all_gather(kv_single, "ctx", axis=2, tiled=True)

    def per_source(running_in, source_step):
        source_block = lax.dynamic_index_in_dim(arrived, source_step, 2, keepdims=False)
        src_keys = split_heads(source_block[:, :, 0])
        src_values = split_heads(source_block[:, :, 1])
        key_pos = positions * cycle_size + source_step
        logits, allowed = score_block(query_heads, src_keys, own_pos, key_pos, slopes)
        run_top, run_total, run_sum = running_in
        row_top = jnp.max(jnp.where(allowed, logits, FLOOR_SCORE), axis=-1)
        fresh_top = jnp.maximum(run_top, row_top)
        weights = jnp.where(allowed, jnp.exp(logits - fresh_top[..., None]), 0.0)
        fade_by = jnp.exp(run_top - fresh_top)
        run_total = run_total * fade_by + jnp.sum(weights, axis=-1)
        run_sum = run_sum * fade_by[..., None] + jnp.einsum(
            "shqk,skhd->shqd",
            weights.astype(jnp.bfloat16),
            src_values,
            preferred_element_type=jnp.float32,
        )
        return ((fresh_top, run_total, run_sum), None)

    running, unused = lax.scan(per_source, running, jnp.arange(arrived.shape[2], dtype=jnp.int32))
    run_top, run_total, run_sum = running
    attended = run_sum / run_total[..., None]
    log_total = run_top + jnp.log(run_total)
    attended_seq = attended.transpose(0, 2, 1, 3)
    attended_bf = attended_seq.reshape(tok_rows, local_width).astype(jnp.bfloat16)

    def back(attend_grad_bf):
        grad_heads = split_heads(attend_grad_bf)
        delta_row = jnp.sum(grad_heads.astype(jnp.float32) * attended_seq, axis=-1).transpose(0, 2, 1)
        head_zeros = jnp.zeros((seq_dev, group_len, heads_loc, HD), jnp.float32)

        def cycle_turn(turn_index, running):
            query_grad, visiting, key_grads = running
            for half_step in range(2):
                source = (cycle_index - 2 * turn_index - half_step) % cycle_size
                key_pos = positions * cycle_size + source
                query_term, key_term, value_term = grad_block(
                    query_heads,
                    grad_heads,
                    log_total,
                    delta_row,
                    own_pos,
                    split_heads(visiting[:, :, 0]),
                    split_heads(visiting[:, :, 1]),
                    key_pos,
                    slopes,
                )
                query_grad = query_grad + query_term
                key_grads = key_grads + jnp.stack(
                    [
                        key_term.reshape(seq_dev, group_len, local_width),
                        value_term.reshape(seq_dev, group_len, local_width),
                    ],
                    2,
                )
                visiting = shifted(visiting, "ctx", 1)
                key_grads = shifted(key_grads.astype(jnp.bfloat16), "ctx", 1).astype(key_grads.dtype)
            return (query_grad, visiting, key_grads)

        pair_zeros = jnp.zeros((seq_dev, group_len, 2, local_width), jnp.float32)
        query_grad, unused, key_grads = lax.fori_loop(
            0, cycle_size // 2, cycle_turn, (head_zeros, kv_pair, pair_zeros)
        )
        return jnp.stack(
            [
                query_grad.reshape(tok_rows, local_width),
                key_grads[:, :, 0].reshape(tok_rows, local_width),
                key_grads[:, :, 1].reshape(tok_rows, local_width),
            ],
            1,
        ).astype(jnp.bfloat16)

    return attended_bf, back


def per_device(
    tokens,
    cotangent,
    norm_gain,
    norm_bias,
    w_qkv,
    qv_bias,
    w_out,
    out_bias,
    w_up,
    hidden_bias,
    w_down,
):
    seq_dev, group_len, model_width = (tokens.shape[0], tokens.shape[1], tokens.shape[3])
    tok_rows = seq_dev * group_len
    local_width = w_qkv.shape[2]
    heads_loc = local_width // HD
    cycle_size = lax.axis_size("ctx")
    slopes = jnp.exp2(
        -8.0
        * (lax.axis_index("tp") * heads_loc + jnp.arange(heads_loc, dtype=jnp.int32) + 1).astype(
            jnp.float32
        )
        / H
    )
    resident = tokens.reshape(tok_rows, model_width).astype(jnp.float32)
    gains = norm_gain.astype(jnp.float32)
    shifts = norm_bias.astype(jnp.float32)
    out_shift = out_bias.astype(jnp.float32)
    qv_shift = qv_bias.astype(jnp.float32)
    hidden_shift = hidden_bias.astype(jnp.float32)
    gathered = (
        whole_rows(w_qkv.reshape(w_qkv.shape[0], 3 * local_width)),
        whole_rows(w_out),
        whole_rows(w_up),
        whole_rows(w_down),
    )
    full_qkv, full_out, full_up, full_down = gathered
    normed_one = normalize(resident, gains[0], shifts[0]).astype(jnp.bfloat16)
    projected = jnp.dot(normed_one, full_qkv, preferred_element_type=jnp.float32)
    projected = projected.reshape(tok_rows, 3, local_width)
    query_bf = (projected[:, 0] + qv_shift[0]).astype(jnp.bfloat16)
    key_bf = projected[:, 1].astype(jnp.bfloat16)
    value_bf = (projected[:, 2] + qv_shift[1]).astype(jnp.bfloat16)
    attend = attend_spread if heads_loc % cycle_size == 0 else attend_ring
    attended_bf, attend_back = attend(query_bf, key_bf, value_bf, slopes, seq_dev, group_len)
    branch = sum_over_tp(
        jnp.einsum("tf,df->td", attended_bf, full_out, preferred_element_type=jnp.float32)
    )
    resid = resident + branch + out_shift[0]
    normed_two = normalize(resid, gains[1], shifts[1]).astype(jnp.bfloat16)
    pre_act = jnp.dot(normed_two, full_up, preferred_element_type=jnp.float32) + hidden_shift
    act_bf = gelu_tanh(pre_act).astype(jnp.bfloat16)
    feed = sum_over_tp(
        jnp.einsum("tf,df->td", act_bf, full_down, preferred_element_type=jnp.float32)
    )
    output = (resid + feed + out_shift[1]).astype(jnp.bfloat16).reshape(tokens.shape)
    back_qkv, back_out, back_up, back_down = gathered
    out_grad = cotangent.reshape(tok_rows, model_width).astype(jnp.float32)
    out_grad_bf = out_grad.astype(jnp.bfloat16)
    grad_down = owned_grad(out_grad_bf, act_bf)
    act_grad = jnp.dot(out_grad_bf, back_down, preferred_element_type=jnp.float32)
    pre_grad = jax.vjp(gelu_tanh, pre_act)[1](act_grad)[0]
    pre_grad_bf = pre_grad.astype(jnp.bfloat16)
    grad_up = owned_grad(normed_two, pre_grad_bf)
    hidden_grad = jnp.sum(pre_grad_bf.astype(jnp.float32), axis=0)
    norm_two_grad = sum_over_tp(
        jnp.einsum("tf,df->td", pre_grad_bf, back_up, preferred_element_type=jnp.float32)
    )
    resid_part, gain_two, shift_two = jax.vjp(normalize, resid, gains[1], shifts[1])[1](
        norm_two_grad
    )
    resid_grad = out_grad + resid_part
    resid_bf = resid_grad.astype(jnp.bfloat16)
    grad_out = owned_grad(resid_bf, attended_bf)
    attend_grad_bf = jnp.dot(resid_bf, back_out, preferred_element_type=jnp.float32).astype(
        jnp.bfloat16
    )
    qkv_grad_bf = attend_back(attend_grad_bf)
    qkv_grad_flat = qkv_grad_bf.reshape(tok_rows, 3 * local_width)
    grad_qkv = owned_grad(normed_one, qkv_grad_flat)
    grad_qkv = grad_qkv.reshape(grad_qkv.shape[0], 3, local_width)
    qv_grad = jnp.stack(
        [
            jnp.sum(qkv_grad_bf[:, 0].astype(jnp.float32), axis=0),
            jnp.sum(qkv_grad_bf[:, 2].astype(jnp.float32), axis=0),
        ]
    )
    norm_one_grad = sum_over_tp(
        jnp.einsum("tf,df->td", qkv_grad_flat, back_qkv, preferred_element_type=jnp.float32)
    )
    input_part, gain_one, shift_one = jax.vjp(normalize, resident, gains[0], shifts[0])[1](
        norm_one_grad
    )
    input_grad = (resid_grad + input_part).reshape(tokens.shape)
    gain_grads = jnp.stack([gain_one, gain_two])
    shift_grads = jnp.stack([shift_one, shift_two])
    out_bias_grad = jnp.stack([jnp.sum(resid_grad, axis=0), jnp.sum(out_grad, axis=0)])
    gain_grads, shift_grads, qv_grad, out_bias_grad, hidden_grad = sum_small(
        (gain_grads, shift_grads, qv_grad, out_bias_grad, hidden_grad), ("shard", "ctx")
    )
    return (
        output,
        input_grad,
        gain_grads,
        shift_grads,
        grad_qkv,
        qv_grad,
        grad_out,
        out_bias_grad,
        grad_up,
        hidden_grad,
        grad_down,
    )


def solution(mesh):
    in_specs = (
        P("shard", None, "ctx", None),
        P("shard", None, "ctx", None),
        P(),
        P(),
        P("shard", None, "tp"),
        P(None, "tp"),
        P("shard", "tp"),
        P(),
        P("shard", "tp"),
        P("tp"),
        P("shard", "tp"),
    )
    out_specs = (
        P("shard", None, "ctx", None),
        P("shard", None, "ctx", None),
        P(),
        P(),
        P(("shard", "ctx"), None, "tp"),
        P(None, "tp"),
        P(("shard", "ctx"), "tp"),
        P(),
        P(("shard", "ctx"), "tp"),
        P("tp"),
        P(("shard", "ctx"), "tp"),
    )
    return jax.shard_map(
        per_device, mesh=mesh, in_specs=in_specs, out_specs=out_specs, check_vma=False
    )
```

time: 782 us -> 391 us (0.50)
  waiting for transfers between devices: 577 us -> 125 us
  other arithmetic: 33.5 us -> 114 us
  starting transfers between devices: 5.33 us -> 77.5 us
  blocking collectives: 48.8 us -> 0 us
  matrix products: 55.5 us -> 22.6 us
  between operations: 14.5 us -> 2.36 us
  Pallas kernels: 0 us -> 11.9 us
  loops' own time: 8.45 us -> 0 us
    reduce_scatter x4 -> x0, waiting for transfers between devices: 279 us -> none  [the longest x1 92 us: per_device(): lax.psum_scatter(grad_up, ('shard', 'ctx'), scatter_dimension=0, tiled=True)]
    all_gather x4 -> x0, waiting for transfers between devices: 128 us -> none  [the longest x1 36.1 us: per_device(): arrived = lax.all_gather(kv_single, 'ctx', axis=2, tiled=True)]
    psum x3 -> x0, waiting for transfers between devices: 91.1 us -> none  [the longest x1 32.3 us: per_device(): lax.psum(jnp.einsum('tf,df->td', attended_bf, full_out, preferred_element...]
    ppermute x0 -> x23, waiting for transfers between devices: none -> 78.2 us  [exchanged(): lax.ppermute(value, axis, [(source, source ^ mask) for source in range(co...]
    ppermute x8 -> x24, starting transfers between devices: 4.23 us -> 49.8 us  [shifted(): return lax.ppermute(value, axis, pairs)]
    psum x1 -> x0, blocking collectives: 40 us -> none  [per_device(): lax.psum((gain_grads, shift_grads, qv_grad, out_bias_grad, hidden_grad),...]
    ppermute x8 -> x24, waiting for transfers between devices: 76.5 us -> 46.4 us  [shifted(): return lax.ppermute(value, axis, pairs)]
    ppermute x0 -> x23, starting transfers between devices: none -> 27.7 us  [exchanged(): lax.ppermute(value, axis, [(source, source ^ mask) for source in range(co...]
  transfers between devices with their start and end apart: 19 -> 47, of which waited for: 19 -> 20; matrix products, arithmetic and copies ran while one was open for 8% -> 35% of each run, Pallas kernels for 0% -> 2%
where the time goes in v1:
time: 391 us; the launch traced here: 387 us
  waiting for transfers between devices  125 us (32%)
  other arithmetic  114 us (29%)
  starting transfers between devices  77.5 us (20%)
  local copies, waits for them, and re-layouts  33.4 us (9%)
  matrix products  22.6 us (6%)
  Pallas kernels  11.9 us (3%)
    ppermute x23, waiting for transfers between devices, exchanged(): lax.ppermute(value, axis, [(source, source ^ mask) for source in range(co...  78.2 us
    ppermute x24, starting transfers between devices, shifted(): return lax.ppermute(value, axis, pairs)  49.8 us
    ppermute x24, waiting for transfers between devices, shifted(): return lax.ppermute(value, axis, pairs)  46.4 us
    ppermute x23, starting transfers between devices, exchanged(): lax.ppermute(value, axis, [(source, source ^ mask) for source in range(co...  27.7 us
    reduce_sum x3, other arithmetic, normalize(): return centred * lax.rsqrt(spread + EPSILON) * scale_by + offset  20.7 us
    reduce_sum x2, other arithmetic, normalize(): centred = values - average  19.7 us
    unnamed x124, local copies, waits for them, and re-layouts  16.5 us
    reduce_sum x2, other arithmetic, normalize(): spread = jnp.mean(centred * centred, axis=-1, keepdims=True)  15.6 us
  transfers between devices with their start and end apart: 47, of which 20 were waited for; matrix products, arithmetic and copies ran while one was open for 35% of the time, Pallas kernels for 2%

profile of v1, /device:TPU:0, one launch (start us, length us, event | category | flops | bytes accessed | tf_op | source)
XLA Modules:
  0.0 386.6 jit_solution(9244768336915082903)
XLA Ops:
  8.2 8.0 %multiply_reduce_fusion.5 = f32[2,256]{1,0:T(2,128)S(1)} fusion(f32[2,256]{1,0:T(2,128)S(1)} %get-tuple-element.110, bf16[2,256,1,1024]{3,1,2,0:T(8,128)(2,1)S(1)} %copy-done), kind=kLoop, calls=%fused_computation.49 | loop fusion | flops 2096640 | bytes 1052672 | tf_op jit(solution)/shard_map/reduce_sum | solution.py:28
  39.5 10.4 %collective-permute-done.2 = bf16[512,192]{0,1:T(8,128)(2,1)} collective-permute-done((bf16[512,192]{0,1:T(8,128)(2,1)S(1)}, bf16[512,192]{0,1:T(8,128)(2,1)}, u32[]{:S(2)}, u32[]{:S(2)}) %collective-permute-start.2) | collective-permute-done | bytes 196640 | tf_op jit(solution)/shard_map/ppermute | solution.py:22
  53.0 4.6 %shard_map.194 = bf16[4,2,256,64]{3,2,1,0:T(8,128)(2,1)S(1)} custom-call(f32[1,1,1024]{2,1,0:T(1,128)S(1)} %mul.305.bias_ref, f32[1,1024]{1,0:T(1,128)S(1)} %convert_element_type.408.row_ref, f32[1024,1]{1,0:T(8,128)S(1)} %convert_element_type.513.column_ref, bf16[4,2,256,192]{3,2,1,0:T(8,128)(2,1)S(1)} %pad_maximum_fusion.7.in_ref), custom_call_target="tpu_custom_call" | custom-call | flops 402653184 | bytes 2097152 | tf_op jit(solution)/shard_map/pallas_call | solution.py:303
  59.3 15.2 %collective-permute-start.4 = (bf16[512,64]{1,0:T(8,128)(2,1)S(1)}, bf16[512,64]{1,0:T(8,128)(2,1)S(1)}, u32[]{:S(2)}, u32[]{:S(2)}) collective-permute-start(bf16[512,64]{1,0:T(8,128)(2,1)S(1)} %bitcast.299), channel_id=1, source_target_pairs={{0,12},{4,0},{8,4},{12,8},{1,13},{5,1},{9,5},{13,9},{2,14},{6,2},{... | collective-permute-start | bytes 196616 | tf_op jit(solution)/shard_map/ppermute | solution.py:22
  89.5 6.0 %collective-permute-done.9 = bf16[256,1024]{1,0:T(8,128)(2,1)} collective-permute-done((bf16[256,1024]{1,0:T(8,128)(2,1)S(1)}, bf16[256,1024]{1,0:T(8,128)(2,1)}, u32[]{:S(2)}, u32[]{:S(2)}) %collective-permute-start.9) | collective-permute-done | bytes 524320 | tf_op jit(solution)/shard_map/ppermute | solution.py:68
  96.8 8.7 %collective-permute-done.11 = bf16[512,1024]{1,0:T(8,128)(2,1)} collective-permute-done((bf16[512,1024]{1,0:T(8,128)(2,1)}, bf16[512,1024]{1,0:T(8,128)(2,1)}, u32[]{:S(2)}, u32[]{:S(2)}) %collective-permute-start.11) | collective-permute-done | bytes 1048608 | tf_op jit(solution)/shard_map/ppermute | solution.py:68
  107.2 20.3 %collective-permute-done.12 = bf16[512,1024]{1,0:T(8,128)(2,1)} collective-permute-done((bf16[512,1024]{1,0:T(8,128)(2,1)}, bf16[512,1024]{1,0:T(8,128)(2,1)}, u32[]{:S(2)}, u32[]{:S(2)}) %collective-permute-start.12) | collective-permute-done | bytes 1048608 | tf_op jit(solution)/shard_map/ppermute | solution.py:68
  129.6 5.7 %fusion.85 = (f32[2,256]{1,0:T(2,128)S(1)}, f32[2,256,1,1024]{3,2,1,0:T(1,128)S(1)}) fusion(f32[1024]{0:T(1024)S(1)} %bitcast.308, f32[2,256,1,1024]{3,1,0,2:T(8,128)S(1)} %bitcast.243, bf16[2,256,1,1024]{3,1,2,0:T(8,128)(2,1)S(1)} %copy-done), kind=kLoop, calls=%fused_computation.235 | loop fusion | flops 2096640 | bytes 5249024 | tf_op jit(solution)/shard_map/reduce_sum | solution.py:26
  136.6 7.6 %multiply_reduce_fusion.4 = f32[2,256]{1,0:T(2,128)S(1)} fusion(f32[2,256,1,1024]{3,2,1,0:T(1,128)S(1)} %get-tuple-element.57, f32[2,256]{1,0:T(2,128)S(1)} %get-tuple-element.118), kind=kLoop, calls=%fused_computation.47 | loop fusion | flops 1572352 | bytes 2101248 | tf_op jit(solution)/shard_map/reduce_sum | solution.py:28
  164.7 8.9 %collective-permute-done.17 = bf16[256,1024]{1,0:T(8,128)(2,1)} collective-permute-done((bf16[256,1024]{1,0:T(8,128)(2,1)}, bf16[256,1024]{1,0:T(8,128)(2,1)}, u32[]{:S(2)}, u32[]{:S(2)}) %collective-permute-start.17) | collective-permute-done | bytes 524320 | tf_op jit(solution)/shard_map/ppermute | solution.py:68
  175.1 7.1 %collective-permute-done.43 = bf16[512,1024]{1,0:T(8,128)(2,1)} collective-permute-done((bf16[512,1024]{1,0:T(8,128)(2,1)}, bf16[512,1024]{1,0:T(8,128)(2,1)}, u32[]{:S(2)}, u32[]{:S(2)}) %collective-permute-start.43) | collective-permute-done | bytes 1048608 | tf_op jit(solution)/shard_map/ppermute | solution.py:68
  184.8 18.9 %collective-permute-done.39 = bf16[512,1024]{1,0:T(8,128)(2,1)} collective-permute-done((bf16[512,1024]{1,0:T(8,128)(2,1)}, bf16[512,1024]{1,0:T(8,128)(2,1)}, u32[]{:S(2)}, u32[]{:S(2)}) %collective-permute-start.39) | collective-permute-done | bytes 1048608 | tf_op jit(solution)/shard_map/ppermute | solution.py:68
  208.9 8.8 %collective-permute-done.40 = bf16[128,1024]{1,0:T(8,128)(2,1)S(1)} collective-permute-done((bf16[128,1024]{1,0:T(8,128)(2,1)S(1)}, bf16[128,1024]{1,0:T(8,128)(2,1)S(1)}, u32[]{:S(2)}, u32[]{:S(2)}) %collective-permute-start.40) | collective-permute-done | bytes 262176 | tf_op jit(solution)/shard_map/ppermute | solution.py:22
  220.2 10.2 %multiply_reduce_fusion = (f32[1024]{0:T(1024)}, f32[2,256]{1,0:T(2,128)S(1)}) fusion(f32[2,256,1,1024]{3,1,0,2:T(8,128)S(1)} %bitcast.239, f32[2,256]{1,0:T(2,128)S(1)} %get-tuple-element.115, f32[2,256,1,1024]{3,2,1,0:T(1,128)S(1)} %copy-done.2, f32[2,256]{1,0:T(2,128)S(1)} %get-tuple-element.118, f32[1024]{0:T(1024)S(1)} %bitcast.301), kind=kLoop, calls=%fused_computation.39 | loop fusion | flops 3668480 | bytes 4208640 | tf_op jit(solution)/shard_map/transpose(jvp())/reduce_sum | solution.py:29
  230.8 10.2 %fusion.84 = (f32[2,256]{1,0:T(2,128)S(1)}, f32[2,256,1,1024]{3,2,1,0:T(1,128)}, bf16[2,256,1,1024]{3,2,1,0:T(2,128)(2,1)}) fusion(f32[2,256]{1,0:T(2,128)S(1)} %multiply_multiply_fusion.4, f32[2,256,1,1024]{3,2,1,0:T(1,128)S(1)} %copy-done.2, f32[2,256]{1,0:T(2,128)S(1)} %get-tuple-element.118, f32[2,256]{1,0:T(2,128)S(1)} %get-tuple-element.115, ...), kind=kLoop, calls=%fused_computation.234 | loop fusion | flops 5242368 | bytes 9453568 | tf_op jit(solution)/shard_map/transpose(jvp())/reduce_sum | solution.py:27
  262.9 7.4 %shard_map.195 = bf16[4,2,256,192]{3,2,1,0:T(8,128)(2,1)S(1)} custom-call(f32[1,1,1024]{2,1,0:T(1,128)S(1)} %mul.305.bias_ref, f32[1,1024]{1,0:T(1,128)S(1)} %convert_element_type.408.row_ref, f32[1024,1]{1,0:T(8,128)S(1)} %convert_element_type.513.column_ref, bf16[4,2,256,192]{3,2,1,0:T(8,128)(2,1)S(1)} %pad_maximum_fusion.7.in_ref, ...), custom_call_target="tpu_custom_call" | custom-call | flops 1073741824 | bytes 2097152 | tf_op jit(solution)/shard_map/pallas_call | solution.py:303
  278.3 7.5 %collective-permute-start.23 = (bf16[512,192]{0,1:T(8,128)(2,1)}, bf16[512,192]{0,1:T(8,128)(2,1)S(1)}, u32[]{:S(2)}, u32[]{:S(2)}) collective-permute-start(bf16[512,192]{0,1:T(8,128)(2,1)} %copy.90), channel_id=1, source_target_pairs={{0,8},{4,12},{8,0},{12,4},{1,9},{5,13},{9,1},{13,5},{2,10},{6,14},... | collective-permute-start | bytes 589832 | tf_op jit(solution)/shard_map/ppermute | solution.py:22
  288.2 6.9 %collective-permute-start.36 = (bf16[128,256]{1,0:T(8,128)(2,1)S(1)}, bf16[128,256]{1,0:T(8,128)(2,1)S(1)}, u32[]{:S(2)}, u32[]{:S(2)}) collective-permute-start(bf16[128,256]{1,0:T(8,128)(2,1)S(1)} %fusion.58), channel_id=1, source_target_pairs={{0,4},{4,8},{8,12},{12,0},{1,5},{5,9},{9,13},{13,1},{2,6},{6,10},{... | collective-permute-start | bytes 196616 | tf_op jit(solution)/shard_map/ppermute | solution.py:22
  300.7 7.9 %collective-permute-start.31 = (bf16[512,768]{1,0:T(8,128)(2,1)S(1)}, bf16[512,768]{1,0:T(8,128)(2,1)S(1)}, u32[]{:S(2)}, u32[]{:S(2)}) collective-permute-start(bf16[512,768]{1,0:T(8,128)(2,1)S(1)} %convolution_convert_fusion.6), channel_id=1, source_target_pairs={{0,16},{16,0},{1,17},{17,1},{2,18},{18,2},{3,19},{19,3},{4,20},{20... | collective-permute-start | bytes 2359304 | tf_op jit(solution)/shard_map/ppermute | solution.py:68
  335.7 10.3 %multiply_reduce_fusion.1 = (f32[1024]{0:T(1024)S(1)}, f32[2,256]{1,0:T(2,128)S(1)}) fusion(f32[2,256,1,1024]{3,1,0,2:T(8,128)S(1)} %bitcast.241, f32[2,256]{1,0:T(2,128)S(1)} %copy-done.33, f32[2,256]{1,0:T(2,128)S(1)} %get-tuple-element.110, bf16[2,256,1,1024]{3,1,2,0:T(8,128)(2,1)S(1)} %copy-done, f32[1024]{0:T(1024)S(1)} %bitcast.306), kind=kLoop, calls=%fused_computation.40 | loop fusion | flops 4192768 | bytes 3160064 | tf_op jit(solution)/shard_map/transpose(jvp())/reduce_sum | solution.py:29
  346.1 9.5 %fusion.83 = (f32[2,256]{1,0:T(2,128)S(1)}, f32[2,256,1,1024]{3,2,1,0:T(1,128)S(1)}) fusion(f32[2,256]{1,0:T(2,128)S(1)} %multiply_multiply_fusion.2, f32[2,256]{1,0:T(2,128)S(1)} %get-tuple-element.110, bf16[2,256,1,1024]{3,1,2,0:T(8,128)(2,1)S(1)} %copy-done, f32[2,256]{1,0:T(2,128)S(1)} %copy-done.33, f32[1024]{0:T(1024)S(1)} %bitcast.307, ...), kind=kLoop, calls=%fused_computation.233 | loop fusion | flops 4193792 | bytes 5255168 | tf_op jit(solution)/shard_map/transpose(jvp())/reduce_sum | solution.py:27
  355.7 7.9 %fusion.82 = (f32[1024]{0:T(1024)S(1)}, f32[1024]{0:T(1024)S(1)}, f32[2,256,1,1024]{3,2,1,0:T(1,128)}) fusion(f32[2,256,1,1024]{3,2,1,0:T(1,128)S(1)} %copy-done.7, f32[2,256]{1,0:T(2,128)S(1)} %copy-done.42, bf16[2,256,1,1024]{3,1,2,0:T(8,128)(2,1)S(1)} %copy-done.12, f32[2,256,1,1024]{3,2,1,0:T(1,128)S(1)} %get-tuple-element.53, ...), kind=kLoop, calls=%fused_computation.232 | loop fusion | flops 3667968 | bytes 7352320 | tf_op jit(solution)/shard_map/reduce_sum | solution.py:557
  368.3 6.5 %collective-permute-done.33 = bf16[128,768]{0,1:T(8,128)(2,1)S(1)} collective-permute-done((bf16[128,768]{0,1:T(8,128)(2,1)S(1)}, bf16[128,768]{0,1:T(8,128)(2,1)S(1)}, u32[]{:S(2)}, u32[]{:S(2)}) %collective-permute-start.33) | collective-permute-done | bytes 196640 | tf_op jit(solution)/shard_map/ppermute | solution.py:22
  377.3 5.1 %collective-permute-done.34 = bf16[128,768]{0,1:T(8,128)(2,1)S(1)} collective-permute-done((bf16[128,768]{0,1:T(8,128)(2,1)S(1)}, bf16[128,768]{0,1:T(8,128)(2,1)S(1)}, u32[]{:S(2)}, u32[]{:S(2)}) %collective-permute-start.34) | collective-permute-done | bytes 196640 | tf_op jit(solution)/shard_map/ppermute | solution.py:22
  (337 shorter events, 164.5 us)
Async XLA Ops:
  0.7 34.3 %collective-permute-start.7 = (bf16[512,256]{1,0:T(8,128)(2,1)}, bf16[512,256]{1,0:T(8,128)(2,1)}, u32[]{:S(2)}, u32[]{:S(2)}) collective-permute-start(bf16[512,256]{1,0:T(8,128)(2,1)} %param.17), channel_id=1, source_target_pairs={{0,16},{16,0},{1,17},{17,1},{2,18},{18,2},{3,19},{19,3},{4,20},{20... | collective-permute-start | bytes 786440 | tf_op jit(solution)/shard_map/ppermute | solution.py:68
  5.1 22.1 %collective-permute-start = (bf16[512,768]{0,1:T(8,128)(2,1)S(1)}, bf16[512,768]{0,1:T(8,128)(2,1)}, u32[]{:S(2)}, u32[]{:S(2)}) collective-permute-start(bf16[512,768]{0,1:T(8,128)(2,1)S(1)} %bitcast.266), channel_id=1, source_target_pairs={{0,16},{16,0},{1,17},{17,1},{2,18},{18,2},{3,19},{19,3},{4,20},{20... | collective-permute-start | bytes 2359304 | tf_op jit(solution)/shard_map/ppermute | solution.py:68
  34.0 17.0 %collective-permute-start.1 = (bf16[512,192]{0,1:T(8,128)(2,1)S(1)}, bf16[512,192]{0,1:T(8,128)(2,1)S(1)}, u32[]{:S(2)}, u32[]{:S(2)}) collective-permute-start(bf16[512,192]{0,1:T(8,128)(2,1)S(1)} %get-tuple-element.89), channel_id=1, source_target_pairs={{0,4},{4,8},{8,12},{12,0},{1,5},{5,9},{9,13},{13,1},{2,6},{6,10},{... | collective-permute-start | bytes 589832 | tf_op jit(solution)/shard_map/ppermute | solution.py:22
  57.6 19.4 %collective-permute-start.5 = (bf16[512,64]{1,0:T(8,128)(2,1)S(1)}, bf16[512,64]{1,0:T(8,128)(2,1)S(1)}, u32[]{:S(2)}, u32[]{:S(2)}) collective-permute-start(bf16[512,64]{1,0:T(8,128)(2,1)S(1)} %bitcast.298), channel_id=1, source_target_pairs={{0,8},{4,12},{8,0},{12,4},{1,9},{5,13},{9,1},{13,5},{2,10},{6,14},... | collective-permute-start | bytes 196616 | tf_op jit(solution)/shard_map/ppermute | solution.py:22
  59.3 17.8 %collective-permute-start.6 = (bf16[512,64]{1,0:T(8,128)(2,1)S(1)}, bf16[512,64]{1,0:T(8,128)(2,1)S(1)}, u32[]{:S(2)}, u32[]{:S(2)}) collective-permute-start(bf16[512,64]{1,0:T(8,128)(2,1)S(1)} %bitcast.297), channel_id=1, source_target_pairs={{0,4},{4,8},{8,12},{12,0},{1,5},{5,9},{9,13},{13,1},{2,6},{6,10},{... | collective-permute-start | bytes 196616 | tf_op jit(solution)/shard_map/ppermute | solution.py:22
  59.3 17.7 %collective-permute-start.4 = (bf16[512,64]{1,0:T(8,128)(2,1)S(1)}, bf16[512,64]{1,0:T(8,128)(2,1)S(1)}, u32[]{:S(2)}, u32[]{:S(2)}) collective-permute-start(bf16[512,64]{1,0:T(8,128)(2,1)S(1)} %bitcast.299), channel_id=1, source_target_pairs={{0,12},{4,0},{8,4},{12,8},{1,13},{5,1},{9,5},{13,9},{2,14},{6,2},{... | collective-permute-start | bytes 196616 | tf_op jit(solution)/shard_map/ppermute | solution.py:22
  79.2 26.3 %collective-permute-start.11 = (bf16[512,1024]{1,0:T(8,128)(2,1)}, bf16[512,1024]{1,0:T(8,128)(2,1)}, u32[]{:S(2)}, u32[]{:S(2)}) collective-permute-start(bf16[512,1024]{1,0:T(8,128)(2,1)} %param.19), channel_id=1, source_target_pairs={{0,16},{16,0},{1,17},{17,1},{2,18},{18,2},{3,19},{19,3},{4,20},{20... | collective-permute-start | bytes 3145736 | tf_op jit(solution)/shard_map/ppermute | solution.py:68
  80.8 46.8 %collective-permute-start.12 = (bf16[512,1024]{1,0:T(8,128)(2,1)}, bf16[512,1024]{1,0:T(8,128)(2,1)}, u32[]{:S(2)}, u32[]{:S(2)}) collective-permute-start(bf16[512,1024]{1,0:T(8,128)(2,1)} %param.21), channel_id=1, source_target_pairs={{0,16},{16,0},{1,17},{17,1},{2,18},{18,2},{3,19},{19,3},{4,20},{20... | collective-permute-start | bytes 3145736 | tf_op jit(solution)/shard_map/ppermute | solution.py:68
  96.7 32.5 %collective-permute-start.10 = (bf16[256,1024]{1,0:T(8,128)(2,1)S(1)}, bf16[256,1024]{1,0:T(8,128)(2,1)S(1)}, u32[]{:S(2)}, u32[]{:S(2)}) collective-permute-start(bf16[256,1024]{1,0:T(8,128)(2,1)S(1)} %add_convert_fusion.8), channel_id=1, source_target_pairs={{0,1},{1,0},{2,3},{3,2},{4,5},{5,4},{6,7},{7,6},{8,9},{9,8},{10,11... | collective-permute-start | bytes 1572872 | tf_op jit(solution)/shard_map/ppermute | solution.py:68
  155.9 26.3 %collective-permute-start.43 = (bf16[512,1024]{1,0:T(8,128)(2,1)}, bf16[512,1024]{1,0:T(8,128)(2,1)}, u32[]{:S(2)}, u32[]{:S(2)}) collective-permute-start(bf16[512,1024]{1,0:T(8,128)(2,1)} %convolution_convert_fusion.4), channel_id=1, source_target_pairs={{0,16},{16,0},{1,17},{17,1},{2,18},{18,2},{3,19},{19,3},{4,20},{20... | collective-permute-start | bytes 3145736 | tf_op jit(solution)/shard_map/ppermute | solution.py:68
  161.8 42.0 %collective-permute-start.39 = (bf16[512,1024]{1,0:T(8,128)(2,1)}, bf16[512,1024]{1,0:T(8,128)(2,1)}, u32[]{:S(2)}, u32[]{:S(2)}) collective-permute-start(bf16[512,1024]{1,0:T(8,128)(2,1)} %convolution_convert_fusion.5), channel_id=1, source_target_pairs={{0,16},{16,0},{1,17},{17,1},{2,18},{18,2},{3,19},{19,3},{4,20},{20... | collective-permute-start | bytes 3145736 | tf_op jit(solution)/shard_map/ppermute | solution.py:68
  164.1 42.7 %collective-permute-start.14 = (bf16[256,1024]{1,0:T(8,128)(2,1)S(1)}, bf16[256,1024]{1,0:T(8,128)(2,1)S(1)}, u32[]{:S(2)}, u32[]{:S(2)}) collective-permute-start(bf16[256,1024]{1,0:T(8,128)(2,1)S(1)} %add_convert_fusion.7), channel_id=1, source_target_pairs={{0,2},{1,3},{2,0},{3,1},{4,6},{5,7},{6,4},{7,5},{8,10},{9,11},{10,... | collective-permute-start | bytes 1572872 | tf_op jit(solution)/shard_map/ppermute | solution.py:68
  175.0 43.5 %collective-permute-start.18 = (bf16[256,1024]{1,0:T(8,128)(2,1)S(1)}, bf16[256,1024]{1,0:T(8,128)(2,1)S(1)}, u32[]{:S(2)}, u32[]{:S(2)}) collective-permute-start(bf16[256,1024]{1,0:T(8,128)(2,1)S(1)} %add_convert_fusion.4), channel_id=1, source_target_pairs={{0,1},{1,0},{2,3},{3,2},{4,5},{5,4},{6,7},{7,6},{8,9},{9,8},{10,11... | collective-permute-start | bytes 1572872 | tf_op jit(solution)/shard_map/ppermute | solution.py:68
  184.3 22.8 %collective-permute-start.44 = (bf16[128,1024]{1,0:T(8,128)(2,1)S(1)}, bf16[128,1024]{1,0:T(8,128)(2,1)S(1)}, u32[]{:S(2)}, u32[]{:S(2)}) collective-permute-start(bf16[128,1024]{1,0:T(8,128)(2,1)S(1)} %fusion.54), channel_id=1, source_target_pairs={{0,4},{4,8},{8,12},{12,0},{1,5},{5,9},{9,13},{13,1},{2,6},{6,10},{... | collective-permute-start | bytes 786440 | tf_op jit(solution)/shard_map/ppermute | solution.py:22
  207.0 23.4 %collective-permute-start.15 = (bf16[256,1024]{1,0:T(8,128)(2,1)S(1)}, bf16[256,1024]{1,0:T(8,128)(2,1)S(1)}, u32[]{:S(2)}, u32[]{:S(2)}) collective-permute-start(bf16[256,1024]{1,0:T(8,128)(2,1)S(1)} %add_convert_fusion.6), channel_id=1, source_target_pairs={{0,1},{1,0},{2,3},{3,2},{4,5},{5,4},{6,7},{7,6},{8,9},{9,8},{10,11... | collective-permute-start | bytes 1572872 | tf_op jit(solution)/shard_map/ppermute | solution.py:68
  207.8 48.6 %collective-permute-start.45 = (bf16[128,1024]{1,0:T(8,128)(2,1)}, bf16[128,1024]{1,0:T(8,128)(2,1)}, u32[]{:S(2)}, u32[]{:S(2)}) collective-permute-start(bf16[128,1024]{1,0:T(8,128)(2,1)} %fusion.27), channel_id=1, source_target_pairs={{0,4},{4,8},{8,12},{12,0},{1,5},{5,9},{9,13},{13,1},{2,6},{6,10},{... | collective-permute-start | bytes 786440 | tf_op jit(solution)/shard_map/ppermute | solution.py:22
  218.5 41.4 %collective-permute-start.41 = (bf16[128,1024]{1,0:T(8,128)(2,1)}, bf16[128,1024]{1,0:T(8,128)(2,1)}, u32[]{:S(2)}, u32[]{:S(2)}) collective-permute-start(bf16[128,1024]{1,0:T(8,128)(2,1)} %fusion.29), channel_id=1, source_target_pairs={{0,4},{4,8},{8,12},{12,0},{1,5},{5,9},{9,13},{13,1},{2,6},{6,10},{... | collective-permute-start | bytes 786440 | tf_op jit(solution)/shard_map/ppermute | solution.py:22
  256.5 29.3 %collective-permute-start.35 = (bf16[512,256]{1,0:T(8,128)(2,1)}, bf16[512,256]{1,0:T(8,128)(2,1)}, u32[]{:S(2)}, u32[]{:S(2)}) collective-permute-start(bf16[512,256]{1,0:T(8,128)(2,1)} %convolution_convert_fusion.7), channel_id=1, source_target_pairs={{0,16},{16,0},{1,17},{17,1},{2,18},{18,2},{3,19},{19,3},{4,20},{20... | collective-permute-start | bytes 786440 | tf_op jit(solution)/shard_map/ppermute | solution.py:68
  259.9 48.8 %collective-permute-start.46 = (bf16[128,1024]{1,0:T(8,128)(2,1)}, bf16[128,1024]{1,0:T(8,128)(2,1)}, u32[]{:S(2)}, u32[]{:S(2)}) collective-permute-start(bf16[128,1024]{1,0:T(8,128)(2,1)} %fusion.26), channel_id=1, source_target_pairs={{0,4},{4,8},{8,12},{12,0},{1,5},{5,9},{9,13},{13,1},{2,6},{6,10},{... | collective-permute-start | bytes 786440 | tf_op jit(solution)/shard_map/ppermute | solution.py:22
  262.6 54.2 %collective-permute-start.42 = (bf16[128,1024]{1,0:T(8,128)(2,1)}, bf16[128,1024]{1,0:T(8,128)(2,1)}, u32[]{:S(2)}, u32[]{:S(2)}) collective-permute-start(bf16[128,1024]{1,0:T(8,128)(2,1)} %fusion.28), channel_id=1, source_target_pairs={{0,4},{4,8},{8,12},{12,0},{1,5},{5,9},{9,13},{13,1},{2,6},{6,10},{... | collective-permute-start | bytes 786440 | tf_op jit(solution)/shard_map/ppermute | solution.py:22
  278.3 18.4 %collective-permute-start.23 = (bf16[512,192]{0,1:T(8,128)(2,1)}, bf16[512,192]{0,1:T(8,128)(2,1)S(1)}, u32[]{:S(2)}, u32[]{:S(2)}) collective-permute-start(bf16[512,192]{0,1:T(8,128)(2,1)} %copy.90), channel_id=1, source_target_pairs={{0,8},{4,12},{8,0},{12,4},{1,9},{5,13},{9,1},{13,5},{2,10},{6,14},... | collective-permute-start | bytes 589832 | tf_op jit(solution)/shard_map/ppermute | solution.py:22
  288.2 22.4 %collective-permute-start.36 = (bf16[128,256]{1,0:T(8,128)(2,1)S(1)}, bf16[128,256]{1,0:T(8,128)(2,1)S(1)}, u32[]{:S(2)}, u32[]{:S(2)}) collective-permute-start(bf16[128,256]{1,0:T(8,128)(2,1)S(1)} %fusion.58), channel_id=1, source_target_pairs={{0,4},{4,8},{8,12},{12,0},{1,5},{5,9},{9,13},{13,1},{2,6},{6,10},{... | collective-permute-start | bytes 196616 | tf_op jit(solution)/shard_map/ppermute | solution.py:22
  300.7 26.0 %collective-permute-start.31 = (bf16[512,768]{1,0:T(8,128)(2,1)S(1)}, bf16[512,768]{1,0:T(8,128)(2,1)S(1)}, u32[]{:S(2)}, u32[]{:S(2)}) collective-permute-start(bf16[512,768]{1,0:T(8,128)(2,1)S(1)} %convolution_convert_fusion.6), channel_id=1, source_target_pairs={{0,16},{16,0},{1,17},{17,1},{2,18},{18,2},{3,19},{19,3},{4,20},{20... | collective-permute-start | bytes 2359304 | tf_op jit(solution)/shard_map/ppermute | solution.py:68
  331.4 34.1 %collective-permute-start.32 = (bf16[128,768]{0,1:T(8,128)(2,1)S(1)}, bf16[128,768]{0,1:T(8,128)(2,1)}, u32[]{:S(2)}, u32[]{:S(2)}) collective-permute-start(bf16[128,768]{0,1:T(8,128)(2,1)S(1)} %bitcast.289), channel_id=1, source_target_pairs={{0,4},{4,8},{8,12},{12,0},{1,5},{5,9},{9,13},{13,1},{2,6},{6,10},{... | collective-permute-start | bytes 589832 | tf_op jit(solution)/shard_map/ppermute | solution.py:22
  (69 other events, 619.0 us)

commit v2 on v1

--- a/solution.py
+++ b/solution.py
@@ -20,13 +20,6 @@
     count = lax.axis_size(axis)
     pairs = [(source, (source + steps) % count) for source in range(count)]
     return lax.ppermute(value, axis, pairs)
-
-
-def normalize(values, scale_by, offset):
-    average = jnp.mean(values, axis=-1, keepdims=True)
-    centred = values - average
-    spread = jnp.mean(centred * centred, axis=-1, keepdims=True)
-    return centred * lax.rsqrt(spread + EPSILON) * scale_by + offset
 
 
 def gelu_tanh(values):
@@ -80,7 +73,7 @@
     count = lax.axis_size("tp")
     partial = partial.astype(jnp.bfloat16)
     if not power_of_two(count):
-        return lax.psum(partial, "tp").astype(jnp.float32)
+        return lax.psum(partial, "tp")
     rows = partial.shape[0] // 2
     even = lax.axis_index("tp") % 2 == 0
     low, high = partial[:rows], partial[rows:]
@@ -94,11 +87,21 @@
     other = exchanged(total, "tp", 1)
     return jnp.concatenate(
         [jnp.where(even, total, other), jnp.where(even, other, total)], 0
-    ).astype(jnp.float32)
+    )
 
 
 def sum_small(values, axes):
-    flat = jnp.concatenate([value.reshape(-1) for value in values]).reshape(-1, 128)
+    flat = sum_over(
+        jnp.concatenate([value.reshape(-1) for value in values]).reshape(-1, 128), axes
+    ).reshape(-1)
+    results, start = [], 0
+    for value in values:
+        results.append(flat[start : start + value.size].reshape(value.shape))
+        start += value.size
+    return results
+
+
+def sum_over(flat, axes):
     for axis in axes:
         count = lax.axis_size(axis)
         if not power_of_two(count):
@@ -108,12 +111,7 @@
         while mask < count:
             flat = flat + exchanged(flat, axis, mask)
             mask *= 2
-    flat = flat.reshape(-1)
-    results, start = [], 0
-    for value in values:
-        results.append(flat[start : start + value.size].reshape(value.shape))
-        start += value.size
-    return results
+    return flat
 
 
 def whole_rows(block):
@@ -128,7 +126,26 @@
     return jnp.einsum("td,tf->df", left, right, preferred_element_type=jnp.float32)
 
 
-def owned_grad(left, right):
+def after(value, gate):
+    if gate is None:
+        return value
+    first = gate[(slice(0, 1),) * gate.ndim].reshape((1,) * value.ndim)
+    return value + (0.0 * first.astype(jnp.float32)).astype(value.dtype)
+
+
+def ring_sum(chunk, gates=()):
+    count = lax.axis_size("ctx")
+    me = lax.axis_index("ctx")
+    moving = chunk(lax.rem(me + count - 1, count))
+    for step in range(count - 1):
+        arrived = shifted(moving.astype(jnp.bfloat16), "ctx", 1)
+        term = chunk(lax.rem(me + 2 * count - 2 - step, count))
+        gate = gates[step] if step < len(gates) else None
+        moving = after(arrived.astype(jnp.float32) + term, gate)
+    return moving
+
+
+def owned_grad(left, right, gate=None):
     count = lax.axis_size("ctx")
     if lax.axis_size("shard") != 2:
         return lax.psum_scatter(
@@ -138,24 +155,133 @@
     shard = lax.axis_index("shard")
     theirs = lax.dynamic_slice_in_dim(left, (1 - shard) * half_width, half_width, 1)
     mine = lax.dynamic_slice_in_dim(left, shard * half_width, half_width, 1)
-    half = outer(mine, right) + exchanged(
-        outer(theirs, right).astype(jnp.bfloat16), "shard", 1
-    ).astype(jnp.float32)
+    arrived = exchanged(outer(theirs, right).astype(jnp.bfloat16), "shard", 1)
+    half = after(outer(mine, right) + arrived.astype(jnp.float32), gate)
     if count > 8:
         return lax.psum_scatter(half, "ctx", scatter_dimension=0, tiled=True)
     chunks = half.reshape(count, half_width // count, half.shape[1])
-    me = lax.axis_index("ctx")
-
-    def chunk(back):
-        return lax.dynamic_index_in_dim(
-            chunks, lax.rem(me + 2 * count - back, count), 0, keepdims=False
-        )
-
-    moving = chunk(1)
-    for step in range(count - 1):
-        arrived = shifted(moving.astype(jnp.bfloat16), "ctx", 1)
-        moving = arrived.astype(jnp.float32) + chunk(step + 2)
-    return moving
+
+    def chunk(member):
+        return lax.dynamic_index_in_dim(chunks, member, 0, keepdims=False)
+
+    return ring_sum(chunk)
+
+
+def owned_grad_ring_first(left, right, gates):
+    count = lax.axis_size("ctx")
+    if lax.axis_size("shard") != 2 or count > 8:
+        return owned_grad(left, right)
+    tokens, width = left.shape
+    rows = width // (2 * count)
+    pieces = left.reshape(tokens, 2, count, rows).transpose(2, 0, 1, 3)
+    pieces = pieces.reshape(count, tokens, 2 * rows)
+
+    def chunk(member):
+        return outer(lax.dynamic_index_in_dim(pieces, member, 0, keepdims=False), right)
+
+    both = ring_sum(chunk, gates)
+    first = lax.axis_index("shard") == 0
+    low, high = both[:rows], both[rows:]
+    arrived = exchanged(jnp.where(first, high, low).astype(jnp.bfloat16), "shard", 1)
+    return jnp.where(first, low, high) + arrived.astype(jnp.float32)
+
+
+NORM_ROWS = 128
+
+
+def unit_rows(values):
+    average = jnp.mean(values, axis=1, keepdims=True)
+    centred = values - average
+    inverse = lax.rsqrt(jnp.mean(centred * centred, axis=1, keepdims=True) + EPSILON)
+    return centred * inverse, inverse
+
+
+def rows_back(unit, inverse, grad, gain):
+    scaled = grad * gain
+    return inverse * (
+        scaled
+        - jnp.mean(scaled, axis=1, keepdims=True)
+        - unit * jnp.mean(scaled * unit, axis=1, keepdims=True)
+    )
+
+
+def row_sum(values):
+    return jnp.sum(values, axis=0, keepdims=True)
+
+
+def add_rows(total_ref, rows):
+    @pl.when(pl.program_id(0) == 0)
+    def _():
+        total_ref[...] = jnp.zeros_like(total_ref)
+
+    for place, row in enumerate(rows):
+        total_ref[place : place + 1, :] += row
+
+
+def norm_one_kernel(gain_ref, shift_ref, x_ref, out_ref):
+    unit, _ = unit_rows(x_ref[...].astype(jnp.float32))
+    out_ref[...] = (unit * gain_ref[0:1, :] + shift_ref[0:1, :]).astype(out_ref.dtype)
+
+
+def norm_two_kernel(gain_ref, shift_ref, bias_ref, x_ref, branch_ref, gate_ref, resid_ref, out_ref):
+    del gate_ref
+    resid = x_ref[...].astype(jnp.float32) + branch_ref[...].astype(jnp.float32) + bias_ref[0:1, :]
+    resid_ref[...] = resid
+    unit, _ = unit_rows(resid)
+    out_ref[...] = (unit * gain_ref[1:2, :] + shift_ref[1:2, :]).astype(out_ref.dtype)
+
+
+def norm_two_back_kernel(gain_ref, resid_ref, grad_ref, dy_ref, out_ref, out_bf_ref, total_ref):
+    unit, inverse = unit_rows(resid_ref[...])
+    grad = grad_ref[...].astype(jnp.float32)
+    dy = dy_ref[...].astype(jnp.float32)
+    result = dy + rows_back(unit, inverse, grad, gain_ref[1:2, :])
+    out_ref[...] = result
+    out_bf_ref[...] = result.astype(jnp.bfloat16)
+    add_rows(total_ref, (row_sum(grad * unit), row_sum(grad), row_sum(result), row_sum(dy)))
+
+
+def norm_one_sums_kernel(weight_ref, grad_ref, x_ref, out_ref, total_ref):
+    unit, _ = unit_rows(x_ref[...].astype(jnp.float32))
+    grad = dot_rows(grad_ref[...], weight_ref[...])
+    out_ref[...] = grad.astype(jnp.bfloat16)
+    add_rows(total_ref, (row_sum(grad * unit), row_sum(grad)))
+
+
+def norm_one_back_kernel(gain_ref, x_ref, grad_ref, resid_grad_ref, out_ref):
+    unit, inverse = unit_rows(x_ref[...].astype(jnp.float32))
+    grad = grad_ref[...].astype(jnp.float32)
+    out_ref[...] = resid_grad_ref[...] + rows_back(unit, inverse, grad, gain_ref[0:1, :])
+
+
+def row_call(kernel, whole, by_rows, gates, outs, sums, flops):
+    tokens, width = by_rows[-1].shape
+    block = NORM_ROWS if tokens % NORM_ROWS == 0 else tokens
+
+    def rows_spec(columns):
+        return pl.BlockSpec((block, columns), lambda step: (step, 0))
+
+    def whole_spec(shape):
+        return pl.BlockSpec(shape, lambda step: (0,) * len(shape))
+
+    out_shape = [jax.ShapeDtypeStruct((tokens, width), kind) for kind in outs]
+    out_specs = [rows_spec(width) for kind in outs]
+    if sums:
+        out_shape.append(jax.ShapeDtypeStruct((8, width), jnp.float32))
+        out_specs.append(whole_spec((8, width)))
+    return pl.pallas_call(
+        kernel,
+        grid=(tokens // block,),
+        out_shape=out_shape,
+        in_specs=[whole_spec(array.shape) for array in whole]
+        + [rows_spec(array.shape[1]) for array in by_rows]
+        + [pl.BlockSpec(memory_space=pl.ANY) for gate in gates],
+        out_specs=out_specs,
+        compiler_params=pltpu.CompilerParams(vmem_limit_bytes=24 * 2**20),
+        cost_estimate=pl.CostEstimate(
+            flops=flops, bytes_accessed=8 * tokens * width, transcendentals=0
+        ),
+    )(*whole, *by_rows, *gates)
 
 
 def spread_heads(groups):
@@ -214,7 +340,10 @@
     return weights, 1.0 / jnp.sum(weights, axis=1, keepdims=True)
 
 
-def attend_kernel(blocks, heads, scale_by, bias_ref, row_ref, column_ref, in_ref, out_ref):
+def attend_kernel(
+    blocks, heads, scale_by, bias_ref, row_ref, column_ref, in_ref, gate_ref, out_ref
+):
+    del gate_ref
     slots, rows = in_ref.shape[0], in_ref.shape[2] // blocks
     size = slots * rows
     for head in range(heads):
@@ -291,7 +420,7 @@
             store(block, columns[2], value_grads[block])
 
 
-def head_call(kernel, blocks, heads, tables, arrays, width, flops):
+def head_call(kernel, blocks, heads, tables, arrays, gates, width, flops):
     slots, seqs, rows = arrays[0].shape[:3]
 
     def table_spec(table):
@@ -305,16 +434,17 @@
         grid=(seqs,),
         out_shape=jax.ShapeDtypeStruct((slots, seqs, rows, width), jnp.bfloat16),
         in_specs=[table_spec(table) for table in tables]
-        + [slot_spec(array.shape[3]) for array in arrays],
+        + [slot_spec(array.shape[3]) for array in arrays]
+        + [pl.BlockSpec(memory_space=pl.ANY) for gate in gates],
         out_specs=slot_spec(width),
         compiler_params=pltpu.CompilerParams(vmem_limit_bytes=40 * 2**20),
         cost_estimate=pl.CostEstimate(
             flops=flops, bytes_accessed=2 * slots * seqs * rows * 512, transcendentals=0
         ),
-    )(*tables, *arrays)
-
-
-def attend_spread(queries, keys, values, slopes, seqs, rows):
+    )(*tables, *arrays, *gates)
+
+
+def attend_spread(queries, keys, values, slopes, seqs, rows, gate):
     count = lax.axis_size("ctx")
     me = lax.axis_index("ctx")
     heads = slopes.shape[0] // count
@@ -338,7 +468,7 @@
     )
     pairs = heads * seqs * (rows * count) ** 2 * HD
     attended = head_call(
-        attend_kernel, blocks, heads, tables, (spread,), width, 3 * pairs
+        attend_kernel, blocks, heads, tables, (spread,), (gate,), width, 3 * pairs
     )
 
     def homeward(slots, kinds):
@@ -350,14 +480,21 @@
         grouped_grads = grads.reshape(tokens, count, width).transpose(1, 0, 2)
         spread_grads = spread_heads(grouped_grads).reshape(count, seqs, rows, width)
         slots = head_call(
-            attend_back_kernel, blocks, heads, tables, (spread, spread_grads), 3 * width, 8 * pairs
+            attend_back_kernel,
+            blocks,
+            heads,
+            tables,
+            (spread, spread_grads),
+            (),
+            3 * width,
+            8 * pairs,
         )
-        return homeward(slots, 3)
+        return homeward(slots, 3), slots
 
     return homeward(attended, 1)[:, 0], back
 
 
-def attend_ring(query_bf, key_bf, value_bf, slopes, seq_dev, group_len):
+def attend_ring(query_bf, key_bf, value_bf, slopes, seq_dev, group_len, gate):
     tok_rows = seq_dev * group_len
     heads_loc = slopes.shape[0]
     local_width = query_bf.shape[1]
@@ -445,7 +582,7 @@
         query_grad, unused, key_grads = lax.fori_loop(
             0, cycle_size // 2, cycle_turn, (head_zeros, kv_pair, pair_zeros)
         )
-        return jnp.stack(
+        qkv_grad_bf = jnp.stack(
             [
                 query_grad.reshape(tok_rows, local_width),
                 key_grads[:, :, 0].reshape(tok_rows, local_width),
@@ -453,6 +590,7 @@
             ],
             1,
         ).astype(jnp.bfloat16)
+        return qkv_grad_bf, qkv_grad_bf
 
     return attended_bf, back
 
@@ -482,61 +620,96 @@
         )
         / H
     )
-    resident = tokens.reshape(tok_rows, model_width).astype(jnp.float32)
+    x_rows = tokens.reshape(tok_rows, model_width)
+    dy_rows = cotangent.reshape(tok_rows, model_width)
     gains = norm_gain.astype(jnp.float32)
     shifts = norm_bias.astype(jnp.float32)
     out_shift = out_bias.astype(jnp.float32)
     qv_shift = qv_bias.astype(jnp.float32)
     hidden_shift = hidden_bias.astype(jnp.float32)
-    gathered = (
-        whole_rows(w_qkv.reshape(w_qkv.shape[0], 3 * local_width)),
-        whole_rows(w_out),
-        whole_rows(w_up),
-        whole_rows(w_down),
-    )
-    full_qkv, full_out, full_up, full_down = gathered
-    normed_one = normalize(resident, gains[0], shifts[0]).astype(jnp.bfloat16)
+    full_qkv = whole_rows(w_qkv.reshape(w_qkv.shape[0], 3 * local_width))
+    full_out = whole_rows(w_out)
+    full_up = whole_rows(w_up)
+    full_down = whole_rows(w_down)
+    row_flops = 16 * tok_rows * model_width
+    (normed_one,) = row_call(
+        norm_one_kernel, (gains, shifts), (x_rows,), (), (jnp.bfloat16,), False, row_flops
+    )
     projected = jnp.dot(normed_one, full_qkv, preferred_element_type=jnp.float32)
     projected = projected.reshape(tok_rows, 3, local_width)
     query_bf = (projected[:, 0] + qv_shift[0]).astype(jnp.bfloat16)
     key_bf = projected[:, 1].astype(jnp.bfloat16)
     value_bf = (projected[:, 2] + qv_shift[1]).astype(jnp.bfloat16)
     attend = attend_spread if heads_loc % cycle_size == 0 else attend_ring
-    attended_bf, attend_back = attend(query_bf, key_bf, value_bf, slopes, seq_dev, group_len)
+    attended_bf, attend_back = attend(
+        query_bf, key_bf, value_bf, slopes, seq_dev, group_len, full_up
+    )
     branch = sum_over_tp(
         jnp.einsum("tf,df->td", attended_bf, full_out, preferred_element_type=jnp.float32)
     )
-    resid = resident + branch + out_shift[0]
-    normed_two = normalize(resid, gains[1], shifts[1]).astype(jnp.bfloat16)
+    resid, normed_two = row_call(
+        norm_two_kernel,
+        (gains, shifts, out_shift),
+        (x_rows, branch),
+        (full_down,),
+        (jnp.float32, jnp.bfloat16),
+        False,
+        row_flops,
+    )
     pre_act = jnp.dot(normed_two, full_up, preferred_element_type=jnp.float32) + hidden_shift
     act_bf = gelu_tanh(pre_act).astype(jnp.bfloat16)
-    feed = sum_over_tp(
-        jnp.einsum("tf,df->td", act_bf, full_down, preferred_element_type=jnp.float32)
-    )
-    output = (resid + feed + out_shift[1]).astype(jnp.bfloat16).reshape(tokens.shape)
-    back_qkv, back_out, back_up, back_down = gathered
-    out_grad = cotangent.reshape(tok_rows, model_width).astype(jnp.float32)
-    out_grad_bf = out_grad.astype(jnp.bfloat16)
-    grad_down = owned_grad(out_grad_bf, act_bf)
-    act_grad = jnp.dot(out_grad_bf, back_down, preferred_element_type=jnp.float32)
+    act_grad = jnp.dot(dy_rows, full_down, preferred_element_type=jnp.float32)
     pre_grad = jax.vjp(gelu_tanh, pre_act)[1](act_grad)[0]
     pre_grad_bf = pre_grad.astype(jnp.bfloat16)
-    grad_up = owned_grad(normed_two, pre_grad_bf)
     hidden_grad = jnp.sum(pre_grad_bf.astype(jnp.float32), axis=0)
     norm_two_grad = sum_over_tp(
-        jnp.einsum("tf,df->td", pre_grad_bf, back_up, preferred_element_type=jnp.float32)
-    )
-    resid_part, gain_two, shift_two = jax.vjp(normalize, resid, gains[1], shifts[1])[1](
-        norm_two_grad
-    )
-    resid_grad = out_grad + resid_part
-    resid_bf = resid_grad.astype(jnp.bfloat16)
-    grad_out = owned_grad(resid_bf, attended_bf)
-    attend_grad_bf = jnp.dot(resid_bf, back_out, preferred_element_type=jnp.float32).astype(
+        jnp.einsum("tf,df->td", pre_grad_bf, full_up, preferred_element_type=jnp.float32)
+    )
+    resid_grad, resid_bf, sums_two = row_call(
+        norm_two_back_kernel,
+        (gains,),
+        (resid, norm_two_grad, dy_rows),
+        (),
+        (jnp.float32, jnp.bfloat16),
+        True,
+        2 * row_flops,
+    )
+    feed = sum_over_tp(
+        after(
+            jnp.einsum("tf,df->td", act_bf, full_down, preferred_element_type=jnp.float32),
+            resid_bf,
+        )
+    )
+    output = (resid + feed.astype(jnp.float32) + out_shift[1]).astype(jnp.bfloat16)
+    output = output.reshape(tokens.shape)
+    attend_grad_bf = jnp.dot(resid_bf, full_out, preferred_element_type=jnp.float32).astype(
         jnp.bfloat16
     )
-    qkv_grad_bf = attend_back(attend_grad_bf)
+    qkv_grad_bf, attend_done = attend_back(attend_grad_bf)
     qkv_grad_flat = qkv_grad_bf.reshape(tok_rows, 3 * local_width)
+    norm_one_part, sums_one = row_call(
+        norm_one_sums_kernel,
+        (full_qkv,),
+        (qkv_grad_flat, x_rows),
+        (),
+        (jnp.bfloat16,),
+        True,
+        row_flops + 6 * tok_rows * model_width * local_width,
+    )
+    norm_one_grad = sum_over_tp(norm_one_part)
+    (input_grad,) = row_call(
+        norm_one_back_kernel,
+        (gains,),
+        (x_rows, norm_one_grad, resid_grad),
+        (),
+        (jnp.float32,),
+        False,
+        2 * row_flops,
+    )
+    input_grad = input_grad.reshape(tokens.shape)
+    grad_down = owned_grad_ring_first(dy_rows, act_bf, (norm_two_grad, attend_done))
+    grad_up = owned_grad(normed_two, pre_grad_bf, attend_done)
+    grad_out = owned_grad(resid_bf, attended_bf, qkv_grad_flat)
     grad_qkv = owned_grad(normed_one, qkv_grad_flat)
     grad_qkv = grad_qkv.reshape(grad_qkv.shape[0], 3, local_width)
     qv_grad = jnp.stack(
@@ -545,19 +718,13 @@
             jnp.sum(qkv_grad_bf[:, 2].astype(jnp.float32), axis=0),
         ]
     )
-    norm_one_grad = sum_over_tp(
-        jnp.einsum("tf,df->td", qkv_grad_flat, back_qkv, preferred_element_type=jnp.float32)
-    )
-    input_part, gain_one, shift_one = jax.vjp(normalize, resident, gains[0], shifts[0])[1](
-        norm_one_grad
-    )
-    input_grad = (resid_grad + input_part).reshape(tokens.shape)
-    gain_grads = jnp.stack([gain_one, gain_two])
-    shift_grads = jnp.stack([shift_one, shift_two])
-    out_bias_grad = jnp.stack([jnp.sum(resid_grad, axis=0), jnp.sum(out_grad, axis=0)])
-    gain_grads, shift_grads, qv_grad, out_bias_grad, hidden_grad = sum_small(
-        (gain_grads, shift_grads, qv_grad, out_bias_grad, hidden_grad), ("shard", "ctx")
-    )
+    sums_one, sums_two, qv_grad, hidden_grad = sum_small(
+        (sums_one[:2], sums_two[:4], qv_grad, hidden_grad), ("shard", "ctx")
+    )
+    sums_one = sum_over(sums_one, ("tp",))
+    gain_grads = jnp.stack([sums_one[0], sums_two[0]])
+    shift_grads = jnp.stack([sums_one[1], sums_two[1]])
+    out_bias_grad = sums_two[2:4]
     return (
         output,
         input_grad,

time: 391 us -> 330 us (0.84)
  other arithmetic: 114 us -> 43 us
  starting transfers between devices: 77.5 us -> 46.2 us
  local copies, waits for them, and re-layouts: 33.4 us -> 60.3 us
  Pallas kernels: 11.9 us -> 20.6 us
  matrix products: 22.6 us -> 26.7 us
    reduce_sum x10 -> x0, other arithmetic: 71.8 us -> none  [the longest x3 20.7 us: normalize(): return centred * lax.rsqrt(spread + EPSILON) * scale_by + offset]
    ppermute x24, starting transfers between devices: 49.8 us -> 20.7 us  [shifted(): return lax.ppermute(value, axis, pairs)]
    ppermute x24, waiting for transfers between devices: 46.4 us -> 59.9 us  [shifted(): return lax.ppermute(value, axis, pairs)]
    ppermute x23 -> x25, waiting for transfers between devices: 78.2 us -> 67.4 us  [exchanged(): lax.ppermute(value, axis, [(source, source ^ mask) for source in range(co...]
    convert_element_type x16 -> x12, other arithmetic: 19.1 us -> 8.76 us  [the longest x7 5.4 us: ring_sum(): arrived = shifted(moving.astype(jnp.bfloat16), 'ctx', 1)]
    another operation x4 -> x6, local copies, waits for them, and re-layouts: 0.38 us -> 10.4 us
    pallas_call x0 -> x5, Pallas kernels: none -> 8.73 us  [row_call(): pl.pallas_call(kernel, grid=(tokens // block,), out_shape=out_shape, in_s...]
    dot_general x8 -> x10, matrix products: 11.1 us -> 16.7 us  [outer(): jnp.einsum('td,tf->df', left, right, preferred_element_type=jnp.float32)]
  transfers between devices with their start and end apart: 47 -> 49, of which waited for: 20 -> 23; matrix products, arithmetic and copies ran while one was open for 35% -> 30% of each run, Pallas kernels for 2% -> 4%
where the time goes in v2:
time: 330 us; the launch traced here: 329 us
  waiting for transfers between devices  127 us (38%)
  local copies, waits for them, and re-layouts  60.3 us (18%)
  starting transfers between devices  46.2 us (14%)
  other arithmetic  43 us (13%)
  matrix products  26.7 us (8%)
  Pallas kernels  20.6 us (6%)
  between operations  4.61 us (1%)
    ppermute x25, waiting for transfers between devices, exchanged(): lax.ppermute(value, axis, [(source, source ^ mask) for source in range(co...  67.4 us
    ppermute x24, waiting for transfers between devices, shifted(): return lax.ppermute(value, axis, pairs)  59.9 us
    ppermute x25, starting transfers between devices, exchanged(): lax.ppermute(value, axis, [(source, source ^ mask) for source in range(co...  25.5 us
    ppermute x24, starting transfers between devices, shifted(): return lax.ppermute(value, axis, pairs)  20.7 us
    unnamed x144, local copies, waits for them, and re-layouts  20.6 us
    dot_general x10, matrix products, outer(): jnp.einsum('td,tf->df', left, right, preferred_element_type=jnp.float32)  16.7 us
    pallas_call x2, Pallas kernels, head_call(): pl.pallas_call(functools.partial(kernel, blocks, heads, 1.0 / math.sqrt(H...  11.9 us
    convert_element_type x8, other arithmetic, add_bf(): (left.astype(jnp.float32) + right.astype(jnp.float32)).astype(jnp.bfloat16)  9.19 us
  transfers between devices with their start and end apart: 49, of which 23 were waited for; matrix products, arithmetic and copies ran while one was open for 30% of the time, Pallas kernels for 4%

profile of v2, /device:TPU:0, one launch (start us, length us, event | category | flops | bytes accessed | tf_op | source)
XLA Modules:
  0.0 328.8 jit_solution(2468882990057140421)
XLA Ops:
  2.5 3.0 collective-permute-start
  11.6 12.4 %collective-permute-done = bf16[512,768]{1,0:T(8,128)(2,1)} collective-permute-done((bf16[512,768]{1,0:T(8,128)(2,1)S(1)}, bf16[512,768]{1,0:T(8,128)(2,1)}, u32[]{:S(2)}, u32[]{:S(2)}) %collective-permute-start) | collective-permute-done | bytes 786464 | tf_op jit(solution)/shard_map/ppermute | solution.py:61
  27.7 4.1 %collective-permute-start.3 = (bf16[512,192]{0,1:T(8,128)(2,1)}, bf16[512,192]{0,1:T(8,128)(2,1)S(1)}, u32[]{:S(2)}, u32[]{:S(2)}) collective-permute-start(bf16[512,192]{0,1:T(8,128)(2,1)} %get-tuple-element.84), channel_id=1, source_target_pairs={{0,12},{4,0},{8,4},{12,8},{1,13},{5,1},{9,5},{13,9},{2,14},{6,2},{... | collective-permute-start | bytes 589832 | tf_op jit(solution)/shard_map/ppermute | solution.py:22
  32.8 18.4 %collective-permute-done.8 = bf16[512,256]{1,0:T(8,128)(2,1)} collective-permute-done((bf16[512,256]{1,0:T(8,128)(2,1)S(1)}, bf16[512,256]{1,0:T(8,128)(2,1)}, u32[]{:S(2)}, u32[]{:S(2)}) %collective-permute-start.8) | collective-permute-done | bytes 262176 | tf_op jit(solution)/shard_map/ppermute | solution.py:61
  61.4 4.5 %shard_map.195 = bf16[4,2,256,64]{3,2,1,0:T(8,128)(2,1)S(1)} custom-call(f32[1,1,1024]{2,1,0:T(1,128)S(1)} %mul.114.bias_ref, f32[1,1024]{1,0:T(1,128)S(1)} %convert_element_type.291.row_ref, f32[1024,1]{1,0:T(8,128)S(1)} %copy-done.14, bf16[4,2,256,192]{3,2,1,0:T(8,128)(2,1)S(1)} %pad_maximum_fusion.3.in_ref, bf16[1024,1024]{1,0:T(8,128)(2,1)S(1)} %pad_maximum_fusion.gate_ref), custom_call_target="tpu_custom_call" | custom-call | flops 402653184 | bytes 2097152 | tf_op jit(solution)/shard_map/pallas_call | solution.py:432
  66.0 3.9 %collective-permute-start.5 = (bf16[512,64]{1,0:T(8,128)(2,1)S(1)}, bf16[512,64]{1,0:T(8,128)(2,1)S(1)}, u32[]{:S(2)}, u32[]{:S(2)}) collective-permute-start(bf16[512,64]{1,0:T(8,128)(2,1)S(1)} %bitcast.254), channel_id=1, source_target_pairs={{0,12},{4,0},{8,4},{12,8},{1,13},{5,1},{9,5},{13,9},{2,14},{6,2},{... | collective-permute-start | bytes 196616 | tf_op jit(solution)/shard_map/ppermute | solution.py:22
  70.9 2.9 collective-permute-done.5
  73.8 6.8 %collective-permute-done.6 = bf16[512,64]{1,0:T(8,128)(2,1)S(1)} collective-permute-done((bf16[512,64]{1,0:T(8,128)(2,1)S(1)}, bf16[512,64]{1,0:T(8,128)(2,1)S(1)}, u32[]{:S(2)}, u32[]{:S(2)}) %collective-permute-start.6) | collective-permute-done | bytes 65568 | tf_op jit(solution)/shard_map/ppermute | solution.py:22
  85.5 12.5 %collective-permute-done.10 = bf16[256,1024]{1,0:T(8,128)(2,1)S(1)} collective-permute-done((bf16[256,1024]{1,0:T(8,128)(2,1)S(1)}, bf16[256,1024]{1,0:T(8,128)(2,1)S(1)}, u32[]{:S(2)}, u32[]{:S(2)}) %collective-permute-start.10) | collective-permute-done | bytes 524320 | tf_op jit(solution)/shard_map/ppermute | solution.py:61
  98.3 9.3 %collective-permute-done.12 = bf16[512,1024]{1,0:T(8,128)(2,1)S(1)} collective-permute-done((bf16[512,1024]{1,0:T(8,128)(2,1)}, bf16[512,1024]{1,0:T(8,128)(2,1)S(1)}, u32[]{:S(2)}, u32[]{:S(2)}) %collective-permute-start.12) | collective-permute-done | bytes 1048608 | tf_op jit(solution)/shard_map/ppermute | solution.py:61
  124.8 2.8 pad_maximum_fusion.2.weight_ref
  135.3 8.0 %collective-permute-done.14 = bf16[256,1024]{1,0:T(8,128)(2,1)S(1)} collective-permute-done((bf16[256,1024]{1,0:T(8,128)(2,1)S(1)}, bf16[256,1024]{1,0:T(8,128)(2,1)S(1)}, u32[]{:S(2)}, u32[]{:S(2)}) %collective-permute-start.14) | collective-permute-done | bytes 524320 | tf_op jit(solution)/shard_map/ppermute | solution.py:61
  176.0 7.4 %shard_map.198 = bf16[4,2,256,192]{3,2,1,0:T(8,128)(2,1)S(1)} custom-call(f32[1,1,1024]{2,1,0:T(1,128)S(1)} %mul.114.bias_ref, f32[1,1024]{1,0:T(1,128)S(1)} %convert_element_type.291.row_ref, f32[1024,1]{1,0:T(8,128)S(1)} %copy-done.15, bf16[4,2,256,192]{3,2,1,0:T(8,128)(2,1)S(1)} %copy-done.7, bf16[4,2,256,64]{3,2,1,0:T(8,128)(2,1)S(1)} %pad_maximum_fusion.8.grad_ref), custom_call_target="tpu_custom_call" | custom-call | flops 1073741824 | bytes 2097152 | tf_op jit(solution)/shard_map/pallas_call | solution.py:432
  188.4 3.8 %collective-permute-start.22 = (bf16[512,192]{0,1:T(8,128)(2,1)}, bf16[512,192]{0,1:T(8,128)(2,1)}, u32[]{:S(2)}, u32[]{:S(2)}) collective-permute-start(bf16[512,192]{0,1:T(8,128)(2,1)} %copy.79), channel_id=1, source_target_pairs={{0,12},{4,0},{8,4},{12,8},{1,13},{5,1},{9,5},{13,9},{2,14},{6,2},{... | collective-permute-start | bytes 589832 | tf_op jit(solution)/shard_map/ppermute | solution.py:22
  201.4 8.1 %collective-permute-done.23 = bf16[512,192]{0,1:T(8,128)(2,1)S(1)} collective-permute-done((bf16[512,192]{0,1:T(8,128)(2,1)}, bf16[512,192]{0,1:T(8,128)(2,1)S(1)}, u32[]{:S(2)}, u32[]{:S(2)}) %collective-permute-start.23) | collective-permute-done | bytes 196640 | tf_op jit(solution)/shard_map/ppermute | solution.py:22
  217.6 2.8 shard_map.199
  228.0 3.5 %collective-permute-done.29 = f32[60,128]{1,0:T(8,128)S(1)} collective-permute-done((f32[60,128]{1,0:T(8,128)S(1)}, f32[60,128]{1,0:T(8,128)S(1)}, u32[]{:S(2)}, u32[]{:S(2)}) %collective-permute-start.29) | collective-permute-done | bytes 30752 | tf_op jit(solution)/shard_map/ppermute | solution.py:61
  239.4 5.1 %collective-permute-done.38 = bf16[128,256]{1,0:T(8,128)(2,1)} collective-permute-done((bf16[128,256]{1,0:T(8,128)(2,1)S(1)}, bf16[128,256]{1,0:T(8,128)(2,1)}, u32[]{:S(2)}, u32[]{:S(2)}) %collective-permute-start.38) | collective-permute-done | bytes 65568 | tf_op jit(solution)/shard_map/ppermute | solution.py:22
  249.3 6.0 %collective-permute-done.39 = bf16[128,256]{1,0:T(8,128)(2,1)S(1)} collective-permute-done((bf16[128,256]{1,0:T(8,128)(2,1)S(1)}, bf16[128,256]{1,0:T(8,128)(2,1)S(1)}, u32[]{:S(2)}, u32[]{:S(2)}) %collective-permute-start.39) | collective-permute-done | bytes 65568 | tf_op jit(solution)/shard_map/ppermute | solution.py:22
  257.0 5.4 %collective-permute-done.40 = bf16[128,256]{1,0:T(8,128)(2,1)S(1)} collective-permute-done((bf16[128,256]{1,0:T(8,128)(2,1)S(1)}, bf16[128,256]{1,0:T(8,128)(2,1)S(1)}, u32[]{:S(2)}, u32[]{:S(2)}) %collective-permute-start.40) | collective-permute-done | bytes 65568 | tf_op jit(solution)/shard_map/ppermute | solution.py:22
  275.8 11.6 %collective-permute-done.44 = bf16[128,1024]{1,0:T(8,128)(2,1)S(1)} collective-permute-done((bf16[128,1024]{1,0:T(8,128)(2,1)S(1)}, bf16[128,1024]{1,0:T(8,128)(2,1)S(1)}, u32[]{:S(2)}, u32[]{:S(2)}) %collective-permute-start.44) | collective-permute-done | bytes 262176 | tf_op jit(solution)/shard_map/ppermute | solution.py:22
  308.8 4.3 %collective-permute-done.35 = bf16[128,768]{0,1:T(8,128)(2,1)S(1)} collective-permute-done((bf16[128,768]{0,1:T(8,128)(2,1)S(1)}, bf16[128,768]{0,1:T(8,128)(2,1)S(1)}, u32[]{:S(2)}, u32[]{:S(2)}) %collective-permute-start.35) | collective-permute-done | bytes 196640 | tf_op jit(solution)/shard_map/ppermute | solution.py:22
  316.0 4.8 %collective-permute-done.36 = bf16[128,768]{0,1:T(8,128)(2,1)S(1)} collective-permute-done((bf16[128,768]{0,1:T(8,128)(2,1)S(1)}, bf16[128,768]{0,1:T(8,128)(2,1)S(1)}, u32[]{:S(2)}, u32[]{:S(2)}) %collective-permute-start.36) | collective-permute-done | bytes 196640 | tf_op jit(solution)/shard_map/ppermute | solution.py:22
  325.3 3.5 %copy.94 = f32[2,256,1,1024]{3,2,1,0:T(1,128)} copy(f32[2,256,1,1024]{3,1,0,2:T(8,128)S(1)} %bitcast.196) | data formatting | bytes 4194304
  (355 shorter events, 169.0 us)
Async XLA Ops:
  2.5 21.5 %collective-permute-start = (bf16[512,768]{1,0:T(8,128)(2,1)S(1)}, bf16[512,768]{1,0:T(8,128)(2,1)}, u32[]{:S(2)}, u32[]{:S(2)}) collective-permute-start(bf16[512,768]{1,0:T(8,128)(2,1)S(1)} %copy.64), channel_id=1, source_target_pairs={{0,16},{16,0},{1,17},{17,1},{2,18},{18,2},{3,19},{19,3},{4,20},{20... | collective-permute-start | bytes 2359304 | tf_op jit(solution)/shard_map/ppermute | solution.py:61
  5.5 51.6 %collective-permute-start.4 = (bf16[512,1024]{1,0:T(8,128)(2,1)}, bf16[512,1024]{1,0:T(8,128)(2,1)}, u32[]{:S(2)}, u32[]{:S(2)}) collective-permute-start(bf16[512,1024]{1,0:T(8,128)(2,1)} %param.19), channel_id=1, source_target_pairs={{0,16},{16,0},{1,17},{17,1},{2,18},{18,2},{3,19},{19,3},{4,20},{20... | collective-permute-start | bytes 3145736 | tf_op jit(solution)/shard_map/ppermute | solution.py:61
  5.6 45.7 %collective-permute-start.8 = (bf16[512,256]{1,0:T(8,128)(2,1)S(1)}, bf16[512,256]{1,0:T(8,128)(2,1)}, u32[]{:S(2)}, u32[]{:S(2)}) collective-permute-start(bf16[512,256]{1,0:T(8,128)(2,1)S(1)} %copy-done.51), channel_id=1, source_target_pairs={{0,16},{16,0},{1,17},{17,1},{2,18},{18,2},{3,19},{19,3},{4,20},{20... | collective-permute-start | bytes 786440 | tf_op jit(solution)/shard_map/ppermute | solution.py:61
  27.7 25.6 %collective-permute-start.3 = (bf16[512,192]{0,1:T(8,128)(2,1)}, bf16[512,192]{0,1:T(8,128)(2,1)S(1)}, u32[]{:S(2)}, u32[]{:S(2)}) collective-permute-start(bf16[512,192]{0,1:T(8,128)(2,1)} %get-tuple-element.84), channel_id=1, source_target_pairs={{0,12},{4,0},{8,4},{12,8},{1,13},{5,1},{9,5},{13,9},{2,14},{6,2},{... | collective-permute-start | bytes 589832 | tf_op jit(solution)/shard_map/ppermute | solution.py:22
  31.8 22.3 %collective-permute-start.2 = (bf16[512,192]{0,1:T(8,128)(2,1)}, bf16[512,192]{0,1:T(8,128)(2,1)S(1)}, u32[]{:S(2)}, u32[]{:S(2)}) collective-permute-start(bf16[512,192]{0,1:T(8,128)(2,1)} %get-tuple-element.85), channel_id=1, source_target_pairs={{0,8},{4,12},{8,0},{12,4},{1,9},{5,13},{9,1},{13,5},{2,10},{6,14},... | collective-permute-start | bytes 589832 | tf_op jit(solution)/shard_map/ppermute | solution.py:22
  31.8 23.1 %collective-permute-start.1 = (bf16[512,192]{0,1:T(8,128)(2,1)}, bf16[512,192]{0,1:T(8,128)(2,1)S(1)}, u32[]{:S(2)}, u32[]{:S(2)}) collective-permute-start(bf16[512,192]{0,1:T(8,128)(2,1)} %get-tuple-element.86), channel_id=1, source_target_pairs={{0,4},{4,8},{8,12},{12,0},{1,5},{5,9},{9,13},{13,1},{2,6},{6,10},{... | collective-permute-start | bytes 589832 | tf_op jit(solution)/shard_map/ppermute | solution.py:22
  81.8 25.8 %collective-permute-start.12 = (bf16[512,1024]{1,0:T(8,128)(2,1)}, bf16[512,1024]{1,0:T(8,128)(2,1)S(1)}, u32[]{:S(2)}, u32[]{:S(2)}) collective-permute-start(bf16[512,1024]{1,0:T(8,128)(2,1)} %param.21), channel_id=1, source_target_pairs={{0,16},{16,0},{1,17},{17,1},{2,18},{18,2},{3,19},{19,3},{4,20},{20... | collective-permute-start | bytes 3145736 | tf_op jit(solution)/shard_map/ppermute | solution.py:61
  84.0 14.0 %collective-permute-start.10 = (bf16[256,1024]{1,0:T(8,128)(2,1)S(1)}, bf16[256,1024]{1,0:T(8,128)(2,1)S(1)}, u32[]{:S(2)}, u32[]{:S(2)}) collective-permute-start(bf16[256,1024]{1,0:T(8,128)(2,1)S(1)} %add_convert_fusion.11), channel_id=1, source_target_pairs={{0,2},{1,3},{2,0},{3,1},{4,6},{5,7},{6,4},{7,5},{8,10},{9,11},{10,... | collective-permute-start | bytes 1572872 | tf_op jit(solution)/shard_map/ppermute | solution.py:61
  129.0 14.4 %collective-permute-start.14 = (bf16[256,1024]{1,0:T(8,128)(2,1)S(1)}, bf16[256,1024]{1,0:T(8,128)(2,1)S(1)}, u32[]{:S(2)}, u32[]{:S(2)}) collective-permute-start(bf16[256,1024]{1,0:T(8,128)(2,1)S(1)} %add_convert_fusion.9), channel_id=1, source_target_pairs={{0,2},{1,3},{2,0},{3,1},{4,6},{5,7},{6,4},{7,5},{8,10},{9,11},{10,... | collective-permute-start | bytes 1572872 | tf_op jit(solution)/shard_map/ppermute | solution.py:61
  132.3 64.1 %collective-permute-start.41 = (bf16[512,1024]{1,0:T(8,128)(2,1)}, bf16[512,1024]{1,0:T(8,128)(2,1)}, u32[]{:S(2)}, u32[]{:S(2)}) collective-permute-start(bf16[512,1024]{1,0:T(8,128)(2,1)} %convolution_convert_fusion.2), channel_id=1, source_target_pairs={{0,16},{16,0},{1,17},{17,1},{2,18},{18,2},{3,19},{19,3},{4,20},{20... | collective-permute-start | bytes 3145736 | tf_op jit(solution)/shard_map/ppermute | solution.py:61
  135.1 28.7 %collective-permute-start.45 = (bf16[256,1024]{1,0:T(8,128)(2,1)}, bf16[256,1024]{1,0:T(8,128)(2,1)}, u32[]{:S(2)}, u32[]{:S(2)}) collective-permute-start(bf16[256,1024]{1,0:T(8,128)(2,1)} %convolution_convert_fusion.4), channel_id=1, source_target_pairs={{0,4},{4,8},{8,12},{12,0},{1,5},{5,9},{9,13},{13,1},{2,6},{6,10},{... | collective-permute-start | bytes 1572872 | tf_op jit(solution)/shard_map/ppermute | solution.py:22
  153.4 110.6 %collective-permute-start.16 = (bf16[256,1024]{1,0:T(8,128)(2,1)}, bf16[256,1024]{1,0:T(8,128)(2,1)}, u32[]{:S(2)}, u32[]{:S(2)}) collective-permute-start(bf16[256,1024]{1,0:T(8,128)(2,1)} %broadcast_select_fusion.11), channel_id=1, source_target_pairs={{0,1},{1,0},{2,3},{3,2},{4,5},{5,4},{6,7},{7,6},{8,9},{9,8},{10,11... | collective-permute-start | bytes 1572872 | tf_op jit(solution)/shard_map/ppermute | solution.py:61
  169.3 54.3 %collective-permute-start.37 = (bf16[512,256]{1,0:T(8,128)(2,1)}, bf16[512,256]{1,0:T(8,128)(2,1)}, u32[]{:S(2)}, u32[]{:S(2)}) collective-permute-start(bf16[512,256]{1,0:T(8,128)(2,1)} %convolution_convert_fusion.5), channel_id=1, source_target_pairs={{0,16},{16,0},{1,17},{17,1},{2,18},{18,2},{3,19},{19,3},{4,20},{20... | collective-permute-start | bytes 786440 | tf_op jit(solution)/shard_map/ppermute | solution.py:61
  172.5 94.9 %collective-permute-start.46 = (bf16[256,1024]{1,0:T(8,128)(2,1)}, bf16[256,1024]{1,0:T(8,128)(2,1)}, u32[]{:S(2)}, u32[]{:S(2)}) collective-permute-start(bf16[256,1024]{1,0:T(8,128)(2,1)} %add_convert_fusion.3), channel_id=1, source_target_pairs={{0,4},{4,8},{8,12},{12,0},{1,5},{5,9},{9,13},{13,1},{2,6},{6,10},{... | collective-permute-start | bytes 1572872 | tf_op jit(solution)/shard_map/ppermute | solution.py:22
  196.4 13.1 %collective-permute-start.23 = (bf16[512,192]{0,1:T(8,128)(2,1)}, bf16[512,192]{0,1:T(8,128)(2,1)S(1)}, u32[]{:S(2)}, u32[]{:S(2)}) collective-permute-start(bf16[512,192]{0,1:T(8,128)(2,1)} %copy.80), channel_id=1, source_target_pairs={{0,8},{4,12},{8,0},{12,4},{1,9},{5,13},{9,1},{13,5},{2,10},{6,14},... | collective-permute-start | bytes 589832 | tf_op jit(solution)/shard_map/ppermute | solution.py:22
  209.5 23.5 %collective-permute-start.42 = (bf16[128,1024]{1,0:T(8,128)(2,1)}, bf16[128,1024]{1,0:T(8,128)(2,1)}, u32[]{:S(2)}, u32[]{:S(2)}) collective-permute-start(bf16[128,1024]{1,0:T(8,128)(2,1)} %fusion.31), channel_id=1, source_target_pairs={{0,4},{4,8},{8,12},{12,0},{1,5},{5,9},{9,13},{13,1},{2,6},{6,10},{... | collective-permute-start | bytes 786440 | tf_op jit(solution)/shard_map/ppermute | solution.py:22
  221.2 49.9 %collective-permute-start.25 = (bf16[256,1024]{1,0:T(8,128)(2,1)}, bf16[256,1024]{1,0:T(8,128)(2,1)}, u32[]{:S(2)}, u32[]{:S(2)}) collective-permute-start(bf16[256,1024]{1,0:T(8,128)(2,1)} %broadcast_select_fusion.8), channel_id=1, source_target_pairs={{0,1},{1,0},{2,3},{3,2},{4,5},{5,4},{6,7},{7,6},{8,9},{9,8},{10,11... | collective-permute-start | bytes 1572872 | tf_op jit(solution)/shard_map/ppermute | solution.py:61
  231.5 58.9 %collective-permute-start.33 = (bf16[512,768]{1,0:T(8,128)(2,1)}, bf16[512,768]{1,0:T(8,128)(2,1)}, u32[]{:S(2)}, u32[]{:S(2)}) collective-permute-start(bf16[512,768]{1,0:T(8,128)(2,1)} %convolution_convert_fusion.3), channel_id=1, source_target_pairs={{0,16},{16,0},{1,17},{17,1},{2,18},{18,2},{3,19},{19,3},{4,20},{20... | collective-permute-start | bytes 2359304 | tf_op jit(solution)/shard_map/ppermute | solution.py:61
  265.8 22.5 %collective-permute-start.17 = (bf16[256,1024]{1,0:T(8,128)(2,1)S(1)}, bf16[256,1024]{1,0:T(8,128)(2,1)S(1)}, u32[]{:S(2)}, u32[]{:S(2)}) collective-permute-start(bf16[256,1024]{1,0:T(8,128)(2,1)S(1)} %add_convert_fusion.7), channel_id=1, source_target_pairs={{0,2},{1,3},{2,0},{3,1},{4,6},{5,7},{6,4},{7,5},{8,10},{9,11},{10,... | collective-permute-start | bytes 1572872 | tf_op jit(solution)/shard_map/ppermute | solution.py:61
  268.6 20.7 %collective-permute-start.47 = (bf16[256,1024]{1,0:T(8,128)(2,1)S(1)}, bf16[256,1024]{1,0:T(8,128)(2,1)S(1)}, u32[]{:S(2)}, u32[]{:S(2)}) collective-permute-start(bf16[256,1024]{1,0:T(8,128)(2,1)S(1)} %add_convert_fusion.2), channel_id=1, source_target_pairs={{0,4},{4,8},{8,12},{12,0},{1,5},{5,9},{9,13},{13,1},{2,6},{6,10},{... | collective-permute-start | bytes 1572872 | tf_op jit(solution)/shard_map/ppermute | solution.py:22
  271.1 16.3 %collective-permute-start.44 = (bf16[128,1024]{1,0:T(8,128)(2,1)S(1)}, bf16[128,1024]{1,0:T(8,128)(2,1)S(1)}, u32[]{:S(2)}, u32[]{:S(2)}) collective-permute-start(bf16[128,1024]{1,0:T(8,128)(2,1)S(1)} %fusion.12), channel_id=1, source_target_pairs={{0,4},{4,8},{8,12},{12,0},{1,5},{5,9},{9,13},{13,1},{2,6},{6,10},{... | collective-permute-start | bytes 786440 | tf_op jit(solution)/shard_map/ppermute | solution.py:22
  273.4 31.4 %collective-permute-start.26 = (bf16[256,1024]{1,0:T(8,128)(2,1)}, bf16[256,1024]{1,0:T(8,128)(2,1)}, u32[]{:S(2)}, u32[]{:S(2)}) collective-permute-start(bf16[256,1024]{1,0:T(8,128)(2,1)} %add_convert_fusion.5), channel_id=1, source_target_pairs={{0,2},{1,3},{2,0},{3,1},{4,6},{5,7},{6,4},{7,5},{8,10},{9,11},{10,... | collective-permute-start | bytes 1572872 | tf_op jit(solution)/shard_map/ppermute | solution.py:61
  289.3 24.0 %collective-permute-start.18 = (bf16[256,1024]{1,0:T(8,128)(2,1)}, bf16[256,1024]{1,0:T(8,128)(2,1)}, u32[]{:S(2)}, u32[]{:S(2)}) collective-permute-start(bf16[256,1024]{1,0:T(8,128)(2,1)} %add_convert_fusion.6), channel_id=1, source_target_pairs={{0,1},{1,0},{2,3},{3,2},{4,5},{5,4},{6,7},{7,6},{8,9},{9,8},{10,11... | collective-permute-start | bytes 1572872 | tf_op jit(solution)/shard_map/ppermute | solution.py:61
  307.0 14.8 %collective-permute-start.27 = (bf16[256,1024]{1,0:T(8,128)(2,1)}, bf16[256,1024]{1,0:T(8,128)(2,1)}, u32[]{:S(2)}, u32[]{:S(2)}) collective-permute-start(bf16[256,1024]{1,0:T(8,128)(2,1)} %add_convert_fusion.4), channel_id=1, source_target_pairs={{0,1},{1,0},{2,3},{3,2},{4,5},{5,4},{6,7},{7,6},{8,9},{9,8},{10,11... | collective-permute-start | bytes 1572872 | tf_op jit(solution)/shard_map/ppermute | solution.py:61
  (85 other events, 498.9 us)

commit v3 on v2

--- a/solution.py
+++ b/solution.py
@@ -88,6 +88,82 @@
     return jnp.concatenate(
         [jnp.where(even, total, other), jnp.where(even, other, total)], 0
     )
+
+
+SUM_PIECES = 4
+
+
+def tp_kernel(x_ref, *refs):
+    out_ref, first, near, far, total, back, sems = refs[-7:]
+    me = lax.axis_index("tp")
+    odd = lax.rem(me, 2)
+    mate = me + 1 - 2 * odd
+    across = lax.rem(me + 2, 4)
+    rows = x_ref.shape[0] // 2
+    size = rows // SUM_PIECES
+    barrier = pltpu.get_barrier_semaphore()
+    for partner in (mate, across):
+        pl.semaphore_signal(
+            barrier, inc=1, device_id={"tp": partner}, device_id_type=pl.DeviceIdType.MESH
+        )
+    pl.semaphore_wait(barrier, 2)
+
+    def copy(source, target, stage, piece, partner):
+        made = pltpu.make_async_remote_copy(
+            src_ref=source,
+            dst_ref=target,
+            send_sem=sems.at[2 * stage, piece],
+            recv_sem=sems.at[2 * stage + 1, piece],
+            device_id={"tp": partner},
+            device_id_type=pl.DeviceIdType.MESH,
+        )
+        made.start()
+        return made
+
+    def span(half, piece):
+        return pl.ds(pl.multiple_of(half * rows + piece * size, size), size)
+
+    stages = [[], [], []]
+    for piece in range(SUM_PIECES):
+        stages[0].append(
+            copy(x_ref.at[span(1 - odd, piece), :], first.at[piece], 0, piece, mate)
+        )
+    for piece in range(SUM_PIECES):
+        stages[0][piece].wait_recv()
+        near[piece] = add_bf(x_ref[span(odd, piece), :], first[piece])
+        stages[1].append(copy(near.at[piece], far.at[piece], 1, piece, across))
+    for piece in range(SUM_PIECES):
+        stages[1][piece].wait_recv()
+        total[piece] = add_bf(near[piece], far[piece])
+        stages[2].append(copy(total.at[piece], back.at[piece], 2, piece, mate))
+        out_ref[span(odd, piece), :] = total[piece]
+    for piece in range(SUM_PIECES):
+        stages[2][piece].wait_recv()
+        out_ref[span(1 - odd, piece), :] = back[piece]
+    for stage in stages:
+        for made in stage:
+            made.wait_send()
+
+
+def sum_over_tp_now(partial, gates=()):
+    rows, width = partial.shape
+    if lax.axis_size("tp") != 4 or rows % (32 * SUM_PIECES) != 0:
+        return sum_over_tp(partial)
+    piece = pltpu.VMEM((SUM_PIECES, rows // (2 * SUM_PIECES), width), jnp.bfloat16)
+    return pl.pallas_call(
+        tp_kernel,
+        out_shape=jax.ShapeDtypeStruct((rows, width), jnp.bfloat16),
+        in_specs=[pl.BlockSpec(memory_space=pltpu.VMEM)]
+        + [pl.BlockSpec(memory_space=pl.ANY) for gate in gates],
+        out_specs=pl.BlockSpec(memory_space=pltpu.VMEM),
+        scratch_shapes=[piece] * 5 + [pltpu.SemaphoreType.DMA((6, SUM_PIECES))],
+        compiler_params=pltpu.CompilerParams(
+            collective_id=len(gates), has_side_effects=True, vmem_limit_bytes=24 * 2**20
+        ),
+        cost_estimate=pl.CostEstimate(
+            flops=2 * rows * width, bytes_accessed=30 * rows * width, transcendentals=0
+        ),
+    )(partial.astype(jnp.bfloat16), *gates)
 
 
 def sum_small(values, axes):
@@ -133,7 +209,7 @@
     return value + (0.0 * first.astype(jnp.float32)).astype(value.dtype)
 
 
-def ring_sum(chunk, gates=()):
+def ring_sum(chunk, gates=(), seen=None):
     count = lax.axis_size("ctx")
     me = lax.axis_index("ctx")
     moving = chunk(lax.rem(me + count - 1, count))
@@ -142,35 +218,44 @@
         term = chunk(lax.rem(me + 2 * count - 2 - step, count))
         gate = gates[step] if step < len(gates) else None
         moving = after(arrived.astype(jnp.float32) + term, gate)
+        if seen is not None:
+            seen.append(moving)
     return moving
 
 
-def owned_grad(left, right, gate=None):
-    count = lax.axis_size("ctx")
+def shard_half(left, right, gate=None):
     if lax.axis_size("shard") != 2:
-        return lax.psum_scatter(
-            outer(left, right), ("shard", "ctx"), scatter_dimension=0, tiled=True
-        )
+        return lax.psum_scatter(outer(left, right), "shard", scatter_dimension=0, tiled=True)
     half_width = left.shape[1] // 2
     shard = lax.axis_index("shard")
     theirs = lax.dynamic_slice_in_dim(left, (1 - shard) * half_width, half_width, 1)
     mine = lax.dynamic_slice_in_dim(left, shard * half_width, half_width, 1)
     arrived = exchanged(outer(theirs, right).astype(jnp.bfloat16), "shard", 1)
-    half = after(outer(mine, right) + arrived.astype(jnp.float32), gate)
+    return after(outer(mine, right) + arrived.astype(jnp.float32), gate)
+
+
+def ctx_share(halves, seen=None):
+    count = lax.axis_size("ctx")
     if count > 8:
-        return lax.psum_scatter(half, "ctx", scatter_dimension=0, tiled=True)
-    chunks = half.reshape(count, half_width // count, half.shape[1])
+        return [lax.psum_scatter(half, "ctx", scatter_dimension=0, tiled=True) for half in halves]
+    rows = halves[0].shape[0] // count
 
     def chunk(member):
-        return lax.dynamic_index_in_dim(chunks, member, 0, keepdims=False)
-
-    return ring_sum(chunk)
-
-
-def owned_grad_ring_first(left, right, gates):
+        pieces = [lax.dynamic_slice_in_dim(half, member * rows, rows, 0) for half in halves]
+        return pieces[0] if len(pieces) == 1 else jnp.concatenate(pieces, 1)
+
+    total = ring_sum(chunk, (), seen)
+    shares, start = [], 0
+    for half in halves:
+        shares.append(total[:, start : start + half.shape[1]])
+        start += half.shape[1]
+    return shares
+
+
+def owned_grad_ring_first(left, right, gates, seen):
     count = lax.axis_size("ctx")
     if lax.axis_size("shard") != 2 or count > 8:
-        return owned_grad(left, right)
+        return ctx_share([shard_half(left, right)])[0]
     tokens, width = left.shape
     rows = width // (2 * count)
     pieces = left.reshape(tokens, 2, count, rows).transpose(2, 0, 1, 3)
@@ -179,7 +264,7 @@
     def chunk(member):
         return outer(lax.dynamic_index_in_dim(pieces, member, 0, keepdims=False), right)
 
-    both = ring_sum(chunk, gates)
+    both = ring_sum(chunk, gates, seen)
     first = lax.axis_index("shard") == 0
     low, high = both[:rows], both[rows:]
     arrived = exchanged(jnp.where(first, high, low).astype(jnp.bfloat16), "shard", 1)
@@ -642,10 +727,13 @@
     value_bf = (projected[:, 2] + qv_shift[1]).astype(jnp.bfloat16)
     attend = attend_spread if heads_loc % cycle_size == 0 else attend_ring
     attended_bf, attend_back = attend(
-        query_bf, key_bf, value_bf, slopes, seq_dev, group_len, full_up
-    )
-    branch = sum_over_tp(
-        jnp.einsum("tf,df->td", attended_bf, full_out, preferred_element_type=jnp.float32)
+        query_bf, key_bf, value_bf, slopes, seq_dev, group_len, full_out
+    )
+    branch = sum_over_tp_now(
+        after(
+            jnp.einsum("tf,df->td", attended_bf, full_out, preferred_element_type=jnp.float32),
+            full_up,
+        )
     )
     resid, normed_two = row_call(
         norm_two_kernel,
@@ -662,7 +750,7 @@
     pre_grad = jax.vjp(gelu_tanh, pre_act)[1](act_grad)[0]
     pre_grad_bf = pre_grad.astype(jnp.bfloat16)
     hidden_grad = jnp.sum(pre_grad_bf.astype(jnp.float32), axis=0)
-    norm_two_grad = sum_over_tp(
+    norm_two_grad = sum_over_tp_now(
         jnp.einsum("tf,df->td", pre_grad_bf, full_up, preferred_element_type=jnp.float32)
     )
     resid_grad, resid_bf, sums_two = row_call(
@@ -696,7 +784,10 @@
         True,
         row_flops + 6 * tok_rows * model_width * local_width,
     )
-    norm_one_grad = sum_over_tp(norm_one_part)
+    down_seen, up_seen = [], []
+    grad_down = owned_grad_ring_first(dy_rows, act_bf, (norm_two_grad, attend_done), down_seen)
+    (grad_up,) = ctx_share([shard_half(normed_two, pre_grad_bf, attend_done)], up_seen)
+    norm_one_grad = sum_over_tp_now(norm_one_part, tuple(down_seen[-1:] + up_seen[:1]))
     (input_grad,) = row_call(
         norm_one_back_kernel,
         (gains,),
@@ -707,10 +798,9 @@
         2 * row_flops,
     )
     input_grad = input_grad.reshape(tokens.shape)
-    grad_down = owned_grad_ring_first(dy_rows, act_bf, (norm_two_grad, attend_done))
-    grad_up = owned_grad(normed_two, pre_grad_bf, attend_done)
-    grad_out = owned_grad(resid_bf, attended_bf, qkv_grad_flat)
-    grad_qkv = owned_grad(normed_one, qkv_grad_flat)
+    half_out = shard_half(resid_bf, attended_bf)
+    half_qkv = shard_half(normed_one, qkv_grad_flat)
+    grad_qkv, grad_out = ctx_share([half_qkv, after(half_out, norm_one_grad)])
     grad_qkv = grad_qkv.reshape(grad_qkv.shape[0], 3, local_width)
     qv_grad = jnp.stack(
         [
@@ -719,7 +809,8 @@
         ]
     )
     sums_one, sums_two, qv_grad, hidden_grad = sum_small(
-        (sums_one[:2], sums_two[:4], qv_grad, hidden_grad), ("shard", "ctx")
+        (after(sums_one[:2], norm_one_grad), sums_two[:4], qv_grad, hidden_grad),
+        ("shard", "ctx"),
     )
     sums_one = sum_over(sums_one, ("tp",))
     gain_grads = jnp.stack([sums_one[0], sums_two[0]])

time: 330 us -> 306 us (0.927)
  Pallas kernels: 20.6 us -> 70.9 us
  local copies, waits for them, and re-layouts: 60.3 us -> 34.2 us
  other arithmetic: 43 us -> 23.3 us
  waiting for transfers between devices: 127 us -> 112 us
  starting transfers between devices: 46.2 us -> 32.3 us
    pallas_call x0 -> x3, Pallas kernels: none -> 50.3 us  [sum_over_tp_now(): pl.pallas_call(tp_kernel, out_shape=jax.ShapeDtypeStruct((rows, width), j...]
    ppermute x25 -> x16, waiting for transfers between devices: 67.4 us -> 43.7 us  [exchanged(): lax.ppermute(value, axis, [(source, source ^ mask) for source in range(co...]
    ppermute x25 -> x16, starting transfers between devices: 25.5 us -> 13.6 us  [exchanged(): lax.ppermute(value, axis, [(source, source ^ mask) for source in range(co...]
    unnamed x144 -> x126, local copies, waits for them, and re-layouts: 20.6 us -> 10.3 us
    ppermute x24 -> x21, waiting for transfers between devices: 59.9 us -> 68.3 us  [shifted(): return lax.ppermute(value, axis, pairs)]
    convert_element_type x8 -> x2, other arithmetic: 9.19 us -> 1.93 us  [add_bf(): (left.astype(jnp.float32) + right.astype(jnp.float32)).astype(jnp.bfloat16)]
    dynamic_slice x5 -> x2, local copies, waits for them, and re-layouts: 6.23 us -> 1.08 us  [chunk(): lax.dynamic_slice_in_dim(half, member * rows, rows, 0)]
    squeeze x3, local copies, waits for them, and re-layouts: 5.25 us -> 0.37 us  [return_heads(): slots[step]]
  transfers between devices with their start and end apart: 49 -> 37, of which waited for: 23 -> 17; matrix products, arithmetic and copies ran while one was open for 30% -> 19% of each run, Pallas kernels for 4% -> 11%
where the time goes in v3:
time: 306 us
  waiting for transfers between devices  112 us (37%)
  Pallas kernels  70.9 us (23%)
  local copies, waits for them, and re-layouts  34.2 us (11%)
  starting transfers between devices  32.3 us (11%)
  matrix products  27.5 us (9%)
  other arithmetic  23.3 us (8%)
  between operations  5.45 us (2%)
    ppermute x21, waiting for transfers between devices, shifted(): return lax.ppermute(value, axis, pairs)  68.3 us
    pallas_call x3, Pallas kernels, sum_over_tp_now(): pl.pallas_call(tp_kernel, out_shape=jax.ShapeDtypeStruct((rows, width), j...  50.3 us
    ppermute x16, waiting for transfers between devices, exchanged(): lax.ppermute(value, axis, [(source, source ^ mask) for source in range(co...  43.7 us
    ppermute x21, starting transfers between devices, shifted(): return lax.ppermute(value, axis, pairs)  18.6 us
    dot_general x10, matrix products, outer(): jnp.einsum('td,tf->df', left, right, preferred_element_type=jnp.float32)  16.6 us
    ppermute x16, starting transfers between devices, exchanged(): lax.ppermute(value, axis, [(source, source ^ mask) for source in range(co...  13.6 us
    pallas_call x2, Pallas kernels, head_call(): pl.pallas_call(functools.partial(kernel, blocks, heads, 1.0 / math.sqrt(H...  11.9 us
    unnamed x126, local copies, waits for them, and re-layouts  10.3 us
  transfers between devices with their start and end apart: 37, of which 17 were waited for; matrix products, arithmetic and copies ran while one was open for 19% of the time, Pallas kernels for 11%

profile of v3, /device:TPU:0, one launch (start us, length us, event | category | flops | bytes accessed | tf_op | source)
XLA Modules:
  0.0 305.6 jit_solution(10876072489979239442)
XLA Ops:
  3.4 3.0 collective-permute-start
  15.8 14.8 %collective-permute-done.4 = bf16[512,256]{1,0:T(8,128)(2,1)S(1)} collective-permute-done((bf16[512,256]{1,0:T(8,128)(2,1)S(1)}, bf16[512,256]{1,0:T(8,128)(2,1)S(1)}, u32[]{:S(2)}, u32[]{:S(2)}) %collective-permute-start.4) | collective-permute-done | bytes 262176 | tf_op jit(solution)/shard_map/ppermute | solution.py:61
  34.6 4.1 %collective-permute-start.3 = (bf16[512,192]{0,1:T(8,128)(2,1)}, bf16[512,192]{0,1:T(8,128)(2,1)}, u32[]{:S(2)}, u32[]{:S(2)}) collective-permute-start(bf16[512,192]{0,1:T(8,128)(2,1)} %get-tuple-element.80), channel_id=1, source_target_pairs={{0,12},{4,0},{8,4},{12,8},{1,13},{5,1},{9,5},{13,9},{2,14},{6,2},{... | collective-permute-start | bytes 589832 | tf_op jit(solution)/shard_map/ppermute | solution.py:22
  45.5 9.3 %collective-permute-done.2 = bf16[512,192]{0,1:T(8,128)(2,1)} collective-permute-done((bf16[512,192]{0,1:T(8,128)(2,1)}, bf16[512,192]{0,1:T(8,128)(2,1)}, u32[]{:S(2)}, u32[]{:S(2)}) %collective-permute-start.2) | collective-permute-done | bytes 196640 | tf_op jit(solution)/shard_map/ppermute | solution.py:22
  57.2 4.5 %shard_map.195 = bf16[4,2,256,64]{3,2,1,0:T(8,128)(2,1)S(1)} custom-call(f32[1,1,1024]{2,1,0:T(1,128)S(1)} %mul.138.bias_ref, f32[1,1024]{1,0:T(1,128)S(1)} %convert_element_type.212.row_ref, f32[1024,1]{1,0:T(8,128)S(1)} %convert_element_type.265.column_ref, bf16[4,2,256,192]{3,2,1,0:T(8,128)(2,1)S(1)} %pad_maximum_fusion.5.in_ref, ...), custom_call_target="tpu_custom_call" | custom-call | flops 402653184 | bytes 2097152 | tf_op jit(solution)/shard_map/pallas_call | solution.py:517
  64.6 10.1 %collective-permute-done.9 = bf16[512,1024]{1,0:T(8,128)(2,1)} collective-permute-done((bf16[512,1024]{1,0:T(8,128)(2,1)}, bf16[512,1024]{1,0:T(8,128)(2,1)}, u32[]{:S(2)}, u32[]{:S(2)}) %collective-permute-start.9) | collective-permute-done | bytes 1048608 | tf_op jit(solution)/shard_map/ppermute | solution.py:61
  74.8 2.8 broadcast_select_fusion
  84.2 16.8 %shard_map.196.branch_ref = bf16[512,1024]{1,0:T(8,128)(2,1)S(1)} custom-call(bf16[512,1024]{1,0:T(8,128)(2,1)S(1)} %add_convert_fusion.2.x_ref), custom_call_target="tpu_custom_call" | custom-call | flops 1048576 | bytes 15728640 | tf_op jit(solution)/shard_map/pallas_call | solution.py:153
  109.1 16.8 %shard_map.198.grad_ref = bf16[512,1024]{1,0:T(8,128)(2,1)S(1)} custom-call(bf16[512,1024]{1,0:T(8,128)(2,1)S(1)} %convolution_convert_fusion.x_ref), custom_call_target="tpu_custom_call" | custom-call | flops 1048576 | bytes 15728640 | tf_op jit(solution)/shard_map/pallas_call | solution.py:153
  137.9 3.9 %collective-permute-start.15 = (bf16[512,64]{1,0:T(8,128)(2,1)S(1)}, bf16[512,64]{1,0:T(8,128)(2,1)}, u32[]{:S(2)}, u32[]{:S(2)}) collective-permute-start(bf16[512,64]{1,0:T(8,128)(2,1)S(1)} %bitcast.198), channel_id=1, source_target_pairs={{0,12},{4,0},{8,4},{12,8},{1,13},{5,1},{9,5},{13,9},{2,14},{6,2},{... | collective-permute-start | bytes 196616 | tf_op jit(solution)/shard_map/ppermute | solution.py:22
  151.3 2.7 collective-permute-start.19
  157.5 7.4 %shard_map.200 = bf16[4,2,256,192]{3,2,1,0:T(8,128)(2,1)S(1)} custom-call(f32[1,1,1024]{2,1,0:T(1,128)S(1)} %mul.138.bias_ref, f32[1,1024]{1,0:T(1,128)S(1)} %convert_element_type.212.row_ref, f32[1024,1]{1,0:T(8,128)S(1)} %copy-done.11, bf16[4,2,256,192]{3,2,1,0:T(8,128)(2,1)S(1)} %copy-done.5, bf16[4,2,256,64]{3,2,1,0:T(8,128)(2,1)S(1)} %pad_maximum_fusion.7.grad_ref), custom_call_target="tpu_custom_call" | custom-call | flops 1073741824 | bytes 2097152 | tf_op jit(solution)/shard_map/pallas_call | solution.py:517
  172.9 8.8 %collective-permute-done.17 = bf16[512,192]{0,1:T(8,128)(2,1)S(1)} collective-permute-done((bf16[512,192]{0,1:T(8,128)(2,1)S(1)}, bf16[512,192]{0,1:T(8,128)(2,1)S(1)}, u32[]{:S(2)}, u32[]{:S(2)}) %collective-permute-start.17) | collective-permute-done | bytes 196640 | tf_op jit(solution)/shard_map/ppermute | solution.py:22
  181.8 7.7 %collective-permute-done.18 = bf16[512,192]{0,1:T(8,128)(2,1)S(1)} collective-permute-done((bf16[512,192]{0,1:T(8,128)(2,1)S(1)}, bf16[512,192]{0,1:T(8,128)(2,1)S(1)}, u32[]{:S(2)}, u32[]{:S(2)}) %collective-permute-start.18) | collective-permute-done | bytes 196640 | tf_op jit(solution)/shard_map/ppermute | solution.py:22
  197.4 2.7 shard_map.201
  202.0 5.4 %collective-permute-done.11 = bf16[256,1024]{1,0:T(8,128)(2,1)S(1)} collective-permute-done((bf16[256,1024]{1,0:T(8,128)(2,1)S(1)}, bf16[256,1024]{1,0:T(8,128)(2,1)S(1)}, u32[]{:S(2)}, u32[]{:S(2)}) %collective-permute-start.11) | collective-permute-done | bytes 524320 | tf_op jit(solution)/shard_map/ppermute | solution.py:61
  209.9 6.2 %collective-permute-done.20 = bf16[256,1024]{1,0:T(8,128)(2,1)S(1)} collective-permute-done((bf16[256,1024]{1,0:T(8,128)(2,1)S(1)}, bf16[256,1024]{1,0:T(8,128)(2,1)S(1)}, u32[]{:S(2)}, u32[]{:S(2)}) %collective-permute-start.20) | collective-permute-done | bytes 524320 | tf_op jit(solution)/shard_map/ppermute | solution.py:22
  216.3 5.4 %collective-permute-done.23 = bf16[128,1024]{1,0:T(8,128)(2,1)S(1)} collective-permute-done((bf16[128,1024]{1,0:T(8,128)(2,1)S(1)}, bf16[128,1024]{1,0:T(8,128)(2,1)S(1)}, u32[]{:S(2)}, u32[]{:S(2)}) %collective-permute-start.23) | collective-permute-done | bytes 262176 | tf_op jit(solution)/shard_map/ppermute | solution.py:22
  223.6 14.3 %collective-permute-done.34 = bf16[128,1024]{1,0:T(8,128)(2,1)S(1)} collective-permute-done((bf16[128,1024]{1,0:T(8,128)(2,1)S(1)}, bf16[128,1024]{1,0:T(8,128)(2,1)S(1)}, u32[]{:S(2)}, u32[]{:S(2)}) %collective-permute-start.34) | collective-permute-done | bytes 262176 | tf_op jit(solution)/shard_map/ppermute | solution.py:22
  238.8 16.8 %shard_map.202.grad_ref = bf16[512,1024]{1,0:T(8,128)(2,1)S(1)} custom-call(bf16[512,1024]{1,0:T(8,128)(2,1)S(1)} %get-tuple-element.21.x_ref, f32[256,1024]{1,0:T(8,128)S(1)} %convert_add_fusion.1.refs_0_, f32[128,1024]{1,0:T(8,128)S(1)} %get-tuple-element.61.refs_1_), custom_call_target="tpu_custom_call" | custom-call | flops 1048576 | bytes 15728640 | tf_op jit(solution)/shard_map/pallas_call | solution.py:153
  261.8 3.5 %copy.90 = f32[2,256,1,1024]{3,2,1,0:T(1,128)} copy(f32[2,256,1,1024]{3,1,0,2:T(8,128)S(1)} %bitcast.157) | data formatting | bytes 4194304
  267.1 8.5 %collective-permute-done.25 = f32[60,128]{1,0:T(8,128)S(1)} collective-permute-done((f32[60,128]{1,0:T(8,128)S(1)}, f32[60,128]{1,0:T(8,128)S(1)}, u32[]{:S(2)}, u32[]{:S(2)}) %collective-permute-start.25) | collective-permute-done | bytes 30752 | tf_op jit(solution)/shard_map/ppermute | solution.py:61
  287.8 7.6 %collective-permute-done.32 = bf16[128,1024]{1,0:T(8,128)(2,1)S(1)} collective-permute-done((bf16[128,1024]{1,0:T(8,128)(2,1)S(1)}, bf16[128,1024]{1,0:T(8,128)(2,1)S(1)}, u32[]{:S(2)}, u32[]{:S(2)}) %collective-permute-start.32) | collective-permute-done | bytes 262176 | tf_op jit(solution)/shard_map/ppermute | solution.py:22
  298.5 5.3 %collective-permute-done.33 = bf16[128,1024]{1,0:T(8,128)(2,1)S(1)} collective-permute-done((bf16[128,1024]{1,0:T(8,128)(2,1)S(1)}, bf16[128,1024]{1,0:T(8,128)(2,1)S(1)}, u32[]{:S(2)}, u32[]{:S(2)}) %collective-permute-start.33) | collective-permute-done | bytes 262176 | tf_op jit(solution)/shard_map/ppermute | solution.py:22
  (302 shorter events, 111.7 us)
Async XLA Ops:
  3.4 27.2 %collective-permute-start = (bf16[512,768]{1,0:T(8,128)(2,1)}, bf16[512,768]{1,0:T(8,128)(2,1)}, u32[]{:S(2)}, u32[]{:S(2)}) collective-permute-start(bf16[512,768]{1,0:T(8,128)(2,1)} %copy.63), channel_id=1, source_target_pairs={{0,16},{16,0},{1,17},{17,1},{2,18},{18,2},{3,19},{19,3},{4,20},{20... | collective-permute-start | bytes 2359304 | tf_op jit(solution)/shard_map/ppermute | solution.py:61
  6.3 24.2 %collective-permute-start.4 = (bf16[512,256]{1,0:T(8,128)(2,1)S(1)}, bf16[512,256]{1,0:T(8,128)(2,1)S(1)}, u32[]{:S(2)}, u32[]{:S(2)}) collective-permute-start(bf16[512,256]{1,0:T(8,128)(2,1)S(1)} %copy-done.44), channel_id=1, source_target_pairs={{0,16},{16,0},{1,17},{17,1},{2,18},{18,2},{3,19},{19,3},{4,20},{20... | collective-permute-start | bytes 786440 | tf_op jit(solution)/shard_map/ppermute | solution.py:61
  6.4 58.2 %collective-permute-start.8 = (bf16[512,1024]{1,0:T(8,128)(2,1)}, bf16[512,1024]{1,0:T(8,128)(2,1)}, u32[]{:S(2)}, u32[]{:S(2)}) collective-permute-start(bf16[512,1024]{1,0:T(8,128)(2,1)} %param.19), channel_id=1, source_target_pairs={{0,16},{16,0},{1,17},{17,1},{2,18},{18,2},{3,19},{19,3},{4,20},{20... | collective-permute-start | bytes 3145736 | tf_op jit(solution)/shard_map/ppermute | solution.py:61
  8.4 66.4 %collective-permute-start.9 = (bf16[512,1024]{1,0:T(8,128)(2,1)}, bf16[512,1024]{1,0:T(8,128)(2,1)}, u32[]{:S(2)}, u32[]{:S(2)}) collective-permute-start(bf16[512,1024]{1,0:T(8,128)(2,1)} %param.21), channel_id=1, source_target_pairs={{0,16},{16,0},{1,17},{17,1},{2,18},{18,2},{3,19},{19,3},{4,20},{20... | collective-permute-start | bytes 3145736 | tf_op jit(solution)/shard_map/ppermute | solution.py:61
  38.7 16.0 %collective-permute-start.2 = (bf16[512,192]{0,1:T(8,128)(2,1)}, bf16[512,192]{0,1:T(8,128)(2,1)}, u32[]{:S(2)}, u32[]{:S(2)}) collective-permute-start(bf16[512,192]{0,1:T(8,128)(2,1)} %get-tuple-element.81), channel_id=1, source_target_pairs={{0,8},{4,12},{8,0},{12,4},{1,9},{5,13},{9,1},{13,5},{2,10},{6,14},... | collective-permute-start | bytes 589832 | tf_op jit(solution)/shard_map/ppermute | solution.py:22
  38.7 17.1 %collective-permute-start.1 = (bf16[512,192]{0,1:T(8,128)(2,1)}, bf16[512,192]{0,1:T(8,128)(2,1)}, u32[]{:S(2)}, u32[]{:S(2)}) collective-permute-start(bf16[512,192]{0,1:T(8,128)(2,1)} %get-tuple-element.82), channel_id=1, source_target_pairs={{0,4},{4,8},{8,12},{12,0},{1,5},{5,9},{9,13},{13,1},{2,6},{6,10},{... | collective-permute-start | bytes 589832 | tf_op jit(solution)/shard_map/ppermute | solution.py:22
  61.8 18.6 %collective-permute-start.5 = (bf16[512,64]{1,0:T(8,128)(2,1)S(1)}, bf16[512,64]{1,0:T(8,128)(2,1)S(1)}, u32[]{:S(2)}, u32[]{:S(2)}) collective-permute-start(bf16[512,64]{1,0:T(8,128)(2,1)S(1)} %bitcast.204), channel_id=1, source_target_pairs={{0,12},{4,0},{8,4},{12,8},{1,13},{5,1},{9,5},{13,9},{2,14},{6,2},{... | collective-permute-start | bytes 196616 | tf_op jit(solution)/shard_map/ppermute | solution.py:22
  61.8 18.6 %collective-permute-start.6 = (bf16[512,64]{1,0:T(8,128)(2,1)S(1)}, bf16[512,64]{1,0:T(8,128)(2,1)S(1)}, u32[]{:S(2)}, u32[]{:S(2)}) collective-permute-start(bf16[512,64]{1,0:T(8,128)(2,1)S(1)} %bitcast.203), channel_id=1, source_target_pairs={{0,8},{4,12},{8,0},{12,4},{1,9},{5,13},{9,1},{13,5},{2,10},{6,14},... | collective-permute-start | bytes 196616 | tf_op jit(solution)/shard_map/ppermute | solution.py:22
  62.8 17.6 %collective-permute-start.7 = (bf16[512,64]{1,0:T(8,128)(2,1)S(1)}, bf16[512,64]{1,0:T(8,128)(2,1)S(1)}, u32[]{:S(2)}, u32[]{:S(2)}) collective-permute-start(bf16[512,64]{1,0:T(8,128)(2,1)S(1)} %bitcast.202), channel_id=1, source_target_pairs={{0,4},{4,8},{8,12},{12,0},{1,5},{5,9},{9,13},{13,1},{2,6},{6,10},{... | collective-permute-start | bytes 196616 | tf_op jit(solution)/shard_map/ppermute | solution.py:22
  137.3 56.2 %collective-permute-start.10 = (bf16[256,1024]{1,0:T(8,128)(2,1)}, bf16[256,1024]{1,0:T(8,128)(2,1)}, u32[]{:S(2)}, u32[]{:S(2)}) collective-permute-start(bf16[256,1024]{1,0:T(8,128)(2,1)} %broadcast_select_fusion.8), channel_id=1, source_target_pairs={{0,1},{1,0},{2,3},{3,2},{4,5},{5,4},{6,7},{7,6},{8,9},{9,8},{10,11... | collective-permute-start | bytes 1572872 | tf_op jit(solution)/shard_map/ppermute | solution.py:61
  137.9 16.8 %collective-permute-start.15 = (bf16[512,64]{1,0:T(8,128)(2,1)S(1)}, bf16[512,64]{1,0:T(8,128)(2,1)}, u32[]{:S(2)}, u32[]{:S(2)}) collective-permute-start(bf16[512,64]{1,0:T(8,128)(2,1)S(1)} %bitcast.198), channel_id=1, source_target_pairs={{0,12},{4,0},{8,4},{12,8},{1,13},{5,1},{9,5},{13,9},{2,14},{6,2},{... | collective-permute-start | bytes 196616 | tf_op jit(solution)/shard_map/ppermute | solution.py:22
  141.9 14.4 %collective-permute-start.14 = (bf16[512,64]{1,0:T(8,128)(2,1)S(1)}, bf16[512,64]{1,0:T(8,128)(2,1)}, u32[]{:S(2)}, u32[]{:S(2)}) collective-permute-start(bf16[512,64]{1,0:T(8,128)(2,1)S(1)} %bitcast.197), channel_id=1, source_target_pairs={{0,8},{4,12},{8,0},{12,4},{1,9},{5,13},{9,1},{13,5},{2,10},{6,14},... | collective-permute-start | bytes 196616 | tf_op jit(solution)/shard_map/ppermute | solution.py:22
  142.7 13.6 %collective-permute-start.13 = (bf16[512,64]{1,0:T(8,128)(2,1)}, bf16[512,64]{1,0:T(8,128)(2,1)}, u32[]{:S(2)}, u32[]{:S(2)}) collective-permute-start(bf16[512,64]{1,0:T(8,128)(2,1)} %bitcast.37), channel_id=1, source_target_pairs={{0,4},{4,8},{8,12},{12,0},{1,5},{5,9},{9,13},{13,1},{2,6},{6,10},{... | collective-permute-start | bytes 196616 | tf_op jit(solution)/shard_map/ppermute | solution.py:22
  151.3 48.9 %collective-permute-start.19 = (bf16[256,1024]{1,0:T(8,128)(2,1)}, bf16[256,1024]{1,0:T(8,128)(2,1)}, u32[]{:S(2)}, u32[]{:S(2)}) collective-permute-start(bf16[256,1024]{1,0:T(8,128)(2,1)} %convolution_convert_fusion.3), channel_id=1, source_target_pairs={{0,4},{4,8},{8,12},{12,0},{1,5},{5,9},{9,13},{13,1},{2,6},{6,10},{... | collective-permute-start | bytes 1572872 | tf_op jit(solution)/shard_map/ppermute | solution.py:22
  154.7 53.0 %collective-permute-start.22 = (bf16[512,1024]{1,0:T(8,128)(2,1)}, bf16[512,1024]{1,0:T(8,128)(2,1)}, u32[]{:S(2)}, u32[]{:S(2)}) collective-permute-start(bf16[512,1024]{1,0:T(8,128)(2,1)} %convolution_convert_fusion.1), channel_id=1, source_target_pairs={{0,16},{16,0},{1,17},{17,1},{2,18},{18,2},{3,19},{19,3},{4,20},{20... | collective-permute-start | bytes 3145736 | tf_op jit(solution)/shard_map/ppermute | solution.py:61
  167.5 91.3 %collective-permute-start.30 = (bf16[512,256]{1,0:T(8,128)(2,1)}, bf16[512,256]{1,0:T(8,128)(2,1)}, u32[]{:S(2)}, u32[]{:S(2)}) collective-permute-start(bf16[512,256]{1,0:T(8,128)(2,1)} %convolution_convert_fusion.4), channel_id=1, source_target_pairs={{0,16},{16,0},{1,17},{17,1},{2,18},{18,2},{3,19},{19,3},{4,20},{20... | collective-permute-start | bytes 786440 | tf_op jit(solution)/shard_map/ppermute | solution.py:61
  196.5 25.3 %collective-permute-start.29 = (bf16[512,768]{1,0:T(8,128)(2,1)S(1)}, bf16[512,768]{1,0:T(8,128)(2,1)S(1)}, u32[]{:S(2)}, u32[]{:S(2)}) collective-permute-start(bf16[512,768]{1,0:T(8,128)(2,1)S(1)} %convolution_convert_fusion.2), channel_id=1, source_target_pairs={{0,16},{16,0},{1,17},{17,1},{2,18},{18,2},{3,19},{19,3},{4,20},{20... | collective-permute-start | bytes 2359304 | tf_op jit(solution)/shard_map/ppermute | solution.py:61
  201.9 14.1 %collective-permute-start.20 = (bf16[256,1024]{1,0:T(8,128)(2,1)S(1)}, bf16[256,1024]{1,0:T(8,128)(2,1)S(1)}, u32[]{:S(2)}, u32[]{:S(2)}) collective-permute-start(bf16[256,1024]{1,0:T(8,128)(2,1)S(1)} %add_convert_fusion.4), channel_id=1, source_target_pairs={{0,4},{4,8},{8,12},{12,0},{1,5},{5,9},{9,13},{13,1},{2,6},{6,10},{... | collective-permute-start | bytes 1572872 | tf_op jit(solution)/shard_map/ppermute | solution.py:22
  207.6 59.4 %collective-permute-start.12 = (bf16[256,1024]{1,0:T(8,128)(2,1)S(1)}, bf16[256,1024]{1,0:T(8,128)(2,1)S(1)}, u32[]{:S(2)}, u32[]{:S(2)}) collective-permute-start(bf16[256,1024]{1,0:T(8,128)(2,1)S(1)} %add_convert_fusion.5), channel_id=1, source_target_pairs={{0,1},{1,0},{2,3},{3,2},{4,5},{5,4},{6,7},{7,6},{8,9},{9,8},{10,11... | collective-permute-start | bytes 1572872 | tf_op jit(solution)/shard_map/ppermute | solution.py:61
  216.2 22.5 %collective-permute-start.21 = (bf16[256,1024]{1,0:T(8,128)(2,1)S(1)}, bf16[256,1024]{1,0:T(8,128)(2,1)S(1)}, u32[]{:S(2)}, u32[]{:S(2)}) collective-permute-start(bf16[256,1024]{1,0:T(8,128)(2,1)S(1)} %add_convert_fusion.3), channel_id=1, source_target_pairs={{0,4},{4,8},{8,12},{12,0},{1,5},{5,9},{9,13},{13,1},{2,6},{6,10},{... | collective-permute-start | bytes 1572872 | tf_op jit(solution)/shard_map/ppermute | solution.py:22
  221.8 16.2 %collective-permute-start.34 = (bf16[128,1024]{1,0:T(8,128)(2,1)S(1)}, bf16[128,1024]{1,0:T(8,128)(2,1)S(1)}, u32[]{:S(2)}, u32[]{:S(2)}) collective-permute-start(bf16[128,1024]{1,0:T(8,128)(2,1)S(1)} %get-tuple-element.60), channel_id=1, source_target_pairs={{0,4},{4,8},{8,12},{12,0},{1,5},{5,9},{9,13},{13,1},{2,6},{6,10},{... | collective-permute-start | bytes 786440 | tf_op jit(solution)/shard_map/ppermute | solution.py:22
  238.7 56.9 %collective-permute-start.35 = (bf16[128,1024]{1,0:T(8,128)(2,1)}, bf16[128,1024]{1,0:T(8,128)(2,1)}, u32[]{:S(2)}, u32[]{:S(2)}) collective-permute-start(bf16[128,1024]{1,0:T(8,128)(2,1)} %add_convert_fusion.7), channel_id=1, source_target_pairs={{0,4},{4,8},{8,12},{12,0},{1,5},{5,9},{9,13},{13,1},{2,6},{6,10},{... | collective-permute-start | bytes 786440 | tf_op jit(solution)/shard_map/ppermute | solution.py:22
  265.2 20.1 %collective-permute-start.31 = (bf16[128,1024]{1,0:T(8,128)(2,1)S(1)}, bf16[128,1024]{1,0:T(8,128)(2,1)}, u32[]{:S(2)}, u32[]{:S(2)}) collective-permute-start(bf16[128,1024]{1,0:T(8,128)(2,1)S(1)} %pad_maximum_fusion.8), channel_id=1, source_target_pairs={{0,4},{4,8},{8,12},{12,0},{1,5},{5,9},{9,13},{13,1},{2,6},{6,10},{... | collective-permute-start | bytes 786440 | tf_op jit(solution)/shard_map/ppermute | solution.py:22
  265.2 32.3 %collective-permute-start.36 = (bf16[128,1024]{1,0:T(8,128)(2,1)}, bf16[128,1024]{1,0:T(8,128)(2,1)S(1)}, u32[]{:S(2)}, u32[]{:S(2)}) collective-permute-start(bf16[128,1024]{1,0:T(8,128)(2,1)} %select_convert_fusion), channel_id=1, source_target_pairs={{0,16},{16,0},{1,17},{17,1},{2,18},{18,2},{3,19},{19,3},{4,20},{20... | collective-permute-start | bytes 786440 | tf_op jit(solution)/shard_map/ppermute | solution.py:61
  (65 other events, 624.8 us)

commit v4 on v3

--- a/solution.py
+++ b/solution.py
@@ -326,7 +326,8 @@
     add_rows(total_ref, (row_sum(grad * unit), row_sum(grad), row_sum(result), row_sum(dy)))
 
 
-def norm_one_sums_kernel(weight_ref, grad_ref, x_ref, out_ref, total_ref):
+def norm_one_sums_kernel(weight_ref, grad_ref, x_ref, *refs):
+    out_ref, total_ref = refs[-2:]
     unit, _ = unit_rows(x_ref[...].astype(jnp.float32))
     grad = dot_rows(grad_ref[...], weight_ref[...])
     out_ref[...] = grad.astype(jnp.bfloat16)
@@ -458,8 +459,9 @@
 
 
 def attend_back_kernel(
-    blocks, heads, scale_by, bias_ref, row_ref, column_ref, in_ref, grad_ref, out_ref
+    blocks, heads, scale_by, bias_ref, row_ref, column_ref, in_ref, grad_ref, *refs
 ):
+    out_ref = refs[-1]
     slots, rows = in_ref.shape[0], in_ref.shape[2] // blocks
     size = slots * rows
 
@@ -561,7 +563,7 @@
         groups = groups.reshape(count, tokens, kinds, width).transpose(1, 2, 0, 3)
         return groups.reshape(tokens, kinds, count * width)
 
-    def back(grads):
+    def back(grads, gates):
         grouped_grads = grads.reshape(tokens, count, width).transpose(1, 0, 2)
         spread_grads = spread_heads(grouped_grads).reshape(count, seqs, rows, width)
         slots = head_call(
@@ -570,11 +572,11 @@
             heads,
             tables,
             (spread, spread_grads),
-            (),
+            gates,
             3 * width,
             8 * pairs,
         )
-        return homeward(slots, 3), slots
+        return homeward(slots, 3)
 
     return homeward(attended, 1)[:, 0], back
 
@@ -630,7 +632,8 @@
     attended_seq = attended.transpose(0, 2, 1, 3)
     attended_bf = attended_seq.reshape(tok_rows, local_width).astype(jnp.bfloat16)
 
-    def back(attend_grad_bf):
+    def back(attend_grad_bf, gates):
+        del gates
         grad_heads = split_heads(attend_grad_bf)
         delta_row = jnp.sum(grad_heads.astype(jnp.float32) * attended_seq, axis=-1).transpose(0, 2, 1)
         head_zeros = jnp.zeros((seq_dev, group_len, heads_loc, HD), jnp.float32)
@@ -675,7 +678,7 @@
             ],
             1,
         ).astype(jnp.bfloat16)
-        return qkv_grad_bf, qkv_grad_bf
+        return qkv_grad_bf
 
     return attended_bf, back
 
@@ -773,21 +776,22 @@
     attend_grad_bf = jnp.dot(resid_bf, full_out, preferred_element_type=jnp.float32).astype(
         jnp.bfloat16
     )
-    qkv_grad_bf, attend_done = attend_back(attend_grad_bf)
+    down_seen, up_seen = [], []
+    grad_down = owned_grad_ring_first(dy_rows, act_bf, (norm_two_grad,), down_seen)
+    half_up = shard_half(normed_two, pre_grad_bf)
+    (grad_up,) = ctx_share([half_up], up_seen)
+    qkv_grad_bf = attend_back(attend_grad_bf, tuple(down_seen[:1]) + (half_up,))
     qkv_grad_flat = qkv_grad_bf.reshape(tok_rows, 3 * local_width)
     norm_one_part, sums_one = row_call(
         norm_one_sums_kernel,
         (full_qkv,),
         (qkv_grad_flat, x_rows),
-        (),
+        tuple(down_seen[1:2] + up_seen[:1]),
         (jnp.bfloat16,),
         True,
         row_flops + 6 * tok_rows * model_width * local_width,
     )
-    down_seen, up_seen = [], []
-    grad_down = owned_grad_ring_first(dy_rows, act_bf, (norm_two_grad, attend_done), down_seen)
-    (grad_up,) = ctx_share([shard_half(normed_two, pre_grad_bf, attend_done)], up_seen)
-    norm_one_grad = sum_over_tp_now(norm_one_part, tuple(down_seen[-1:] + up_seen[:1]))
+    norm_one_grad = sum_over_tp_now(norm_one_part)
     (input_grad,) = row_call(
         norm_one_back_kernel,
         (gains,),

time: 306 us -> 311 us (1.016)
  waiting for transfers between devices: 112 us -> 76.5 us
  local copies, waits for them, and re-layouts: 34.2 us -> 51.4 us
  starting transfers between devices: 32.3 us -> 49.4 us
  other arithmetic: 23.3 us -> 28.9 us
    ppermute x21, waiting for transfers between devices: 68.3 us -> 35.9 us  [shifted(): return lax.ppermute(value, axis, pairs)]
    ppermute x21, starting transfers between devices: 18.6 us -> 32.4 us  [shifted(): return lax.ppermute(value, axis, pairs)]
    unnamed x126 -> x136, local copies, waits for them, and re-layouts: 10.3 us -> 15.5 us
    another operation x6, local copies, waits for them, and re-layouts: 1.06 us -> 6.14 us
    squeeze x3, local copies, waits for them, and re-layouts: 0.37 us -> 5.27 us  [return_heads(): slots[step]]
    convert_element_type x5, other arithmetic: 2.03 us -> 5.56 us  [ring_sum(): arrived = shifted(moving.astype(jnp.bfloat16), 'ctx', 1)]
    ppermute x16, starting transfers between devices: 13.6 us -> 17 us  [exchanged(): lax.ppermute(value, axis, [(source, source ^ mask) for source in range(co...]
    ppermute x16, waiting for transfers between devices: 43.7 us -> 40.5 us  [exchanged(): lax.ppermute(value, axis, [(source, source ^ mask) for source in range(co...]
  transfers between devices with their start and end apart: 37 -> 37, of which waited for: 17 -> 16; matrix products, arithmetic and copies ran while one was open for 19% -> 28% of each run, Pallas kernels for 11% -> 11%
where the time goes in v4:
time: 311 us; the launch traced here: 310 us
  waiting for transfers between devices  76.5 us (25%)
  Pallas kernels  69.9 us (22%)
  local copies, waits for them, and re-layouts  51.4 us (17%)
  starting transfers between devices  49.4 us (16%)
  other arithmetic  28.9 us (9%)
  matrix products  28.8 us (9%)
  between operations  4.61 us (1%)
    pallas_call x3, Pallas kernels, sum_over_tp_now(): pl.pallas_call(tp_kernel, out_shape=jax.ShapeDtypeStruct((rows, width), j...  49.4 us
    ppermute x16, waiting for transfers between devices, exchanged(): lax.ppermute(value, axis, [(source, source ^ mask) for source in range(co...  40.5 us
    ppermute x21, waiting for transfers between devices, shifted(): return lax.ppermute(value, axis, pairs)  35.9 us
    ppermute x21, starting transfers between devices, shifted(): return lax.ppermute(value, axis, pairs)  32.4 us
    dot_general x10, matrix products, outer(): jnp.einsum('td,tf->df', left, right, preferred_element_type=jnp.float32)  18.9 us
    ppermute x16, starting transfers between devices, exchanged(): lax.ppermute(value, axis, [(source, source ^ mask) for source in range(co...  17 us
    unnamed x136, local copies, waits for them, and re-layouts  15.5 us
    pallas_call x2, Pallas kernels, head_call(): pl.pallas_call(functools.partial(kernel, blocks, heads, 1.0 / math.sqrt(H...  11.9 us
  transfers between devices with their start and end apart: 37, of which 16 were waited for; matrix products, arithmetic and copies ran while one was open for 28% of the time, Pallas kernels for 11%

profile of v4, /device:TPU:0, one launch (start us, length us, event | category | flops | bytes accessed | tf_op | source)
XLA Modules:
  0.0 309.6 jit_solution(16069899414714711299)
XLA Ops:
  3.4 3.0 collective-permute-start
  15.8 14.7 %collective-permute-done.4 = bf16[512,256]{1,0:T(8,128)(2,1)S(1)} collective-permute-done((bf16[512,256]{1,0:T(8,128)(2,1)S(1)}, bf16[512,256]{1,0:T(8,128)(2,1)S(1)}, u32[]{:S(2)}, u32[]{:S(2)}) %collective-permute-start.4) | collective-permute-done | bytes 262176 | tf_op jit(solution)/shard_map/ppermute | solution.py:61
  34.6 4.1 %collective-permute-start.3 = (bf16[512,192]{0,1:T(8,128)(2,1)}, bf16[512,192]{0,1:T(8,128)(2,1)}, u32[]{:S(2)}, u32[]{:S(2)}) collective-permute-start(bf16[512,192]{0,1:T(8,128)(2,1)} %get-tuple-element.82), channel_id=1, source_target_pairs={{0,12},{4,0},{8,4},{12,8},{1,13},{5,1},{9,5},{13,9},{2,14},{6,2},{... | collective-permute-start | bytes 589832 | tf_op jit(solution)/shard_map/ppermute | solution.py:22
  45.5 9.3 %collective-permute-done.2 = bf16[512,192]{0,1:T(8,128)(2,1)} collective-permute-done((bf16[512,192]{0,1:T(8,128)(2,1)}, bf16[512,192]{0,1:T(8,128)(2,1)}, u32[]{:S(2)}, u32[]{:S(2)}) %collective-permute-start.2) | collective-permute-done | bytes 196640 | tf_op jit(solution)/shard_map/ppermute | solution.py:22
  57.2 4.5 %shard_map.195 = bf16[4,2,256,64]{3,2,1,0:T(8,128)(2,1)S(1)} custom-call(f32[1,1,1024]{2,1,0:T(1,128)S(1)} %mul.133.bias_ref, f32[1,1024]{1,0:T(1,128)S(1)} %convert_element_type.207.row_ref, f32[1024,1]{1,0:T(8,128)S(1)} %convert_element_type.259.column_ref, bf16[4,2,256,192]{3,2,1,0:T(8,128)(2,1)S(1)} %pad_maximum_fusion.5.in_ref, ...), custom_call_target="tpu_custom_call" | custom-call | flops 402653184 | bytes 2097152 | tf_op jit(solution)/shard_map/pallas_call | solution.py:519
  64.6 10.1 %collective-permute-done.9 = bf16[512,1024]{1,0:T(8,128)(2,1)} collective-permute-done((bf16[512,1024]{1,0:T(8,128)(2,1)}, bf16[512,1024]{1,0:T(8,128)(2,1)}, u32[]{:S(2)}, u32[]{:S(2)}) %collective-permute-start.9) | collective-permute-done | bytes 1048608 | tf_op jit(solution)/shard_map/ppermute | solution.py:61
  74.8 2.8 broadcast_select_fusion
  84.2 16.8 %shard_map.196.branch_ref = bf16[512,1024]{1,0:T(8,128)(2,1)S(1)} custom-call(bf16[512,1024]{1,0:T(8,128)(2,1)S(1)} %add_convert_fusion.2.x_ref), custom_call_target="tpu_custom_call" | custom-call | flops 1048576 | bytes 15728640 | tf_op jit(solution)/shard_map/pallas_call | solution.py:153
  105.1 2.6 convert_reduce_fusion
  109.1 16.8 %shard_map.198.grad_ref = bf16[512,1024]{1,0:T(8,128)(2,1)S(1)} custom-call(bf16[512,1024]{1,0:T(8,128)(2,1)S(1)} %convolution_convert_fusion.x_ref), custom_call_target="tpu_custom_call" | custom-call | flops 1048576 | bytes 15728640 | tf_op jit(solution)/shard_map/pallas_call | solution.py:153
  134.8 3.8 %collective-permute-start.15 = (bf16[512,64]{1,0:T(8,128)(2,1)}, bf16[512,64]{1,0:T(8,128)(2,1)}, u32[]{:S(2)}, u32[]{:S(2)}) collective-permute-start(bf16[512,64]{1,0:T(8,128)(2,1)} %bitcast.200), channel_id=1, source_target_pairs={{0,12},{4,0},{8,4},{12,8},{1,13},{5,1},{9,5},{13,9},{2,14},{6,2},{... | collective-permute-start | bytes 196616 | tf_op jit(solution)/shard_map/ppermute | solution.py:22
  142.9 2.7 convolution_convert_fusion.3
  148.1 3.1 %convolution_convert_fusion.1 = bf16[512,1024]{1,0:T(8,128)(2,1)} fusion(bf16[512,1024]{1,0:T(8,128)(2,1)} %copy-done.41, bf16[512,1024]{1,0:T(8,128)(2,1)} %copy-done.19, s32[]{:T(128)S(6)} %select_n.174), kind=kOutput, calls=%fused_computation.25 | convolution fusion | flops 537395200 | bytes 2621444 | tf_op jit(solution)/shard_map/td,tf->df/dot_general | solution.py:202
  167.8 3.9 %collective-permute-done.11 = bf16[256,1024]{1,0:T(8,128)(2,1)} collective-permute-done((bf16[256,1024]{1,0:T(8,128)(2,1)}, bf16[256,1024]{1,0:T(8,128)(2,1)}, u32[]{:S(2)}, u32[]{:S(2)}) %collective-permute-start.11) | collective-permute-done | bytes 524320 | tf_op jit(solution)/shard_map/ppermute | solution.py:61
  173.9 7.7 %collective-permute-done.17 = bf16[512,1024]{1,0:T(8,128)(2,1)} collective-permute-done((bf16[512,1024]{1,0:T(8,128)(2,1)}, bf16[512,1024]{1,0:T(8,128)(2,1)}, u32[]{:S(2)}, u32[]{:S(2)}) %collective-permute-start.17) | collective-permute-done | bytes 1048608 | tf_op jit(solution)/shard_map/ppermute | solution.py:61
  183.6 7.4 %shard_map.200 = bf16[4,2,256,192]{3,2,1,0:T(8,128)(2,1)S(1)} custom-call(f32[1,1,1024]{2,1,0:T(1,128)S(1)} %mul.133.bias_ref, f32[1,1024]{1,0:T(1,128)S(1)} %convert_element_type.207.row_ref, f32[1024,1]{1,0:T(8,128)S(1)} %copy-done.7, bf16[4,2,256,192]{3,2,1,0:T(8,128)(2,1)S(1)} %copy-done.2, bf16[4,2,256,64]{3,2,1,0:T(8,128)(2,1)S(1)} %pad_maximum_fusion.7.grad_ref, ...), custom_call_target="tpu_custom_call" | custom-call | flops 1073741824 | bytes 2097152 | tf_op jit(solution)/shard_map/pallas_call | solution.py:519
  202.0 2.7 fusion.58
  205.5 11.6 %collective-permute-start.22 = (bf16[128,1024]{1,0:T(8,128)(2,1)}, bf16[128,1024]{1,0:T(8,128)(2,1)}, u32[]{:S(2)}, u32[]{:S(2)}) collective-permute-start(bf16[128,1024]{1,0:T(8,128)(2,1)} %dynamic-slice_convert_fusion), channel_id=1, source_target_pairs={{0,4},{4,8},{8,12},{12,0},{1,5},{5,9},{9,13},{13,1},{2,6},{6,10},{... | collective-permute-start | bytes 786440 | tf_op jit(solution)/shard_map/ppermute | solution.py:22
  230.3 2.7 shard_map.201
  233.1 15.8 %shard_map.202.grad_ref = bf16[512,1024]{1,0:T(8,128)(2,1)S(1)} custom-call(bf16[512,1024]{1,0:T(8,128)(2,1)S(1)} %get-tuple-element.21.x_ref), custom_call_target="tpu_custom_call" | custom-call | flops 1048576 | bytes 15728640 | tf_op jit(solution)/shard_map/pallas_call | solution.py:153
  262.7 3.5 %copy.90 = f32[2,256,1,1024]{3,2,1,0:T(1,128)} copy(f32[2,256,1,1024]{3,1,0,2:T(8,128)S(1)} %bitcast.158) | data formatting | bytes 4194304
  282.9 7.8 %collective-permute-done.30 = bf16[128,1024]{1,0:T(8,128)(2,1)S(1)} collective-permute-done((bf16[128,1024]{1,0:T(8,128)(2,1)S(1)}, bf16[128,1024]{1,0:T(8,128)(2,1)S(1)}, u32[]{:S(2)}, u32[]{:S(2)}) %collective-permute-start.30) | collective-permute-done | bytes 262176 | tf_op jit(solution)/shard_map/ppermute | solution.py:22
  292.2 7.2 %collective-permute-done.31 = bf16[128,1024]{1,0:T(8,128)(2,1)S(1)} collective-permute-done((bf16[128,1024]{1,0:T(8,128)(2,1)S(1)}, bf16[128,1024]{1,0:T(8,128)(2,1)S(1)}, u32[]{:S(2)}, u32[]{:S(2)}) %collective-permute-start.31) | collective-permute-done | bytes 262176 | tf_op jit(solution)/shard_map/ppermute | solution.py:22
  301.4 6.4 %collective-permute-done.32 = bf16[128,1024]{1,0:T(8,128)(2,1)S(1)} collective-permute-done((bf16[128,1024]{1,0:T(8,128)(2,1)S(1)}, bf16[128,1024]{1,0:T(8,128)(2,1)S(1)}, u32[]{:S(2)}, u32[]{:S(2)}) %collective-permute-start.32) | collective-permute-done | bytes 262176 | tf_op jit(solution)/shard_map/ppermute | solution.py:22
  (311 shorter events, 133.9 us)
Async XLA Ops:
  3.4 27.2 %collective-permute-start = (bf16[512,768]{1,0:T(8,128)(2,1)}, bf16[512,768]{1,0:T(8,128)(2,1)}, u32[]{:S(2)}, u32[]{:S(2)}) collective-permute-start(bf16[512,768]{1,0:T(8,128)(2,1)} %copy.63), channel_id=1, source_target_pairs={{0,16},{16,0},{1,17},{17,1},{2,18},{18,2},{3,19},{19,3},{4,20},{20... | collective-permute-start | bytes 2359304 | tf_op jit(solution)/shard_map/ppermute | solution.py:61
  6.3 24.2 %collective-permute-start.4 = (bf16[512,256]{1,0:T(8,128)(2,1)S(1)}, bf16[512,256]{1,0:T(8,128)(2,1)S(1)}, u32[]{:S(2)}, u32[]{:S(2)}) collective-permute-start(bf16[512,256]{1,0:T(8,128)(2,1)S(1)} %copy-done.50), channel_id=1, source_target_pairs={{0,16},{16,0},{1,17},{17,1},{2,18},{18,2},{3,19},{19,3},{4,20},{20... | collective-permute-start | bytes 786440 | tf_op jit(solution)/shard_map/ppermute | solution.py:61
  6.4 58.2 %collective-permute-start.8 = (bf16[512,1024]{1,0:T(8,128)(2,1)}, bf16[512,1024]{1,0:T(8,128)(2,1)}, u32[]{:S(2)}, u32[]{:S(2)}) collective-permute-start(bf16[512,1024]{1,0:T(8,128)(2,1)} %param.19), channel_id=1, source_target_pairs={{0,16},{16,0},{1,17},{17,1},{2,18},{18,2},{3,19},{19,3},{4,20},{20... | collective-permute-start | bytes 3145736 | tf_op jit(solution)/shard_map/ppermute | solution.py:61
  8.4 66.4 %collective-permute-start.9 = (bf16[512,1024]{1,0:T(8,128)(2,1)}, bf16[512,1024]{1,0:T(8,128)(2,1)}, u32[]{:S(2)}, u32[]{:S(2)}) collective-permute-start(bf16[512,1024]{1,0:T(8,128)(2,1)} %param.21), channel_id=1, source_target_pairs={{0,16},{16,0},{1,17},{17,1},{2,18},{18,2},{3,19},{19,3},{4,20},{20... | collective-permute-start | bytes 3145736 | tf_op jit(solution)/shard_map/ppermute | solution.py:61
  38.7 17.1 %collective-permute-start.1 = (bf16[512,192]{0,1:T(8,128)(2,1)}, bf16[512,192]{0,1:T(8,128)(2,1)}, u32[]{:S(2)}, u32[]{:S(2)}) collective-permute-start(bf16[512,192]{0,1:T(8,128)(2,1)} %get-tuple-element.84), channel_id=1, source_target_pairs={{0,4},{4,8},{8,12},{12,0},{1,5},{5,9},{9,13},{13,1},{2,6},{6,10},{... | collective-permute-start | bytes 589832 | tf_op jit(solution)/shard_map/ppermute | solution.py:22
  61.7 18.6 %collective-permute-start.5 = (bf16[512,64]{1,0:T(8,128)(2,1)S(1)}, bf16[512,64]{1,0:T(8,128)(2,1)S(1)}, u32[]{:S(2)}, u32[]{:S(2)}) collective-permute-start(bf16[512,64]{1,0:T(8,128)(2,1)S(1)} %bitcast.206), channel_id=1, source_target_pairs={{0,12},{4,0},{8,4},{12,8},{1,13},{5,1},{9,5},{13,9},{2,14},{6,2},{... | collective-permute-start | bytes 196616 | tf_op jit(solution)/shard_map/ppermute | solution.py:22
  61.8 18.6 %collective-permute-start.6 = (bf16[512,64]{1,0:T(8,128)(2,1)S(1)}, bf16[512,64]{1,0:T(8,128)(2,1)S(1)}, u32[]{:S(2)}, u32[]{:S(2)}) collective-permute-start(bf16[512,64]{1,0:T(8,128)(2,1)S(1)} %bitcast.205), channel_id=1, source_target_pairs={{0,8},{4,12},{8,0},{12,4},{1,9},{5,13},{9,1},{13,5},{2,10},{6,14},... | collective-permute-start | bytes 196616 | tf_op jit(solution)/shard_map/ppermute | solution.py:22
  62.8 17.7 %collective-permute-start.7 = (bf16[512,64]{1,0:T(8,128)(2,1)S(1)}, bf16[512,64]{1,0:T(8,128)(2,1)S(1)}, u32[]{:S(2)}, u32[]{:S(2)}) collective-permute-start(bf16[512,64]{1,0:T(8,128)(2,1)S(1)} %bitcast.204), channel_id=1, source_target_pairs={{0,4},{4,8},{8,12},{12,0},{1,5},{5,9},{9,13},{13,1},{2,6},{6,10},{... | collective-permute-start | bytes 196616 | tf_op jit(solution)/shard_map/ppermute | solution.py:22
  132.2 23.0 %collective-permute-start.10 = (bf16[256,1024]{1,0:T(8,128)(2,1)}, bf16[256,1024]{1,0:T(8,128)(2,1)}, u32[]{:S(2)}, u32[]{:S(2)}) collective-permute-start(bf16[256,1024]{1,0:T(8,128)(2,1)} %broadcast_select_fusion.8), channel_id=1, source_target_pairs={{0,1},{1,0},{2,3},{3,2},{4,5},{5,4},{6,7},{7,6},{8,9},{9,8},{10,11... | collective-permute-start | bytes 1572872 | tf_op jit(solution)/shard_map/ppermute | solution.py:61
  134.8 24.0 %collective-permute-start.15 = (bf16[512,64]{1,0:T(8,128)(2,1)}, bf16[512,64]{1,0:T(8,128)(2,1)}, u32[]{:S(2)}, u32[]{:S(2)}) collective-permute-start(bf16[512,64]{1,0:T(8,128)(2,1)} %bitcast.200), channel_id=1, source_target_pairs={{0,12},{4,0},{8,4},{12,8},{1,13},{5,1},{9,5},{13,9},{2,14},{6,2},{... | collective-permute-start | bytes 196616 | tf_op jit(solution)/shard_map/ppermute | solution.py:22
  140.3 22.3 %collective-permute-start.14 = (bf16[512,64]{1,0:T(8,128)(2,1)}, bf16[512,64]{1,0:T(8,128)(2,1)}, u32[]{:S(2)}, u32[]{:S(2)}) collective-permute-start(bf16[512,64]{1,0:T(8,128)(2,1)} %bitcast.199), channel_id=1, source_target_pairs={{0,8},{4,12},{8,0},{12,4},{1,9},{5,13},{9,1},{13,5},{2,10},{6,14},... | collective-permute-start | bytes 196616 | tf_op jit(solution)/shard_map/ppermute | solution.py:22
  141.9 22.2 %collective-permute-start.13 = (bf16[512,64]{1,0:T(8,128)(2,1)}, bf16[512,64]{1,0:T(8,128)(2,1)}, u32[]{:S(2)}, u32[]{:S(2)}) collective-permute-start(bf16[512,64]{1,0:T(8,128)(2,1)} %bitcast.198), channel_id=1, source_target_pairs={{0,4},{4,8},{8,12},{12,0},{1,5},{5,9},{9,13},{13,1},{2,6},{6,10},{... | collective-permute-start | bytes 196616 | tf_op jit(solution)/shard_map/ppermute | solution.py:22
  145.6 19.7 %collective-permute-start.16 = (bf16[256,1024]{1,0:T(8,128)(2,1)}, bf16[256,1024]{1,0:T(8,128)(2,1)}, u32[]{:S(2)}, u32[]{:S(2)}) collective-permute-start(bf16[256,1024]{1,0:T(8,128)(2,1)} %convolution_convert_fusion.3), channel_id=1, source_target_pairs={{0,4},{4,8},{8,12},{12,0},{1,5},{5,9},{9,13},{13,1},{2,6},{6,10},{... | collective-permute-start | bytes 1572872 | tf_op jit(solution)/shard_map/ppermute | solution.py:22
  155.2 26.4 %collective-permute-start.17 = (bf16[512,1024]{1,0:T(8,128)(2,1)}, bf16[512,1024]{1,0:T(8,128)(2,1)}, u32[]{:S(2)}, u32[]{:S(2)}) collective-permute-start(bf16[512,1024]{1,0:T(8,128)(2,1)} %convolution_convert_fusion.1), channel_id=1, source_target_pairs={{0,16},{16,0},{1,17},{17,1},{2,18},{18,2},{3,19},{19,3},{4,20},{20... | collective-permute-start | bytes 3145736 | tf_op jit(solution)/shard_map/ppermute | solution.py:61
  162.6 91.9 %collective-permute-start.29 = (bf16[512,256]{1,0:T(8,128)(2,1)}, bf16[512,256]{1,0:T(8,128)(2,1)}, u32[]{:S(2)}, u32[]{:S(2)}) collective-permute-start(bf16[512,256]{1,0:T(8,128)(2,1)} %convolution_convert_fusion.4), channel_id=1, source_target_pairs={{0,16},{16,0},{1,17},{17,1},{2,18},{18,2},{3,19},{19,3},{4,20},{20... | collective-permute-start | bytes 786440 | tf_op jit(solution)/shard_map/ppermute | solution.py:61
  167.8 32.7 %collective-permute-start.21 = (bf16[256,1024]{1,0:T(8,128)(2,1)}, bf16[256,1024]{1,0:T(8,128)(2,1)}, u32[]{:S(2)}, u32[]{:S(2)}) collective-permute-start(bf16[256,1024]{1,0:T(8,128)(2,1)} %get-tuple-element.109), channel_id=1, source_target_pairs={{0,4},{4,8},{8,12},{12,0},{1,5},{5,9},{9,13},{13,1},{2,6},{6,10},{... | collective-permute-start | bytes 1572872 | tf_op jit(solution)/shard_map/ppermute | solution.py:22
  173.9 107.6 %collective-permute-start.12 = (bf16[256,1024]{1,0:T(8,128)(2,1)}, bf16[256,1024]{1,0:T(8,128)(2,1)}, u32[]{:S(2)}, u32[]{:S(2)}) collective-permute-start(bf16[256,1024]{1,0:T(8,128)(2,1)} %add_convert_fusion.3), channel_id=1, source_target_pairs={{0,1},{1,0},{2,3},{3,2},{4,5},{5,4},{6,7},{7,6},{8,9},{9,8},{10,11... | collective-permute-start | bytes 1572872 | tf_op jit(solution)/shard_map/ppermute | solution.py:61
  198.6 20.0 %collective-permute-start.19 = (bf16[512,192]{0,1:T(8,128)(2,1)}, bf16[512,192]{0,1:T(8,128)(2,1)}, u32[]{:S(2)}, u32[]{:S(2)}) collective-permute-start(bf16[512,192]{0,1:T(8,128)(2,1)} %copy.80), channel_id=1, source_target_pairs={{0,8},{4,12},{8,0},{12,4},{1,9},{5,13},{9,1},{13,5},{2,10},{6,14},... | collective-permute-start | bytes 589832 | tf_op jit(solution)/shard_map/ppermute | solution.py:22
  200.5 19.0 %collective-permute-start.20 = (bf16[512,192]{0,1:T(8,128)(2,1)}, bf16[512,192]{0,1:T(8,128)(2,1)S(1)}, u32[]{:S(2)}, u32[]{:S(2)}) collective-permute-start(bf16[512,192]{0,1:T(8,128)(2,1)} %copy.81), channel_id=1, source_target_pairs={{0,4},{4,8},{8,12},{12,0},{1,5},{5,9},{9,13},{13,1},{2,6},{6,10},{... | collective-permute-start | bytes 589832 | tf_op jit(solution)/shard_map/ppermute | solution.py:22
  205.5 20.7 %collective-permute-start.22 = (bf16[128,1024]{1,0:T(8,128)(2,1)}, bf16[128,1024]{1,0:T(8,128)(2,1)}, u32[]{:S(2)}, u32[]{:S(2)}) collective-permute-start(bf16[128,1024]{1,0:T(8,128)(2,1)} %dynamic-slice_convert_fusion), channel_id=1, source_target_pairs={{0,4},{4,8},{8,12},{12,0},{1,5},{5,9},{9,13},{13,1},{2,6},{6,10},{... | collective-permute-start | bytes 786440 | tf_op jit(solution)/shard_map/ppermute | solution.py:22
  218.6 57.5 %collective-permute-start.35 = (bf16[256,1024]{1,0:T(8,128)(2,1)}, bf16[256,1024]{1,0:T(8,128)(2,1)}, u32[]{:S(2)}, u32[]{:S(2)}) collective-permute-start(bf16[256,1024]{1,0:T(8,128)(2,1)} %get-tuple-element.60), channel_id=1, source_target_pairs={{0,4},{4,8},{8,12},{12,0},{1,5},{5,9},{9,13},{13,1},{2,6},{6,10},{... | collective-permute-start | bytes 1572872 | tf_op jit(solution)/shard_map/ppermute | solution.py:22
  253.2 26.0 %collective-permute-start.28 = (bf16[512,768]{1,0:T(8,128)(2,1)}, bf16[512,768]{1,0:T(8,128)(2,1)}, u32[]{:S(2)}, u32[]{:S(2)}) collective-permute-start(bf16[512,768]{1,0:T(8,128)(2,1)} %convolution_convert_fusion.2), channel_id=1, source_target_pairs={{0,16},{16,0},{1,17},{17,1},{2,18},{18,2},{3,19},{19,3},{4,20},{20... | collective-permute-start | bytes 2359304 | tf_op jit(solution)/shard_map/ppermute | solution.py:61
  276.0 23.6 %collective-permute-start.34 = (bf16[128,1024]{1,0:T(8,128)(2,1)S(1)}, bf16[128,1024]{1,0:T(8,128)(2,1)S(1)}, u32[]{:S(2)}, u32[]{:S(2)}) collective-permute-start(bf16[128,1024]{1,0:T(8,128)(2,1)S(1)} %add_convert_fusion.5), channel_id=1, source_target_pairs={{0,4},{4,8},{8,12},{12,0},{1,5},{5,9},{9,13},{13,1},{2,6},{6,10},{... | collective-permute-start | bytes 786440 | tf_op jit(solution)/shard_map/ppermute | solution.py:22
  277.7 22.8 %collective-permute-start.36 = (bf16[128,1024]{1,0:T(8,128)(2,1)S(1)}, bf16[128,1024]{1,0:T(8,128)(2,1)S(1)}, u32[]{:S(2)}, u32[]{:S(2)}) collective-permute-start(bf16[128,1024]{1,0:T(8,128)(2,1)S(1)} %select_convert_fusion), channel_id=1, source_target_pairs={{0,16},{16,0},{1,17},{17,1},{2,18},{18,2},{3,19},{19,3},{4,20},{20... | collective-permute-start | bytes 786440 | tf_op jit(solution)/shard_map/ppermute | solution.py:61
  (70 other events, 611.6 us)
